TPU v7x, 32 devices: a whole 2x2x4 slice. The times are simulated.
32 devices in a mesh: fsdp: 2 (over x), ctx: 4 (over z), tp: 4 (over y, core).
Axes of the slice: x: 2, y: 2, z: 4, core: 2. Of those that a mesh axis runs over, the one named last changes fastest.
Arguments:
- hidden_in: bfloat16 [5120, 2048], P(('fsdp', 'ctx')), may hold values from -6 to 6
- teacher: bfloat16 [5120, 2048], P(('fsdp', 'ctx')), may hold values from -6 to 6
- w_query: bfloat16 [2048, 2048], P('fsdp', 'tp'), may hold values from -0.125 to 0.125
- w_key: bfloat16 [2048, 1024], P('fsdp', 'tp'), may hold values from -0.125 to 0.125
- w_value: bfloat16 [2048, 1024], P('fsdp', 'tp'), may hold values from -0.125 to 0.125
- w_out: bfloat16 [2048, 2048], P('tp', 'fsdp'), may hold values from -0.75 to 0.75
- w_gate: bfloat16 [2048, 8192], P('fsdp', 'tp'), may hold values from -0.125 to 0.125
- w_up: bfloat16 [2048, 8192], P('fsdp', 'tp'), may hold values from -0.125 to 0.125
- w_down: bfloat16 [8192, 2048], P('tp', 'fsdp'), may hold values from -0.0625 to 0.0625
- attn_gain: bfloat16 [2048], P('fsdp'), may hold values from 0.5 to 1.5
- ffn_gain: bfloat16 [2048], P('fsdp'), may hold values from 0.5 to 1.5
- segment_ids: int32 [5120], P(('fsdp', 'ctx')), may hold values from 0 to 25, as said below
- parents: int32 [26], replicated, may hold values from -1 to 25, as said below
- positions: int32 [5120], P(('fsdp', 'ctx')), may hold values from 0 to 1279, as said below
- valid_mask: int32 [5120], P(('fsdp', 'ctx')), may hold values from 0 to 1, as said below
Outputs:
- output: bfloat16 [5120, 2048], P(('fsdp', 'ctx'))
- mean_loss: float32 [], replicated
- grad_hidden: float32 [5120, 2048], P(('fsdp', 'ctx'))
- grad_w_query: float32 [2048, 2048], P('fsdp', 'tp')
- grad_w_key: float32 [2048, 1024], P('fsdp', 'tp')
- grad_w_value: float32 [2048, 1024], P('fsdp', 'tp')
- grad_w_out: float32 [2048, 2048], P('tp', 'fsdp')
- grad_w_gate: float32 [2048, 8192], P('fsdp', 'tp')
- grad_w_up: float32 [2048, 8192], P('fsdp', 'tp')
- grad_w_down: float32 [8192, 2048], P('tp', 'fsdp')
- grad_attn_gain: float32 [2048], P('fsdp')
- grad_ffn_gain: float32 [2048], P('fsdp')
Inputs may be any that keep to these rules, and one draw needn't show every extreme that they name: `segment_ids`: tree t fills slots t * 2560 onward and has segments t * 13 to t * 13 + 12 in some numbering: its trunk holds the first 1024 slots, then twelve runs of 128 slots each hold one whole segment, four branches and eight leaves, in any order. `parents`: entry s is the parent of segment s: -1 for a trunk, the trunk of its tree for a branch, a branch of its tree for a leaf, two leaves to each branch. `positions`: trunk slots count 0 up in order; the j-th token of a branch has 1024 + j, of a leaf 9 * 128 + j. `valid_mask`: 0 on exactly the slots of one or two whole absent leaves in each tree, 1 elsewhere.
All inputs are finite; a program needn't handle non-finite values.
Results may differ from a plain program's by a relative error of at most 0.01.
The roundings to bfloat16 on the way count: a program that leaves them out, or rounds other values in their place, can miss the bound.
Values may be sent and summed in bfloat16 or wider, within the bound.
No kernel may reach another device: no remote copies, remote signals or barrier semaphores. Data moves between devices by JAX's collectives and lax.ppermute only.
A program may use at most 256 MiB of HBM per device.

v0:
```python
from functools import partial
import math

import jax
import jax.numpy as jnp
from jax import lax
from jax.sharding import PartitionSpec as P

D = 2048
HD = 128


epsilon = 1e-05
rope_base = 1000000.0


def rms_scale(values, gain):
    return values * lax.rsqrt(jnp.mean(values * values, axis=-1, keepdims=True) + epsilon) * gain


def rope_angles(positions, width):
    steps = jnp.arange(width // 2, dtype=jnp.float32)
    inverse = jnp.power(rope_base, -2.0 * steps / width)
    return positions.astype(jnp.float32)[:, None] * inverse[None, :]


def rotary(values, angles):
    half_width = values.shape[-1] // 2
    cosine = jnp.cos(angles)[:, None, :]
    sine_part = jnp.sin(angles)[:, None, :]
    first_half = values[..., :half_width]
    second_half = values[..., half_width:]
    return jnp.concatenate(
        [
            first_half * cosine - second_half * sine_part,
            second_half * cosine + first_half * sine_part,
        ],
        axis=-1,
    )


def ancestry(segment_ids, parents):
    labels = jnp.arange(parents.shape[0], dtype=jnp.int32)
    parent_of = jnp.sum(
        jnp.where(segment_ids[:, None] == labels[None, :], parents[None, :], 0), axis=1
    )
    grand_raw = jnp.sum(
        jnp.where(parent_of[:, None] == labels[None, :], parents[None, :], 0), axis=1
    )
    grand_of = jnp.where(parent_of < 0, -1, grand_raw)
    return (parent_of, grand_of)


def allowed_pairs(query_seg, query_parent, query_grand, query_place, key_seg, key_valid, key_place):
    same_seg = (key_seg[None, :] == query_seg[:, None]) & (
        key_place[None, :] <= query_place[:, None]
    )
    ancestor_hit = (key_seg[None, :] == query_parent[:, None]) | (
        key_seg[None, :] == query_grand[:, None]
    )
    return (key_valid[None, :] == 1) & (same_seg | ancestor_hit)


def matmul(left, right):
    return jnp.dot(left, right, preferred_element_type=jnp.float32)


def rows_product(left, right):
    return lax.dot_general(
        left, right, (((0,), (0,)), ((), ())), preferred_element_type=jnp.float32
    )


def cols_product(left, right):
    return lax.dot_general(
        left, right, (((1,), (1,)), ((), ())), preferred_element_type=jnp.float32
    )


def swiglu(gate_in, up_in):
    return jax.nn.silu(gate_in) * up_in


def per_device(
    hidden_in,
    teacher,
    w_query,
    w_key,
    w_value,
    w_out,
    w_gate,
    w_up,
    w_down,
    attn_gain,
    ffn_gain,
    segment_ids,
    parents,
    positions,
    valid_mask,
):
    row_count = hidden_in.shape[0]
    ctx_count = lax.axis_size("ctx")
    tree_len = row_count * ctx_count
    unit_len = tree_len // 20
    key_block = min(1024, 4 * unit_len)
    block_count = tree_len // key_block
    score_scale = 1.0 / math.sqrt(HD)
    (
        query_full,
        key_full,
        value_full,
        out_full,
        gate_full,
        up_full,
        down_full,
        attn_gain_all,
        ffn_gain_all,
    ) = (
        lax.all_gather(w_query, "fsdp", axis=0, tiled=True),
        lax.all_gather(w_key, "fsdp", axis=0, tiled=True),
        lax.all_gather(w_value, "fsdp", axis=0, tiled=True),
        lax.all_gather(w_out, "fsdp", axis=1, tiled=True),
        lax.all_gather(w_gate, "fsdp", axis=0, tiled=True),
        lax.all_gather(w_up, "fsdp", axis=0, tiled=True),
        lax.all_gather(w_down, "fsdp", axis=1, tiled=True),
        lax.all_gather(attn_gain, "fsdp", axis=0, tiled=True),
        lax.all_gather(ffn_gain, "fsdp", axis=0, tiled=True),
    )
    gain_attn = attn_gain_all.astype(jnp.float32)
    gain_ffn = ffn_gain_all.astype(jnp.float32)
    head_count = query_full.shape[1] // HD
    kv_heads = key_full.shape[1] // HD
    per_group = head_count // kv_heads
    hidden = hidden_in.astype(jnp.float32)
    angles = rope_angles(positions, HD)
    normed = rms_scale(hidden, gain_attn).astype(jnp.bfloat16)
    query_pre = matmul(normed, query_full).reshape(row_count, head_count, HD)
    key_pre = matmul(normed, key_full).reshape(row_count, kv_heads, HD)
    query_rot, rope_query_back = jax.vjp(partial(rotary, angles=angles), query_pre)
    key_rot, rope_key_back = jax.vjp(partial(rotary, angles=angles), key_pre)
    query_rot = query_rot.astype(jnp.bfloat16)
    key_rot = key_rot.astype(jnp.bfloat16)
    value_b = matmul(normed, value_full).astype(jnp.bfloat16)
    key_meta = (segment_ids * 2 + valid_mask).astype(jnp.float32).astype(jnp.bfloat16)
    query_parent, query_grand = ancestry(segment_ids, parents)
    query_place = lax.axis_index("ctx") * row_count + jnp.arange(row_count, dtype=jnp.int32)
    grouped = query_rot.reshape(row_count, kv_heads, per_group, HD)
    carried = (
        lax.all_gather(key_rot.reshape(row_count, kv_heads * HD), "ctx", axis=0, tiled=True),
        lax.all_gather(value_b, "ctx", axis=0, tiled=True),
        lax.all_gather(key_meta, "ctx", axis=0, tiled=True),
    )

    def blocks_of(gathered):
        keys_all, values_all, meta_all = gathered
        return (
            keys_all.reshape(block_count, key_block, kv_heads, HD),
            values_all.reshape(block_count, key_block, kv_heads, HD),
            meta_all.reshape(block_count, key_block),
            jnp.arange(block_count, dtype=jnp.int32) * key_block,
        )

    def unnormed_of(keys_blk, meta_blk, key_start):
        meta_int = meta_blk.astype(jnp.float32).astype(jnp.int32)
        allowed = allowed_pairs(
            segment_ids,
            query_parent,
            query_grand,
            query_place,
            meta_int // 2,
            meta_int % 2,
            key_start + jnp.arange(key_block, dtype=jnp.int32),
        )
        scores = (
            jnp.einsum("rkgd,skd->kgrs", grouped, keys_blk, preferred_element_type=jnp.float32)
            * score_scale
        )
        return jnp.where(allowed[None, None], jnp.exp(scores), 0.0)

    def forward_step(carry, block_data):
        row_total, accumulated = carry
        keys_blk, values_blk, meta_blk, key_start = block_data
        unnormed = unnormed_of(keys_blk, meta_blk, key_start)
        row_total = row_total + jnp.sum(unnormed, axis=-1)
        accumulated = accumulated + jnp.einsum(
            "kgrs,skd->kgrd",
            unnormed.astype(jnp.bfloat16),
            values_blk,
            preferred_element_type=jnp.float32,
        )
        return ((row_total, accumulated), None)

    start_total = jnp.zeros((kv_heads, per_group, row_count), jnp.float32)
    start_accum = jnp.zeros((kv_heads, per_group, row_count, HD), jnp.float32)
    (row_total, accumulated), _ = lax.scan(
        forward_step, (start_total, start_accum), blocks_of(carried)
    )
    context = accumulated / row_total[..., None]
    attended = (
        context.transpose(2, 0, 1, 3).reshape(row_count, head_count * HD).astype(jnp.bfloat16)
    )
    attn_out = lax.psum(matmul(attended, out_full), "tp")
    middle = hidden + attn_out
    normed_ffn = rms_scale(middle, gain_ffn).astype(jnp.bfloat16)
    gate_proj = matmul(normed_ffn, gate_full)
    up_proj = matmul(normed_ffn, up_full)
    activated_f, swiglu_back = jax.vjp(swiglu, gate_proj, up_proj)
    activated = activated_f.astype(jnp.bfloat16)
    ffn_out = lax.psum(matmul(activated, down_full), "tp")
    output_f = middle + ffn_out
    deviation = output_f - teacher.astype(jnp.float32)
    valid_f = valid_mask.astype(jnp.float32)
    valid_count, error_sum = lax.psum(
        (jnp.sum(valid_f), jnp.sum(valid_f * jnp.mean(deviation * deviation, axis=1))),
        ("fsdp", "ctx"),
    )
    loss_value = error_sum / valid_count
    tokens_all = row_count * lax.axis_size("fsdp") * ctx_count
    loss_factor = float(D * tokens_all // 2)
    grad_output = loss_factor * 2.0 / D * valid_f[:, None] * deviation / valid_count
    grad_ffn = grad_output.astype(jnp.bfloat16)
    grad_w_down = rows_product(activated, grad_ffn)
    grad_act = cols_product(grad_ffn, down_full)
    grad_gate_f, grad_up_f = swiglu_back(grad_act)
    grad_gate = grad_gate_f.astype(jnp.bfloat16)
    grad_up = grad_up_f.astype(jnp.bfloat16)
    grad_w_gate = rows_product(normed_ffn, grad_gate)
    grad_w_up = rows_product(normed_ffn, grad_up)
    grad_normed_ffn = lax.psum(
        cols_product(grad_gate, gate_full) + cols_product(grad_up, up_full), "tp"
    )
    _, norm_ffn_back = jax.vjp(rms_scale, middle, gain_ffn)
    grad_middle_part, grad_ffn_gain = norm_ffn_back(grad_normed_ffn)
    grad_middle = grad_output + grad_middle_part
    grad_attn = grad_middle.astype(jnp.bfloat16)
    grad_w_out = rows_product(attended, grad_attn)
    grad_context = (
        cols_product(grad_attn, out_full)
        .reshape(row_count, kv_heads, per_group, HD)
        .transpose(1, 2, 0, 3)
    )
    grad_accum = (grad_context / row_total[..., None]).astype(jnp.bfloat16)
    delta_row = jnp.sum(grad_context * context, axis=-1) / row_total

    def backward_step(grad_query_acc, block_data):
        keys_blk, values_blk, meta_blk, key_start = block_data
        unnormed = unnormed_of(keys_blk, meta_blk, key_start)
        grad_prob = jnp.einsum(
            "kgrd,skd->kgrs", grad_accum, values_blk, preferred_element_type=jnp.float32
        )
        grad_scores = (unnormed * (grad_prob - delta_row[..., None])).astype(jnp.bfloat16)
        grad_query_acc = grad_query_acc + jnp.einsum(
            "kgrs,skd->kgrd", grad_scores, keys_blk, preferred_element_type=jnp.float32
        )
        key_term = jnp.einsum(
            "kgrs,rkgd->skd", grad_scores, grouped, preferred_element_type=jnp.float32
        )
        value_term = jnp.einsum(
            "kgrs,kgrd->skd",
            unnormed.astype(jnp.bfloat16),
            grad_accum,
            preferred_element_type=jnp.float32,
        )
        return (
            grad_query_acc,
            (
                key_term.reshape(key_block, kv_heads * HD),
                value_term.reshape(key_block, kv_heads * HD),
            ),
        )

    grad_query_rot, (key_terms, value_terms) = lax.scan(
        backward_step,
        jnp.zeros((kv_heads, per_group, row_count, HD), jnp.float32),
        blocks_of(carried),
    )
    key_sums, value_sums = (
        lax.psum_scatter(
            key_terms.reshape(tree_len, kv_heads * HD) * score_scale,
            "ctx",
            scatter_dimension=0,
            tiled=True,
        ),
        lax.psum_scatter(
            value_terms.reshape(tree_len, kv_heads * HD), "ctx", scatter_dimension=0, tiled=True
        ),
    )
    grad_query_rows = (
        grad_query_rot.transpose(2, 0, 1, 3).reshape(row_count, head_count, HD) * score_scale
    )
    grad_query = (
        rope_query_back(grad_query_rows)[0].reshape(row_count, head_count * HD).astype(jnp.bfloat16)
    )
    grad_key = (
        rope_key_back(key_sums.reshape(row_count, kv_heads, HD))[0]
        .reshape(row_count, kv_heads * HD)
        .astype(jnp.bfloat16)
    )
    grad_value = value_sums.astype(jnp.bfloat16)
    grad_w_query = rows_product(normed, grad_query)
    grad_w_key = rows_product(normed, grad_key)
    grad_w_value = rows_product(normed, grad_value)
    grad_normed = lax.psum(
        cols_product(grad_query, query_full)
        + cols_product(grad_key, key_full)
        + cols_product(grad_value, value_full),
        "tp",
    )
    _, norm_attn_back = jax.vjp(rms_scale, hidden, gain_attn)
    grad_hidden_part, grad_attn_gain = norm_attn_back(grad_normed)
    grad_hidden = grad_middle + grad_hidden_part
    halves = (
        lax.psum_scatter(grad_w_query, "fsdp", scatter_dimension=0, tiled=True),
        lax.psum_scatter(grad_w_key, "fsdp", scatter_dimension=0, tiled=True),
        lax.psum_scatter(grad_w_value, "fsdp", scatter_dimension=0, tiled=True),
        lax.psum_scatter(grad_w_out, "fsdp", scatter_dimension=1, tiled=True),
        lax.psum_scatter(grad_w_gate, "fsdp", scatter_dimension=0, tiled=True),
        lax.psum_scatter(grad_w_up, "fsdp", scatter_dimension=0, tiled=True),
        lax.psum_scatter(grad_w_down, "fsdp", scatter_dimension=1, tiled=True),
        lax.psum_scatter(grad_attn_gain, "fsdp", scatter_dimension=0, tiled=True),
        lax.psum_scatter(grad_ffn_gain, "fsdp", scatter_dimension=0, tiled=True),
    )
    slices = (
        lax.psum_scatter(halves[0], "ctx", scatter_dimension=0, tiled=True),
        lax.psum_scatter(halves[1], "ctx", scatter_dimension=0, tiled=True),
        lax.psum_scatter(halves[2], "ctx", scatter_dimension=0, tiled=True),
        lax.psum_scatter(halves[3], "ctx", scatter_dimension=1, tiled=True),
        lax.psum_scatter(halves[4], "ctx", scatter_dimension=0, tiled=True),
        lax.psum_scatter(halves[5], "ctx", scatter_dimension=0, tiled=True),
        lax.psum_scatter(halves[6], "ctx", scatter_dimension=1, tiled=True),
        lax.psum_scatter(halves[7], "ctx", scatter_dimension=0, tiled=True),
        lax.psum_scatter(halves[8], "ctx", scatter_dimension=0, tiled=True),
    )
    reduced = (
        lax.all_gather(slices[0], "ctx", axis=0, tiled=True),
        lax.all_gather(slices[1], "ctx", axis=0, tiled=True),
        lax.all_gather(slices[2], "ctx", axis=0, tiled=True),
        lax.all_gather(slices[3], "ctx", axis=1, tiled=True),
        lax.all_gather(slices[4], "ctx", axis=0, tiled=True),
        lax.all_gather(slices[5], "ctx", axis=0, tiled=True),
        lax.all_gather(slices[6], "ctx", axis=1, tiled=True),
        lax.all_gather(slices[7], "ctx", axis=0, tiled=True),
        lax.all_gather(slices[8], "ctx", axis=0, tiled=True),
    )
    return (
        output_f.astype(jnp.bfloat16),
        loss_value,
        grad_hidden,
        reduced[0],
        reduced[1],
        reduced[2],
        reduced[3],
        reduced[4],
        reduced[5],
        reduced[6],
        reduced[7],
        reduced[8],
    )


def solution(mesh):
    placed = (
        P(("fsdp", "ctx"), None),
        P(("fsdp", "ctx"), None),
        P("fsdp", "tp"),
        P("fsdp", "tp"),
        P("fsdp", "tp"),
        P("tp", "fsdp"),
        P("fsdp", "tp"),
        P("fsdp", "tp"),
        P("tp", "fsdp"),
        P("fsdp"),
        P("fsdp"),
        P(("fsdp", "ctx")),
        P(),
        P(("fsdp", "ctx")),
        P(("fsdp", "ctx")),
    )
    return jax.shard_map(
        per_device,
        mesh=mesh,
        in_specs=placed,
        out_specs=(
            P(("fsdp", "ctx"), None),
            P(),
            P(("fsdp", "ctx"), None),
            P("fsdp", "tp"),
            P("fsdp", "tp"),
            P("fsdp", "tp"),
            P("tp", "fsdp"),
            P("fsdp", "tp"),
            P("fsdp", "tp"),
            P("tp", "fsdp"),
            P("fsdp"),
            P("fsdp"),
        ),
        check_vma=False,
    )
```

profile of v0, /device:TPU:0, one launch (start us, length us, event | category | flops | bytes accessed | tf_op | source)
XLA Modules:
  0.0 3236.9 jit_solution(8783736360348244462)
XLA Ops:
  98.8 27.1 all-gather.22.cloned.1.call-done
  130.1 29.5 all-gather.28.cloned.1.call-done
  165.0 56.1 %while.32 = (s32[]{:T(128)}, f32[2,2,640]{2,1,0:T(2,128)S(1)}, f32[2,2,640,128]{3,2,1,0:T(8,128)S(1)}, bf16[5,512]{1,0:T(8,128)(2,1)S(1)}, s32[640]{0:T(1024)S(1...) while((s32[]{:T(128)}, f32[2,2,640]{2,1,0:T(2,128)S(1)}, ...), condition=%wide.region_5.6_spmd.clone, body=%wide.region_3.5_spmd.clone.sunk | while | flops 682245248 | bytes 15338668 | solution.py:195
  235.5 95.0 %all-reduce.15.cloned.1.call-done = f32[640,2048]{1,0:T(8,128)} async-done(((f32[640,2048]{1,0:T(8,128)}), f32[640,2048]{1,0:T(8,128)}) %all-reduce.15.cloned.1.call-update) | async-done | bytes 5242896 | tf_op jit(solution)/shard_map/psum | solution.py:202
  336.5 99.6 %all-gather.32.cloned.1.call-done = bf16[2048,2048]{1,0:T(8,128)(2,1)} async-done(((bf16[1024,2048]{1,0:T(8,128)(2,1)}), bf16[2048,2048]{1,0:T(8,128)(2,1)}) %all-gather.32.cloned.1.call-update) | async-done | bytes 8388624 | tf_op jit(solution)/shard_map/all_gather | solution.py:123
  445.6 96.2 %all-gather.34.cloned.1.call-done = bf16[2048,2048]{1,0:T(8,128)(2,1)} async-done(((bf16[1024,2048]{1,0:T(8,128)(2,1)}), bf16[2048,2048]{1,0:T(8,128)(2,1)}) %all-gather.34.cloned.1.call-update) | async-done | bytes 8388624 | tf_op jit(solution)/shard_map/all_gather | solution.py:124
  554.1 93.1 %all-gather.36.cloned.1.call-done = bf16[2048,2048]{1,0:T(8,128)(2,1)} async-done(((bf16[2048,1024]{1,0:T(8,128)(2,1)}), bf16[2048,2048]{1,0:T(8,128)(2,1)}) %all-gather.36.cloned.1.call-update) | async-done | bytes 8388624 | tf_op jit(solution)/shard_map/all_gather | solution.py:125
  658.9 21.4 psum.45
  680.3 80.7 %all-reduce.17.cloned.1.call-done = f32[640,2048]{1,0:T(8,128)} async-done(((f32[640,2048]{1,0:T(8,128)}), f32[640,2048]{1,0:T(8,128)}) %all-reduce.17.cloned.1.call-update) | async-done | bytes 5242896 | tf_op jit(solution)/shard_map/psum | solution.py:209
  804.5 102.4 %all-reduce.19.cloned.1.call-done = f32[640,2048]{1,0:T(8,128)} async-done(((f32[640,2048]{1,0:T(8,128)}), f32[640,2048]{1,0:T(8,128)}) %all-reduce.19.cloned.1.call-update) | async-done | bytes 5242896 | tf_op jit(solution)/shard_map/psum | solution.py:229
  924.5 115.2 %while.33 = (s32[]{:T(128)}, f32[2,2,640,128]{3,2,1,0:T(8,128)}, f32[5,512,256]{2,1,0:T(8,128)}, f32[5,512,256]{2,1,0:T(8,128)}, bf16[5,512]{1,0:T(8,128)(2,1)S(...) while((s32[]{:T(128)}, f32[2,2,640,128]{3,2,1,0:T(8,128)}, ...), condition=%wide.region_18.19_spmd.clone, body=%wide.region_17.18_spmd.clone.sunk | while | flops 1691497088 | bytes 59480820 | solution.py:272
  1044.1 51.6 %reduce-scatter.17.cloned.1.call-done = f32[640,256]{1,0:T(8,128)} async-done(((f32[2560,256]{1,0:T(8,128)}), f32[640,256]{1,0:T(8,128)}) %reduce-scatter.17.cloned.1.call-update) | async-done | bytes 655376 | tf_op jit(solution)/shard_map/reduce_scatter | solution.py:278
  1102.6 47.2 %reduce-scatter.19.cloned.1.call-done = f32[640,256]{1,0:T(8,128)} async-done(((f32[2560,256]{1,0:T(8,128)}), f32[640,256]{1,0:T(8,128)}) %reduce-scatter.19.cloned.1.call-update) | async-done | bytes 655376 | tf_op jit(solution)/shard_map/reduce_scatter | solution.py:284
  1218.6 57.0 %reduce-scatter.21.cloned.1.call-done = f32[1024,512]{1,0:T(8,128)} async-done(((f32[2048,512]{1,0:T(8,128)}), f32[1024,512]{1,0:T(8,128)}) %reduce-scatter.21.cloned.1.call-update) | async-done | bytes 2097168 | tf_op jit(solution)/shard_map/reduce_scatter | solution.py:313
  1275.7 57.1 %reduce-scatter.33.cloned.1.call-done = f32[512,1024]{1,0:T(8,128)} async-done(((f32[512,2048]{1,0:T(8,128)}), f32[512,1024]{1,0:T(8,128)}) %reduce-scatter.33.cloned.1.call-update) | async-done | bytes 2097168 | tf_op jit(solution)/shard_map/reduce_scatter | solution.py:316
  1332.9 191.4 %reduce-scatter.45.cloned.1.call-done = f32[2048,1024]{1,0:T(8,128)} async-done(((f32[2048,2048]{1,0:T(8,128)}), f32[2048,1024]{1,0:T(8,128)}) %reduce-scatter.45.cloned.1.call-update) | async-done | bytes 8388624 | tf_op jit(solution)/shard_map/reduce_scatter | solution.py:319
  1524.3 191.3 %reduce-scatter.37.cloned.1.call-done = f32[1024,2048]{1,0:T(8,128)} async-done(((f32[2048,2048]{1,0:T(8,128)}), f32[1024,2048]{1,0:T(8,128)}) %reduce-scatter.37.cloned.1.call-update) | async-done | bytes 8388624 | tf_op jit(solution)/shard_map/reduce_scatter | solution.py:317
  1715.7 191.4 %reduce-scatter.41.cloned.1.call-done = f32[1024,2048]{1,0:T(8,128)} async-done(((f32[2048,2048]{1,0:T(8,128)}), f32[1024,2048]{1,0:T(8,128)}) %reduce-scatter.41.cloned.1.call-update) | async-done | bytes 8388624 | tf_op jit(solution)/shard_map/reduce_scatter | solution.py:318
  1915.3 21.4 reduce-scatter.27.cloned.1.call-done
  1936.8 28.0 reduce-scatter.31.cloned.1.call-done
  1964.9 44.7 %reduce-scatter.23.cloned.1.call-done = f32[256,512]{1,0:T(8,128)} async-done(((f32[1024,512]{1,0:T(8,128)}), f32[256,512]{1,0:T(8,128)}) %reduce-scatter.23.cloned.1.call-update) | async-done | bytes 524304 | tf_op jit(solution)/shard_map/reduce_scatter | solution.py:324
  2009.7 45.4 %reduce-scatter.35.cloned.1.call-done = f32[512,256]{1,0:T(8,128)} async-done(((f32[512,1024]{1,0:T(8,128)}), f32[512,256]{1,0:T(8,128)}) %reduce-scatter.35.cloned.1.call-update) | async-done | bytes 524304 | tf_op jit(solution)/shard_map/reduce_scatter | solution.py:327
  2055.2 146.1 %reduce-scatter.47.cloned.1.call-done = f32[2048,256]{1,0:T(8,128)} async-done(((f32[2048,1024]{1,0:T(8,128)}), f32[2048,256]{1,0:T(8,128)}) %reduce-scatter.47.cloned.1.call-update) | async-done | bytes 2097168 | tf_op jit(solution)/shard_map/reduce_scatter | solution.py:330
  2201.4 147.5 %reduce-scatter.39.cloned.1.call-done = f32[256,2048]{1,0:T(8,128)} async-done(((f32[1024,2048]{1,0:T(8,128)}), f32[256,2048]{1,0:T(8,128)}) %reduce-scatter.39.cloned.1.call-update) | async-done | bytes 2097168 | tf_op jit(solution)/shard_map/reduce_scatter | solution.py:328
  2348.9 147.6 %reduce-scatter.43.cloned.1.call-done = f32[256,2048]{1,0:T(8,128)} async-done(((f32[1024,2048]{1,0:T(8,128)}), f32[256,2048]{1,0:T(8,128)}) %reduce-scatter.43.cloned.1.call-update) | async-done | bytes 2097168 | tf_op jit(solution)/shard_map/reduce_scatter | solution.py:329
  2499.7 22.0 psum.44
  2523.0 79.9 %all-reduce.21.cloned.1.call-done = f32[640,2048]{1,0:T(8,128)} async-done(((f32[640,2048]{1,0:T(8,128)}), f32[640,2048]{1,0:T(8,128)}) %all-reduce.21.cloned.1.call-update) | async-done | bytes 5242896 | tf_op jit(solution)/shard_map/psum | solution.py:303
  2662.3 47.1 %all-gather.38.cloned.1.call-done = f32[1024,512]{1,0:T(8,128)} async-done(((f32[256,512]{1,0:T(8,128)}), f32[1024,512]{1,0:T(8,128)}) %all-gather.38.cloned.1.call-update) | async-done | bytes 2097168 | tf_op jit(solution)/shard_map/all_gather | solution.py:335
  2709.4 46.2 %all-gather.44.cloned.1.call-done = f32[512,1024]{1,0:T(8,128)} async-done(((f32[512,256]{1,0:T(8,128)}), f32[512,1024]{1,0:T(8,128)}) %all-gather.44.cloned.1.call-update) | async-done | bytes 2097168 | tf_op jit(solution)/shard_map/all_gather | solution.py:338
  2755.6 150.0 %all-gather.50.cloned.1.call-done = f32[2048,1024]{1,0:T(8,128)} async-done(((f32[2048,256]{1,0:T(8,128)}), f32[2048,1024]{1,0:T(8,128)}) %all-gather.50.cloned.1.call-update) | async-done | bytes 8388624 | tf_op jit(solution)/shard_map/all_gather | solution.py:341
  2905.6 149.5 %all-gather.46.cloned.1.call-done = f32[1024,2048]{1,0:T(8,128)} async-done(((f32[256,2048]{1,0:T(8,128)}), f32[1024,2048]{1,0:T(8,128)}) %all-gather.46.cloned.1.call-update) | async-done | bytes 8388624 | tf_op jit(solution)/shard_map/all_gather | solution.py:339
  3055.1 149.4 %all-gather.48.cloned.1.call-done = f32[1024,2048]{1,0:T(8,128)} async-done(((f32[256,2048]{1,0:T(8,128)}), f32[1024,2048]{1,0:T(8,128)}) %all-gather.48.cloned.1.call-update) | async-done | bytes 8388624 | tf_op jit(solution)/shard_map/all_gather | solution.py:340
  (423 shorter events, 560.5 us)
Async XLA Ops:
  9.4 116.5 %all-gather.22.cloned.1.call-start = ((), (), s32[]{:S(2)}) async-start(), calls=%async_computation.17 | async-start | bytes 1638400 | tf_op jit(solution)/shard_map/all_gather | solution.py:149
  37.8 121.8 %all-gather.28.cloned.1.call-start = ((), (), s32[]{:S(2)}) async-start(), calls=%async_computation.20 | async-start | bytes 1638400 | tf_op jit(solution)/shard_map/all_gather | solution.py:150
  59.4 163.3 %all-gather.30.cloned.1.call-start = ((), (), s32[]{:S(2)}) async-start(), calls=%async_computation.21 | async-start | bytes 3145728 | tf_op jit(solution)/shard_map/all_gather | solution.py:122
  59.9 270.5 %all-reduce.15.cloned.1.call-start = ((), (), s32[]{:S(2)}) async-start(), calls=%async_computation.22 | async-start | bytes 10485760 | tf_op jit(solution)/shard_map/psum | solution.py:202
  228.8 207.4 %all-gather.32.cloned.1.call-start = ((), (), s32[]{:S(2)}) async-start(), calls=%async_computation.23 | async-start | bytes 12582912 | tf_op jit(solution)/shard_map/all_gather | solution.py:123
  229.6 312.2 %all-gather.34.cloned.1.call-start = ((), (), s32[]{:S(2)}) async-start(), calls=%async_computation.24 | async-start | bytes 12582912 | tf_op jit(solution)/shard_map/all_gather | solution.py:124
  230.3 416.9 %all-gather.36.cloned.1.call-start = ((), (), s32[]{:S(2)}) async-start(), calls=%async_computation.25 | async-start | bytes 12582912 | tf_op jit(solution)/shard_map/all_gather | solution.py:125
  230.9 530.1 %all-reduce.17.cloned.1.call-start = ((), (), s32[]{:S(2)}) async-start(), calls=%async_computation.26 | async-start | bytes 10485760 | tf_op jit(solution)/shard_map/psum | solution.py:209
  658.2 248.6 %all-reduce.19.cloned.1.call-start = ((), (), s32[]{:S(2)}) async-start(), calls=%async_computation.27 | async-start | bytes 10485760 | tf_op jit(solution)/shard_map/psum | solution.py:229
  804.0 291.8 %reduce-scatter.17.cloned.1.call-start = ((), (), s32[]{:S(2)}) async-start(), calls=%async_computation.28 | async-start | bytes 3276800 | tf_op jit(solution)/shard_map/reduce_scatter | solution.py:278
  1043.9 169.1 %reduce-scatter.25.cloned.1.call-start = ((), (), s32[]{:S(2)}) async-start(), calls=%async_computation.34 | async-start | bytes 3145728 | tf_op jit(solution)/shard_map/reduce_scatter | solution.py:314
  1102.5 116.1 %reduce-scatter.29.cloned.1.call-start = ((), (), s32[]{:S(2)}) async-start(), calls=%async_computation.37 | async-start | bytes 3145728 | tf_op jit(solution)/shard_map/reduce_scatter | solution.py:315
  1154.2 121.4 %reduce-scatter.21.cloned.1.call-start = ((), (), s32[]{:S(2)}) async-start(), calls=%async_computation.31 | async-start | bytes 6291456 | tf_op jit(solution)/shard_map/reduce_scatter | solution.py:313
  1168.0 164.8 %reduce-scatter.33.cloned.1.call-start = ((), (), s32[]{:S(2)}) async-start(), calls=%async_computation.40 | async-start | bytes 6291456 | tf_op jit(solution)/shard_map/reduce_scatter | solution.py:316
  1174.4 349.9 %reduce-scatter.45.cloned.1.call-start = ((), (), s32[]{:S(2)}) async-start(), calls=%async_computation.49 | async-start | bytes 25165824 | tf_op jit(solution)/shard_map/reduce_scatter | solution.py:319
  1187.6 528.0 %reduce-scatter.37.cloned.1.call-start = ((), (), s32[]{:S(2)}) async-start(), calls=%async_computation.43 | async-start | bytes 25165824 | tf_op jit(solution)/shard_map/reduce_scatter | solution.py:317
  1200.4 706.8 %reduce-scatter.41.cloned.1.call-start = ((), (), s32[]{:S(2)}) async-start(), calls=%async_computation.46 | async-start | bytes 25165824 | tf_op jit(solution)/shard_map/reduce_scatter | solution.py:318
  1213.0 723.7 %reduce-scatter.27.cloned.1.call-start = ((), (), s32[]{:S(2)}) async-start(), calls=%async_computation.35 | async-start | bytes 1310720 | tf_op jit(solution)/shard_map/reduce_scatter | solution.py:325
  1213.7 751.1 %reduce-scatter.31.cloned.1.call-start = ((), (), s32[]{:S(2)}) async-start(), calls=%async_computation.38 | async-start | bytes 1310720 | tf_op jit(solution)/shard_map/reduce_scatter | solution.py:326
  1218.6 791.0 %reduce-scatter.23.cloned.1.call-start = ((), (), s32[]{:S(2)}) async-start(), calls=%async_computation.32 | async-start | bytes 2621440 | tf_op jit(solution)/shard_map/reduce_scatter | solution.py:324
  1275.7 779.5 %reduce-scatter.35.cloned.1.call-start = ((), (), s32[]{:S(2)}) async-start(), calls=%async_computation.41 | async-start | bytes 2621440 | tf_op jit(solution)/shard_map/reduce_scatter | solution.py:327
  1332.8 868.5 %reduce-scatter.47.cloned.1.call-start = ((), (), s32[]{:S(2)}) async-start(), calls=%async_computation.50 | async-start | bytes 10485760 | tf_op jit(solution)/shard_map/reduce_scatter | solution.py:330
  1524.3 824.6 %reduce-scatter.39.cloned.1.call-start = ((), (), s32[]{:S(2)}) async-start(), calls=%async_computation.44 | async-start | bytes 10485760 | tf_op jit(solution)/shard_map/reduce_scatter | solution.py:328
  1715.7 780.8 %reduce-scatter.43.cloned.1.call-start = ((), (), s32[]{:S(2)}) async-start(), calls=%async_computation.47 | async-start | bytes 10485760 | tf_op jit(solution)/shard_map/reduce_scatter | solution.py:329
  1907.2 695.8 %all-reduce.21.cloned.1.call-start = ((), (), s32[]{:S(2)}) async-start(), calls=%async_computation.30 | async-start | bytes 10485760 | tf_op jit(solution)/shard_map/psum | solution.py:303
  1915.3 737.3 %all-gather.40.cloned.1.call-start = ((), (), s32[]{:S(2)}) async-start(), calls=%async_computation.36 | async-start | bytes 1310720 | tf_op jit(solution)/shard_map/all_gather | solution.py:336
  1936.7 725.5 %all-gather.42.cloned.1.call-start = ((), (), s32[]{:S(2)}) async-start(), calls=%async_computation.39 | async-start | bytes 1310720 | tf_op jit(solution)/shard_map/all_gather | solution.py:337
  1964.9 744.5 %all-gather.38.cloned.1.call-start = ((), (), s32[]{:S(2)}) async-start(), calls=%async_computation.33 | async-start | bytes 2621440 | tf_op jit(solution)/shard_map/all_gather | solution.py:335
  2009.7 745.9 %all-gather.44.cloned.1.call-start = ((), (), s32[]{:S(2)}) async-start(), calls=%async_computation.42 | async-start | bytes 2621440 | tf_op jit(solution)/shard_map/all_gather | solution.py:338
  2055.2 850.4 %all-gather.50.cloned.1.call-start = ((), (), s32[]{:S(2)}) async-start(), calls=%async_computation.51 | async-start | bytes 10485760 | tf_op jit(solution)/shard_map/all_gather | solution.py:341
  2201.3 853.8 %all-gather.46.cloned.1.call-start = ((), (), s32[]{:S(2)}) async-start(), calls=%async_computation.45 | async-start | bytes 10485760 | tf_op jit(solution)/shard_map/all_gather | solution.py:339
  2348.9 855.6 %all-gather.48.cloned.1.call-start = ((), (), s32[]{:S(2)}) async-start(), calls=%async_computation.48 | async-start | bytes 10485760 | tf_op jit(solution)/shard_map/all_gather | solution.py:340
  (67 other events, 5704.7 us)
Sparse Core Ops, SparseCore 0:
  58.0 33.1 all-gather.23
  93.2 32.6 all-gather.21
  127.9 31.6 all-gather.27
  161.0 32.0 all-gather.29
  228.9 101.4 all-reduce.14
  331.9 104.1 all-gather.31
  437.7 103.9 all-gather.33
  543.1 103.9 all-gather.35
  658.4 102.5 all-reduce.16
  804.1 102.6 all-reduce.18
  1043.5 52.2 reduce-scatter.16
  1097.9 51.7 reduce-scatter.18
  1152.4 31.4 reduce-scatter.24
  1186.7 31.8 reduce-scatter.28
  1221.3 54.3 reduce-scatter.20
  1278.5 54.2 reduce-scatter.32
  1335.1 189.1 reduce-scatter.44
  1526.5 189.1 reduce-scatter.36
  1718.0 189.1 reduce-scatter.40
  1967.1 42.5 reduce-scatter.22
  2011.9 43.1 reduce-scatter.34
  2057.5 143.7 reduce-scatter.46
  2203.6 145.1 reduce-scatter.38
  2351.3 145.1 reduce-scatter.42
  2499.6 103.2 all-reduce.20
  2604.4 28.6 all-gather.39
  2634.8 27.4 all-gather.41
  2663.9 45.4 all-gather.37
  2710.9 44.6 all-gather.43
  2757.2 148.3 all-gather.49
  2907.3 147.8 all-gather.45
  3056.6 147.8 all-gather.47
  (4 shorter events, 98.0 us)
where the time goes:
time: 3240 us
  waiting for transfers between devices  2680 us (83%)
  matrix products  275 us (8%)
  blocking collectives  105 us (3%)
  local copies, waits for them, and re-layouts  87.8 us (3%)
  other arithmetic  63.1 us (2%)
    reduce_scatter x1, waiting for transfers between devices, per_device(): lax.psum_scatter(grad_w_down, 'fsdp', scatter_dimension=1, tiled=True)  191 us
    reduce_scatter x1, waiting for transfers between devices, per_device(): lax.psum_scatter(grad_w_up, 'fsdp', scatter_dimension=0, tiled=True)  191 us
    reduce_scatter x1, waiting for transfers between devices, per_device(): lax.psum_scatter(grad_w_gate, 'fsdp', scatter_dimension=0, tiled=True)  191 us
    all_gather x1, waiting for transfers between devices, per_device(): lax.all_gather(slices[6], 'ctx', axis=1, tiled=True)  150 us
    all_gather x1, waiting for transfers between devices, per_device(): lax.all_gather(slices[4], 'ctx', axis=0, tiled=True)  150 us
    all_gather x1, waiting for transfers between devices, per_device(): lax.all_gather(slices[5], 'ctx', axis=0, tiled=True)  149 us
    reduce_scatter x1, waiting for transfers between devices, per_device(): lax.psum_scatter(halves[5], 'ctx', scatter_dimension=0, tiled=True)  148 us
    reduce_scatter x1, waiting for transfers between devices, per_device(): lax.psum_scatter(halves[4], 'ctx', scatter_dimension=0, tiled=True)  147 us
  transfers between devices with their start and end apart: 36, of which 33 were waited for; matrix products, arithmetic and copies ran while one was open for 6% of the time, Pallas kernels for 0%

commit v1 on v0

v1 whole, which is shorter than its diff:
```python
from functools import partial
import math

import jax
import jax.numpy as jnp
from jax import lax
from jax.experimental import pallas as pl
from jax.experimental.pallas import tpu as pltpu
from jax.sharding import PartitionSpec as P

HD = 128
BLK = 128
EPSILON = 1e-05
ROPE_BASE = 1000000.0
SCALE = 1.0 / math.sqrt(HD)
F32 = jnp.float32
BF16 = jnp.bfloat16
VMEM_LIMIT = 56 * 1024 * 1024
BIG = 1 << 30


def swap_x(a):
    return lax.ppermute(a, "fsdp", [(0, 1), (1, 0)])


def swap_core(a):
    return lax.ppermute(a, "tp", [(0, 1), (1, 0), (2, 3), (3, 2)])


def swap_y(a):
    return lax.ppermute(a, "tp", [(0, 2), (2, 0), (1, 3), (3, 1)])


def swap_xy(a):
    pairs = [(f * 4 + t, (1 - f) * 4 + (t ^ 2)) for f in range(2) for t in range(4)]
    return lax.ppermute(a, ("fsdp", "tp"), pairs)


def after(value, *others):
    return lax.optimization_barrier((value, *others))[0]


def halves_swapped(a):
    half = a.shape[-1] // 2
    return jnp.concatenate([a[..., half:], a[..., :half]], axis=-1)


def table(values, index):
    out = jnp.int32(values[-1])
    for i, v in enumerate(values[:-1]):
        out = jnp.where(index == i, jnp.int32(v), out)
    return out


def dot(a, b, out=F32):
    return jnp.dot(a, b, preferred_element_type=F32).astype(out)


def dot_tn(a, b, out=F32):
    return lax.dot_general(
        a, b, (((0,), (0,)), ((), ())), preferred_element_type=F32
    ).astype(out)


def dot_nt(a, b, out=F32):
    return lax.dot_general(
        a, b, (((1,), (1,)), ((), ())), preferred_element_type=F32
    ).astype(out)


def kdot(a, b, ca, cb):
    return lax.dot_general(a, b, (((ca,), (cb,)), ((), ())), preferred_element_type=F32)


def rms_scale(values, gain):
    return (
        values
        * lax.rsqrt(jnp.mean(values * values, axis=-1, keepdims=True) + EPSILON)
        * gain
    )


def swiglu(gate_in, up_in):
    return jax.nn.silu(gate_in) * up_in


def rope_tables(positions):
    steps = jnp.arange(HD // 2, dtype=F32)
    inverse = jnp.power(ROPE_BASE, -2.0 * steps / HD)
    angles = positions.astype(F32)[:, None] * inverse[None, :]
    cosine, sine = jnp.cos(angles), jnp.sin(angles)
    return (
        jnp.concatenate([cosine, cosine], axis=1),
        jnp.concatenate([-sine, sine], axis=1),
    )


def qkv_kernel(nq, nk, part_ref, x_ref, w_ref, cos_ref, sin_ref, q_ref, kv_ref):
    acc = part_ref[...] + kdot(x_ref[...], w_ref[...], 1, 0)
    cosine, sine = cos_ref[...], sin_ref[...]
    for h in range(nq + nk):
        u = acc[:, h * HD : (h + 1) * HD]
        r = (u * cosine + pltpu.roll(u, HD // 2, 1) * sine).astype(BF16)
        if h < nq:
            q_ref[:, h * HD : (h + 1) * HD] = r
        else:
            kv_ref[:, (h - nq) * HD : (h - nq + 1) * HD] = r
    kv_ref[:, nk * HD :] = acc[:, (nq + nk) * HD :].astype(BF16)


def qkv_call(part, x, w, cosine, sine, nq, nk):
    rows, width = part.shape
    depth = x.shape[1]
    return pl.pallas_call(
        partial(qkv_kernel, nq, nk),
        grid=(rows // BLK,),
        in_specs=[
            pl.BlockSpec((BLK, width), lambda i: (i, 0)),
            pl.BlockSpec((BLK, depth), lambda i: (i, 0)),
            pl.BlockSpec((depth, width), lambda i: (0, 0)),
            pl.BlockSpec((BLK, HD), lambda i: (i, 0)),
            pl.BlockSpec((BLK, HD), lambda i: (i, 0)),
        ],
        out_specs=[
            pl.BlockSpec((BLK, nq * HD), lambda i: (i, 0)),
            pl.BlockSpec((BLK, 2 * nk * HD), lambda i: (i, 0)),
        ],
        out_shape=[
            jax.ShapeDtypeStruct((rows, nq * HD), BF16),
            jax.ShapeDtypeStruct((rows, 2 * nk * HD), BF16),
        ],
        compiler_params=pltpu.CompilerParams(vmem_limit_bytes=VMEM_LIMIT),
        cost_estimate=pl.CostEstimate(
            flops=2 * rows * width * depth,
            bytes_accessed=rows * width * 6 + rows * depth * 2 + depth * width * 2,
            transcendentals=0,
        ),
    )(part, x, w, cosine, sine)


def attend_parts(meta_ref, block, unit, trunk, step):
    base = meta_ref[block * 8]
    rows = (lax.broadcasted_iota(jnp.int32, (2 * BLK, 1), 0) & (BLK - 1)) + base
    chunk = min(trunk, 1024)
    for j in range(trunk // chunk):
        step(j * chunk, chunk, rows)
    own_start = pl.multiple_of(meta_ref[block * 8 + 1], BLK)
    step(own_start, unit, jnp.where(meta_ref[block * 8 + 2] > 0, rows, -1))
    parent_start = pl.multiple_of(meta_ref[block * 8 + 3], BLK)
    step(parent_start, unit, jnp.where(meta_ref[block * 8 + 4] > 0, BIG, -1) + rows * 0)


def stacked(ref):
    a = ref[...]
    return jnp.concatenate([a[:, :HD], a[:, HD:]], axis=0)


def unstacked(a):
    return jnp.concatenate([a[:BLK], a[BLK:]], axis=1)


def weights_of(q2, keys, start, limit):
    scores = kdot(q2, keys, 1, 1) * SCALE
    place = lax.broadcasted_iota(jnp.int32, scores.shape, 1) + start
    return jnp.where(place <= limit, jnp.exp(scores), 0.0)


def fwd_kernel(unit, trunk, meta_ref, q_ref, k_ref, v_ref, att_ref, ctx_ref, tot_ref, acc, tot):
    q2 = stacked(q_ref)
    acc[...] = jnp.zeros_like(acc)
    tot[...] = jnp.zeros_like(tot)

    def step(start, size, limit):
        e = weights_of(q2, k_ref[pl.ds(start, size), :], start, limit)
        tot[...] += jnp.sum(e, axis=1, keepdims=True)
        acc[...] += kdot(e.astype(BF16), v_ref[pl.ds(start, size), :], 1, 0)

    attend_parts(meta_ref, pl.program_id(1), unit, trunk, step)
    total = jnp.broadcast_to(tot[...], acc.shape)
    context = unstacked(acc[...] / total)
    ctx_ref[...] = context
    att_ref[...] = context.astype(BF16)
    tot_ref[...] = unstacked(total)


def fwd_call(meta, q, kv, nk, unit, trunk):
    rows = q.shape[0]
    length = kv.shape[0]
    pair = 2 * HD
    tile = pl.BlockSpec((BLK, pair), lambda g, b, m: (b, g))
    return pl.pallas_call(
        partial(fwd_kernel, unit, trunk),
        grid_spec=pltpu.PrefetchScalarGridSpec(
            num_scalar_prefetch=1,
            grid=(nk, rows // BLK),
            in_specs=[
                tile,
                pl.BlockSpec((length, HD), lambda g, b, m: (0, g)),
                pl.BlockSpec((length, HD), lambda g, b, m: (0, nk + g)),
            ],
            out_specs=[tile, tile, tile],
            scratch_shapes=[pltpu.VMEM((2 * BLK, HD), F32), pltpu.VMEM((2 * BLK, 1), F32)],
        ),
        out_shape=[
            jax.ShapeDtypeStruct(q.shape, BF16),
            jax.ShapeDtypeStruct(q.shape, F32),
            jax.ShapeDtypeStruct(q.shape, F32),
        ],
        compiler_params=pltpu.CompilerParams(vmem_limit_bytes=VMEM_LIMIT),
        cost_estimate=pl.CostEstimate(
            flops=8 * rows * nk * HD * (trunk + 2 * unit),
            bytes_accessed=kv.size * 2 + q.size * 12,
            transcendentals=2 * rows * nk * (trunk + 2 * unit),
        ),
    )(meta, q, kv, kv)


def bwd_kernel(
    unit, trunk, meta_ref, q_ref, k_ref, v_ref, gc_ref, ctx_ref, tot_ref, cos_ref, sin_ref,
    dq_ref, dk_ref, dv_ref, acc,
):
    block = pl.program_id(1)

    @pl.when(block == 0)
    def _():
        dk_ref[...] = jnp.zeros_like(dk_ref)
        dv_ref[...] = jnp.zeros_like(dv_ref)

    q2 = stacked(q_ref)
    grad_context = stacked(gc_ref)
    context = stacked(ctx_ref)
    total = stacked(tot_ref)
    grad_accum = (grad_context / total).astype(BF16)
    delta = jnp.sum(grad_context * context, axis=1, keepdims=True) / total[:, :1]
    acc[...] = jnp.zeros_like(acc)

    def step(start, size, limit):
        here = pl.ds(start, size)
        keys = k_ref[here, :]
        e = weights_of(q2, keys, start, limit)
        grad_prob = kdot(grad_accum, v_ref[here, :], 1, 1)
        grad_scores = (e * (grad_prob - delta)).astype(BF16)
        acc[...] += kdot(grad_scores, keys, 1, 0)
        dk_ref[here, :] += kdot(grad_scores, q2, 0, 0)
        dv_ref[here, :] += kdot(e.astype(BF16), grad_accum, 0, 0)

    attend_parts(meta_ref, block, unit, trunk, step)
    cosine, sine = cos_ref[...], sin_ref[...]
    g = acc[...] * SCALE
    for h in range(2):
        u = g[h * BLK : (h + 1) * BLK]
        dq_ref[:, h * HD : (h + 1) * HD] = (
            u * cosine - pltpu.roll(u, HD // 2, 1) * sine
        ).astype(BF16)


def bwd_call(meta, q, kv, grad_context, context, total, cosine, sine, nk, unit, trunk):
    rows = q.shape[0]
    length = kv.shape[0]
    tile = pl.BlockSpec((BLK, 2 * HD), lambda g, b, m: (b, g))
    angle = pl.BlockSpec((BLK, HD), lambda g, b, m: (b, 0))
    head = pl.BlockSpec((length, HD), lambda g, b, m: (0, g))
    return pl.pallas_call(
        partial(bwd_kernel, unit, trunk),
        grid_spec=pltpu.PrefetchScalarGridSpec(
            num_scalar_prefetch=1,
            grid=(nk, rows // BLK),
            in_specs=[
                tile,
                head,
                pl.BlockSpec((length, HD), lambda g, b, m: (0, nk + g)),
                tile,
                tile,
                tile,
                angle,
                angle,
            ],
            out_specs=[tile, head, head],
            scratch_shapes=[pltpu.VMEM((2 * BLK, HD), F32)],
        ),
        out_shape=[
            jax.ShapeDtypeStruct(q.shape, BF16),
            jax.ShapeDtypeStruct((length, nk * HD), F32),
            jax.ShapeDtypeStruct((length, nk * HD), F32),
        ],
        compiler_params=pltpu.CompilerParams(vmem_limit_bytes=VMEM_LIMIT),
        cost_estimate=pl.CostEstimate(
            flops=20 * rows * nk * HD * (trunk + 2 * unit),
            bytes_accessed=kv.size * 6 + q.size * 16,
            transcendentals=2 * rows * nk * (trunk + 2 * unit),
        ),
    )(meta, q, kv, kv, grad_context, context, total, cosine, sine)


def dkv_kernel(nk, sum_ref, cos_ref, sin_ref, out_ref):
    cosine, sine = cos_ref[...], sin_ref[...]
    for h in range(nk):
        u = sum_ref[:, h * HD : (h + 1) * HD] * SCALE
        out_ref[:, h * HD : (h + 1) * HD] = (
            u * cosine - pltpu.roll(u, HD // 2, 1) * sine
        ).astype(BF16)
    out_ref[:, nk * HD :] = sum_ref[:, nk * HD :].astype(BF16)


def dkv_call(sums, cosine, sine, nk):
    rows, width = sums.shape
    return pl.pallas_call(
        partial(dkv_kernel, nk),
        out_shape=jax.ShapeDtypeStruct((rows, width), BF16),
        compiler_params=pltpu.CompilerParams(vmem_limit_bytes=VMEM_LIMIT),
    )(sums, cosine, sine)


def gather_ctx(a, count, c):
    if count != 4:
        return lax.all_gather(a, "ctx", axis=0, tiled=True)
    rows = a.shape[0]
    ring = [(0, 1), (1, 3), (3, 2), (2, 0)]
    origins = [c, table((2, 0, 3, 1), c), 3 - c, table((1, 3, 0, 2), c)]
    out = jnp.zeros((rows * count, a.shape[1]), a.dtype)
    for step in range(4):
        out = lax.dynamic_update_slice_in_dim(out, a, origins[step] * rows, axis=0)
        if step < 3:
            a = lax.ppermute(a, "ctx", ring)
    return out


def scatter_ctx(a, count, c):
    rows = a.shape[0] // count
    if count != 4:
        return lax.psum_scatter(a, "ctx", scatter_dimension=0, tiled=True)
    ring = [(0, 1), (1, 3), (3, 2), (2, 0)]
    owners = [table((2, 0, 3, 1), c), 3 - c, table((1, 3, 0, 2), c), c]
    carried = None
    for step in range(4):
        mine = lax.dynamic_slice_in_dim(a, owners[step] * rows, rows, axis=0)
        if carried is not None:
            mine = mine + carried.astype(F32)
        if step == 3:
            return mine
        carried = lax.ppermute(mine.astype(BF16), "ctx", ring)


class LineSum:
    def __init__(self, count, c):
        self.count = count
        self.middle = (c == 1) | (c == 2)
        self.last = [[], [], []]

    def move(self, stage, a, pairs):
        past = self.last[stage]
        if len(past) >= 2:
            a = after(a, past[-2])
        a = lax.ppermute(a, "ctx", pairs)
        past.append(a)
        return a

    def __call__(self, a):
        if self.count != 4:
            return lax.psum(a.astype(F32), "ctx")
        got = self.move(0, a, [(0, 1), (3, 2)])
        pair = (a.astype(F32) + got.astype(F32)).astype(BF16)
        got = self.move(1, pair, [(1, 2), (2, 1)])
        whole = (pair.astype(F32) + got.astype(F32)).astype(BF16)
        got = self.move(2, whole, [(1, 0), (2, 3)])
        return jnp.where(self.middle, whole, got).astype(F32)


def sum_all(a, count):
    a = a + swap_core(a)
    a = a + swap_y(a)
    a = a + swap_x(a)
    return sum_ctx(a, count)


def sum_ctx(a, count):
    step = 1
    while step < count:
        a = a + lax.ppermute(a, "ctx", [(i, i ^ step) for i in range(count)])
        step *= 2
    return a


def per_device(
    hidden_in, teacher, w_query, w_key, w_value, w_out, w_gate, w_up, w_down,
    attn_gain, ffn_gain, segment_ids, parents, positions, valid_mask,
):
    rows, width = hidden_in.shape
    half = width // 2
    quarter = rows // 4
    count = lax.axis_size("ctx")
    f, c, t = (lax.axis_index(a) for a in ("fsdp", "ctx", "tp"))
    tree_len = rows * count
    unit = tree_len // 20
    trunk = 8 * unit
    nq, nk = w_query.shape[1] // HD, w_key.shape[1] // HD
    eighth = w_gate.shape[1] // 2
    first = f == 0

    def turned(a):
        return jnp.where(first, a, halves_swapped(a))

    def reordered(a):
        cols = a.shape[1]
        a = a.reshape(2, 2, quarter, cols)
        a = jnp.where(t < 2, a, jnp.concatenate([a[1:], a[:1]], axis=0))
        a = jnp.where(t % 2 == 0, a, jnp.concatenate([a[:, 1:], a[:, :1]], axis=1))
        return a.reshape(rows, cols)

    def own_rows(a):
        return lax.dynamic_slice_in_dim(a, t * quarter, quarter, axis=0)

    def gather_tp(x):
        over_core, over_y = swap_core(x), swap_y(x)
        return [x, over_core, over_y, swap_core(over_y)]

    def gather_plane(x):
        flipped = halves_swapped(x)
        over_x, over_y, over_xy = swap_x(flipped), swap_y(x), swap_xy(flipped)
        group = jnp.concatenate([x, over_y, over_x, over_xy], axis=0)
        return jnp.concatenate([group, swap_core(group)], axis=0)

    def scatter_tp(product, a):
        cols = a.shape[1]
        blocks = a.reshape(2, 2, quarter, cols)
        sent = swap_core(product(blocks[:, 1].reshape(2 * quarter, cols)).astype(BF16))
        kept = product(blocks[:, 0].reshape(2 * quarter, cols)) + sent.astype(F32)
        over_y = swap_y(kept[quarter:].astype(BF16))
        return kept[:quarter] + over_y.astype(F32)

    def scatter_plane(product, *arrays):
        near = [a[: 4 * quarter] for a in arrays]
        far = [a[4 * quarter :] for a in arrays]
        sent = swap_core(product(*far).astype(BF16))
        kept = product(*near) + sent.astype(F32)
        to_y = kept[quarter : 2 * quarter].astype(BF16)
        to_x = halves_swapped(kept[2 * quarter : 3 * quarter].astype(BF16))
        to_xy = halves_swapped(kept[3 * quarter :].astype(BF16))
        over_xy, over_y, over_x = swap_xy(to_xy), swap_y(to_y), swap_x(to_x)
        return (
            kept[:quarter]
            + over_y.astype(F32)
            + over_x.astype(F32)
            + over_xy.astype(F32)
        )

    near_qkv = jnp.concatenate([w_query, w_key, w_value], axis=1)
    far_qkv = swap_x(near_qkv)
    far_gains = swap_x(jnp.stack([attn_gain, ffn_gain]))
    gain_attn = jnp.concatenate([attn_gain, far_gains[0]]).astype(F32)
    gain_ffn = jnp.concatenate([ffn_gain, far_gains[1]]).astype(F32)
    far_out = swap_x(after(w_out, far_qkv))
    out_full = jnp.concatenate([w_out, far_out], axis=1)

    def exchanged(w, axis, *behind):
        kept = lax.dynamic_slice_in_dim(w, f * eighth, eighth, axis=axis)
        sent = lax.dynamic_slice_in_dim(w, (1 - f) * eighth, eighth, axis=axis)
        got = swap_x(after(sent, *behind))
        return jnp.concatenate([kept, got], axis=1 - axis), got

    gate_w, got = exchanged(w_gate, 1, far_out)
    up_w, got = exchanged(w_up, 1, got)
    down_w, got = exchanged(w_down, 0, got)

    labels = jnp.arange(parents.shape[0], dtype=jnp.int32)
    seg = segment_ids[::BLK]
    parent = jnp.sum(jnp.where(seg[:, None] == labels[None, :], parents[None, :], 0), axis=1)
    grand = jnp.sum(jnp.where(parent[:, None] == labels[None, :], parents[None, :], 0), axis=1)
    all_seg = lax.all_gather(seg, "ctx", axis=0, tiled=True)
    spots = jnp.arange(all_seg.shape[0], dtype=jnp.int32)
    parent_spot = jnp.min(
        jnp.where(all_seg[None, :] == parent[:, None], spots[None, :], all_seg.shape[0] - 1),
        axis=1,
    )
    slot = c * rows + jnp.arange(seg.shape[0], dtype=jnp.int32) * BLK
    branch_or_leaf = parent >= 0
    leaf = branch_or_leaf & (grand >= 0)
    own_ok = branch_or_leaf & (valid_mask[::BLK] == 1)
    nothing = jnp.zeros_like(slot)
    meta = jnp.stack(
        [
            slot,
            jnp.where(branch_or_leaf, slot // unit * unit, 0),
            own_ok.astype(jnp.int32),
            jnp.where(leaf, parent_spot * BLK, 0),
            leaf.astype(jnp.int32),
            nothing,
            nothing,
            nothing,
        ],
        axis=1,
    ).reshape(-1)

    valid_f = valid_mask.astype(F32)
    valid_count = jnp.sum(valid_f).reshape(1, 1)
    valid_count = sum_ctx(valid_count + swap_x(valid_count), count)[0, 0]
    cosine, sine = rope_tables(positions)

    hidden = turned(hidden_in)
    normed = rms_scale(hidden.astype(F32), gain_attn).astype(BF16)
    near_normed, far_normed = normed[:, :half], normed[:, half:]
    query, kv = qkv_call(dot(near_normed, near_qkv), far_normed, far_qkv, cosine, sine, nq, nk)
    kv_all = gather_ctx(kv, count, c)
    attended, context, total = fwd_call(meta, query, kv_all, nk, unit, trunk)
    attended = reordered(attended)
    attn_out = scatter_tp(lambda a: dot(a, out_full), attended)

    hidden_own = own_rows(hidden).astype(F32)
    middle = hidden_own + attn_out
    normed_ffn = gather_plane(rms_scale(middle, gain_ffn).astype(BF16))
    gate_proj = dot(normed_ffn, gate_w)
    up_proj = dot(normed_ffn, up_w)
    activated_f, swiglu_back = jax.vjp(swiglu, gate_proj, up_proj)
    activated = activated_f.astype(BF16)
    output_f = middle + scatter_plane(lambda a: dot(a, down_w), activated)

    deviation = output_f - turned(own_rows(teacher)).astype(F32)
    valid_own = lax.dynamic_slice_in_dim(valid_f, t * quarter, quarter, axis=0)
    error_sum = jnp.sum(valid_own * jnp.mean(deviation * deviation, axis=1))
    tokens_all = rows * lax.axis_size("fsdp") * count
    loss_factor = float(width * tokens_all // 2)
    grad_output = loss_factor * 2.0 / width * valid_own[:, None] * deviation / valid_count

    line_sum = LineSum(count, c)
    grad_ffn = gather_plane(grad_output.astype(BF16))
    grad_act = dot_nt(grad_ffn, down_w)
    grad_gate_f, grad_up_f = swiglu_back(grad_act)
    grad_gate, grad_up = grad_gate_f.astype(BF16), grad_up_f.astype(BF16)

    down_sent = swap_x(dot_tn(activated, grad_ffn[:, half:], BF16))
    down_near = line_sum(dot_tn(activated, grad_ffn[:, :half], BF16))
    gate_sent = swap_x(after(dot_tn(normed_ffn[:, half:], grad_gate, BF16), down_sent))
    down_far = line_sum(down_sent)
    up_sent = swap_x(after(dot_tn(normed_ffn[:, half:], grad_up, BF16), gate_sent))
    gate_near = line_sum(dot_tn(normed_ffn[:, :half], grad_gate, BF16))
    gate_far = line_sum(gate_sent)
    up_near = line_sum(dot_tn(normed_ffn[:, :half], grad_up, BF16))
    up_far = line_sum(up_sent)

    grad_normed_ffn = scatter_plane(
        lambda a, b: dot_nt(a, gate_w) + dot_nt(b, up_w), grad_gate, grad_up
    )
    _, norm_ffn_back = jax.vjp(rms_scale, middle, gain_ffn)
    grad_middle_part, grad_ffn_gain = norm_ffn_back(grad_normed_ffn)
    grad_middle = grad_output + grad_middle_part

    grad_attn = jnp.concatenate(gather_tp(grad_middle.astype(BF16)), axis=0)
    out_sent = swap_x(dot_tn(attended, grad_attn[:, half:], BF16))
    grad_out = line_sum(
        (dot_tn(attended, grad_attn[:, :half]) + out_sent.astype(F32)).astype(BF16)
    )
    grad_context = reordered(dot_nt(grad_attn, out_full))
    grad_query, key_terms, value_terms = bwd_call(
        meta, query, kv_all, grad_context, context, total, cosine, sine, nk, unit, trunk
    )
    kv_sums = scatter_ctx(jnp.concatenate([key_terms, value_terms], axis=1), count, c)
    grad_kv = dkv_call(kv_sums, cosine, sine, nk)
    grad_qkv = jnp.concatenate([grad_query, grad_kv], axis=1)
    qkv_sent = swap_x(dot_tn(far_normed, grad_qkv, BF16))
    grad_qkv_w = line_sum(
        (dot_tn(near_normed, grad_qkv) + qkv_sent.astype(F32)).astype(BF16)
    )
    grad_normed = scatter_tp(
        lambda a: jnp.concatenate([dot_nt(a, near_qkv), dot_nt(a, far_qkv)], axis=1),
        reordered(grad_qkv),
    )
    _, norm_attn_back = jax.vjp(rms_scale, hidden_own, gain_attn)
    grad_hidden_part, grad_attn_gain = norm_attn_back(grad_normed)
    grad_hidden = grad_middle + grad_hidden_part

    def whole_rows(x, kind):
        out = jnp.zeros((rows, width), kind)
        for j, block in enumerate(gather_tp(x)):
            out = lax.dynamic_update_slice_in_dim(
                out, block.astype(kind), (t ^ j) * quarter, axis=0
            )
        return out

    def joined(near, far, axis):
        shape = list(near.shape)
        shape[axis] *= 2
        out = jnp.zeros(shape, F32)
        out = lax.dynamic_update_slice_in_dim(out, near, f * eighth, axis=axis)
        return lax.dynamic_update_slice_in_dim(out, far, (1 - f) * eighth, axis=axis)

    small = jnp.concatenate([turned(grad_attn_gain), turned(grad_ffn_gain)])
    small = jnp.concatenate([small, jnp.full((HD,), error_sum, F32)]).reshape(1, -1)
    small = sum_all(small, count)[0]
    loss_value = small[2 * width] / valid_count
    own_attn_gain = lax.dynamic_slice_in_dim(small[:width], f * half, half)
    own_ffn_gain = lax.dynamic_slice_in_dim(small[width : 2 * width], f * half, half)
    nqw, nkw = nq * HD, nk * HD
    return (
        whole_rows(turned(output_f).astype(BF16), BF16),
        loss_value,
        whole_rows(turned(grad_hidden).astype(BF16), F32),
        grad_qkv_w[:, :nqw],
        grad_qkv_w[:, nqw : nqw + nkw],
        grad_qkv_w[:, nqw + nkw :],
        grad_out,
        joined(gate_near, gate_far, 1),
        joined(up_near, up_far, 1),
        joined(down_near, down_far, 0),
        own_attn_gain,
        own_ffn_gain,
    )


def solution(mesh):
    tokens = P(("fsdp", "ctx"))
    token_rows = P(("fsdp", "ctx"), None)
    column = P("fsdp", "tp")
    row = P("tp", "fsdp")
    gain = P("fsdp")
    weights = (column, column, column, row, column, column, row, gain, gain)
    return jax.shard_map(
        per_device,
        mesh=mesh,
        in_specs=(token_rows, token_rows, *weights, tokens, P(), tokens, tokens),
        out_specs=(token_rows, P(), token_rows, *weights),
        check_vma=False,
    )
```

time: 3240 us -> 1180 us (0.36)
  waiting for transfers between devices: 2680 us -> 710 us
  matrix products: 275 us -> 126 us
  starting transfers between devices: 2.21 us -> 105 us
  blocking collectives: 105 us -> 16 us
  Pallas kernels: 0 us -> 41 us
  other arithmetic: 63.1 us -> 104 us
    reduce_scatter x16 -> x0, waiting for transfers between devices: 1370 us -> none  [the longest x1 191 us: per_device(): lax.psum_scatter(grad_w_down, 'fsdp', scatter_dimension=1, tiled=True)]
    all_gather x16 -> x0, waiting for transfers between devices: 948 us -> none  [the longest x1 150 us: per_device(): lax.all_gather(slices[6], 'ctx', axis=1, tiled=True)]
    ppermute x0 -> x78, waiting for transfers between devices: none -> 710 us  [the longest x17 214 us: swap_x(): return lax.ppermute(a, 'fsdp', [(0, 1), (1, 0)])]
    psum x4 -> x0, waiting for transfers between devices: 358 us -> none  [the longest x1 102 us: per_device(): lax.psum(cols_product(grad_gate, gate_full) + cols_product(grad_up, up_fu...]
    dot_general x56 -> x27, matrix products: 275 us -> 126 us  [the longest x10 51.9 us: dot_nt(): lax.dot_general(a, b, (((1,), (1,)), ((), ())), preferred_element_type=F32)]
    ppermute x0 -> x78, starting transfers between devices: none -> 105 us  [the longest x24 50.9 us: move(): a = lax.ppermute(a, 'ctx', pairs)]
    convert_element_type x8 -> x27, other arithmetic: 1.43 us -> 45.2 us  [the longest x8 20.8 us: __call__(): pair = (a.astype(F32) + got.astype(F32)).astype(BF16)]
    psum x2 -> x0, blocking collectives: 43.4 us -> none  [per_device(): lax.psum((jnp.sum(valid_f), jnp.sum(valid_f * jnp.mean(deviation * deviat...]
  transfers between devices with their start and end apart: 36 -> 78, of which waited for: 33 -> 38; matrix products, arithmetic and copies ran while one was open for 6% -> 18% of each run, Pallas kernels for 0% -> 2%
where the time goes in v1:
time: 1180 us; the launch traced here: 1170 us
  waiting for transfers between devices  710 us (60%)
  matrix products  126 us (11%)
  starting transfers between devices  105 us (9%)
  other arithmetic  104 us (9%)
  local copies, waits for them, and re-layouts  61 us (5%)
  Pallas kernels  41 us (3%)
  blocking collectives  16 us (1%)
    ppermute x17, waiting for transfers between devices, swap_x(): return lax.ppermute(a, 'fsdp', [(0, 1), (1, 0)])  214 us
    ppermute x24, waiting for transfers between devices, move(): a = lax.ppermute(a, 'ctx', pairs)  189 us
    ppermute x3, waiting for transfers between devices, scatter_ctx(): carried = lax.ppermute(mine.astype(BF16), 'ctx', ring)  116 us
    ppermute x4, waiting for transfers between devices, sum_ctx(): a = a + lax.ppermute(a, 'ctx', [(i, i ^ step) for i in range(count)])  65.7 us
    ppermute x10, waiting for transfers between devices, swap_y(): return lax.ppermute(a, 'tp', [(0, 2), (2, 0), (1, 3), (3, 1)])  63.9 us
    dot_general x10, matrix products, dot_nt(): lax.dot_general(a, b, (((1,), (1,)), ((), ())), preferred_element_type=F32)  51.9 us
    ppermute x24, starting transfers between devices, move(): a = lax.ppermute(a, 'ctx', pairs)  50.9 us
    dot_general x10, matrix products, dot_tn(): lax.dot_general(a, b, (((0,), (0,)), ((), ())), preferred_element_type=F32)  38.8 us
  transfers between devices with their start and end apart: 78, of which 38 were waited for; matrix products, arithmetic and copies ran while one was open for 18% of the time, Pallas kernels for 2%

profile of v1, /device:TPU:0, one launch (start us, length us, event | category | flops | bytes accessed | tf_op | source)
XLA Modules:
  0.0 1170.8 jit_solution(10074630623417643890)
XLA Ops:
  24.2 33.5 %collective-permute-done.1.w_ref = bf16[1024,1024]{1,0:T(8,128)(2,1)} collective-permute-done((bf16[1024,1024]{1,0:T(8,128)(2,1)}, bf16[1024,1024]{1,0:T(8,128)(2,1)}, u32[]{:S(2)}, u32[]{:S(2)}) %collective-permute-start.1) | collective-permute-done | bytes 2097184 | tf_op jit(solution)/shard_map/ppermute | solution.py:23
  68.3 16.0 %all-reduce = s32[20]{0:T(128)S(1)} all-reduce(s32[20]{0:T(128)S(1)} %dynamic-update-slice), channel_id=1, replica_groups=mesh['fsdp'=2,'ctx'=4,'tp'=4] {'ctx'}, use_global_device_ids=true, to_apply=%add | all-reduce | flops 20 | bytes 160
  86.7 13.1 %collective-permute-done.3 = bf16[640,512]{1,0:T(8,128)(2,1)} collective-permute-done((bf16[640,512]{1,0:T(8,128)(2,1)S(1)}, bf16[640,512]{1,0:T(8,128)(2,1)}, u32[]{:S(2)}, u32[]{:S(2)}) %collective-permute-start.3) | collective-permute-done | bytes 655392 | tf_op jit(solution)/shard_map/ppermute | solution.py:324
  115.2 12.4 %shard_map.239 = (bf16[640,512]{1,0:T(8,128)(2,1)}, f32[640,512]{1,0:T(8,128)}, f32[640,512]{1,0:T(8,128)}) custom-call(s32[40]{0:T(128)} %reshape.260.meta_ref, bf16[640,512]{1,0:T(8,128)(2,1)} %get-tuple-element.44.q_ref, bf16[2560,512]{1,0:T(8,128)(2,1)} %copy-done.30, bf16[2560,512]{1,0:T(8,128)(2,1)} %copy-done.30), custom_call_target="tpu_custom_call" | custom-call | flops 1677721600 | bytes 6553600 | tf_op jit(solution)/shard_map/pallas_call | solution.py:191
  143.2 12.0 %collective-permute-done.7 = bf16[160,2048]{1,0:T(8,128)(2,1)S(1)} collective-permute-done((bf16[160,2048]{1,0:T(8,128)(2,1)S(1)}, bf16[160,2048]{1,0:T(8,128)(2,1)S(1)}, u32[]{:S(2)}, u32[]{:S(2)}) %collective-permute-start.7) | collective-permute-done | bytes 655392 | tf_op jit(solution)/shard_map/ppermute | solution.py:31
  160.7 12.3 %collective-permute-done.8 = bf16[160,2048]{1,0:T(8,128)(2,1)S(1)} collective-permute-done((bf16[160,2048]{1,0:T(8,128)(2,1)S(1)}, bf16[160,2048]{1,0:T(8,128)(2,1)S(1)}, u32[]{:S(2)}, u32[]{:S(2)}) %collective-permute-start.8) | collective-permute-done | bytes 655392 | tf_op jit(solution)/shard_map/ppermute | solution.py:31
  173.0 31.3 %collective-permute-done.9 = bf16[160,2048]{1,0:T(8,128)(2,1)S(1)} collective-permute-done((bf16[160,2048]{1,0:T(8,128)(2,1)S(1)}, bf16[160,2048]{1,0:T(8,128)(2,1)S(1)}, u32[]{:S(2)}, u32[]{:S(2)}) %collective-permute-start.9) | collective-permute-done | bytes 655392 | tf_op jit(solution)/shard_map/ppermute | solution.py:23
  204.3 14.0 %collective-permute-done.10 = bf16[160,2048]{1,0:T(8,128)(2,1)S(1)} collective-permute-done((bf16[160,2048]{1,0:T(8,128)(2,1)S(1)}, bf16[160,2048]{1,0:T(8,128)(2,1)S(1)}, u32[]{:S(2)}, u32[]{:S(2)}) %collective-permute-start.10) | collective-permute-done | bytes 655392 | tf_op jit(solution)/shard_map/ppermute | solution.py:36
  223.0 45.7 %collective-permute-done.13 = bf16[1024,1024]{1,0:T(8,128)(2,1)S(1)} collective-permute-done((bf16[1024,1024]{1,0:T(8,128)(2,1)S(1)}, bf16[1024,1024]{1,0:T(8,128)(2,1)S(1)}, u32[]{:S(2)}, u32[]{:S(2)}) %collective-permute-start.13) | collective-permute-done | bytes 2097184 | tf_op jit(solution)/shard_map/ppermute | solution.py:23
  278.4 10.3 multiply_convert_fusion.1
  288.8 27.3 %collective-permute-done.14 = bf16[1024,1024]{1,0:T(8,128)(2,1)} collective-permute-done((bf16[1024,1024]{1,0:T(8,128)(2,1)S(1)}, bf16[1024,1024]{1,0:T(8,128)(2,1)}, u32[]{:S(2)}, u32[]{:S(2)}) %collective-permute-start.14) | collective-permute-done | bytes 2097184 | tf_op jit(solution)/shard_map/ppermute | solution.py:23
  339.5 23.9 %collective-permute-done.22 = f32[1,1]{1,0:T(1,128)} collective-permute-done((f32[1,1]{1,0:T(1,128)}, f32[1,1]{1,0:T(1,128)}, u32[]{:S(2)}, u32[]{:S(2)}) %collective-permute-start.22) | collective-permute-done | bytes 36 | tf_op jit(solution)/shard_map/ppermute | solution.py:23
  381.8 12.9 %collective-permute-done.25 = bf16[160,2048]{1,0:T(8,128)(2,1)S(1)} collective-permute-done((bf16[160,2048]{1,0:T(8,128)(2,1)S(1)}, bf16[160,2048]{1,0:T(8,128)(2,1)S(1)}, u32[]{:S(2)}, u32[]{:S(2)}) %collective-permute-start.25) | collective-permute-done | bytes 655392 | tf_op jit(solution)/shard_map/ppermute | solution.py:31
  397.6 9.9 collective-permute-done.27
  417.3 12.5 %collective-permute-done.20 = bf16[160,2048]{1,0:T(8,128)(2,1)} collective-permute-done((bf16[160,2048]{1,0:T(8,128)(2,1)}, bf16[160,2048]{1,0:T(8,128)(2,1)}, u32[]{:S(2)}, u32[]{:S(2)}) %collective-permute-start.20) | collective-permute-done | bytes 655392 | tf_op jit(solution)/shard_map/ppermute | solution.py:31
  446.1 12.2 %fusion.5 = (bf16[1280,1024]{1,0:T(8,128)(2,1)S(1)}, bf16[1280,1024]{1,0:T(8,128)(2,1)}) fusion(f32[1280,1024]{1,0:T(8,128)} %fusion.63, f32[1280,1024]{1,0:T(8,128)} %get-tuple-element.167, bf16[1280,2048]{1,0:T(8,128)(2,1)S(1)} %copy-done.61, bf16[1024,1024]{1,0:T(8,128)(2,1)} %collective-permute-done.14, bf16[1024,1024]{1,0:T(8,128)(2,1)S(1)} %copy-done.37), kind=kOutput, calls=%fused_computation.8 | convolution fusion | flops 5395447808 | bytes 25165824 | tf_op jit(solution)/shard_map/dot_general | solution.py:66
  458.3 8.7 fusion.47
  533.7 10.6 collective-permute-done.32
  547.0 10.2 collective-permute-done.31
  566.1 9.0 collective-permute-done.34
  578.2 23.1 %collective-permute-done.51 = bf16[1024,1024]{1,0:T(8,128)(2,1)} collective-permute-done((bf16[1024,1024]{1,0:T(8,128)(2,1)S(1)}, bf16[1024,1024]{1,0:T(8,128)(2,1)}, u32[]{:S(2)}, u32[]{:S(2)}) %collective-permute-start.51) | collective-permute-done | bytes 2097184 | tf_op jit(solution)/shard_map/ppermute | solution.py:23
  602.1 20.3 %collective-permute-done.53 = bf16[1024,1024]{1,0:T(8,128)(2,1)S(1)} collective-permute-done((bf16[1024,1024]{1,0:T(8,128)(2,1)}, bf16[1024,1024]{1,0:T(8,128)(2,1)S(1)}, u32[]{:S(2)}, u32[]{:S(2)}) %collective-permute-start.53) | collective-permute-done | bytes 2097184 | tf_op jit(solution)/shard_map/ppermute | solution.py:354
  632.7 19.3 %shard_map.240 = (bf16[640,512]{1,0:T(8,128)(2,1)}, f32[2560,256]{1,0:T(8,128)}, f32[2560,256]{1,0:T(8,128)}) custom-call(s32[40]{0:T(128)} %reshape.260.meta_ref, bf16[640,512]{1,0:T(8,128)(2,1)} %get-tuple-element.44.q_ref, bf16[2560,512]{1,0:T(8,128)(2,1)} %copy-done.30, bf16[2560,512]{1,0:T(8,128)(2,1)} %copy-done.30, ...), custom_call_target="tpu_custom_call" | custom-call | flops 4194304000 | bytes 13107200 | tf_op jit(solution)/shard_map/pallas_call | solution.py:263
  661.5 22.8 %collective-permute-done.36 = bf16[640,512]{1,0:T(8,128)(2,1)S(1)} collective-permute-done((bf16[640,512]{1,0:T(8,128)(2,1)S(1)}, bf16[640,512]{1,0:T(8,128)(2,1)S(1)}, u32[]{:S(2)}, u32[]{:S(2)}) %collective-permute-start.36) | collective-permute-done | bytes 655392 | tf_op jit(solution)/shard_map/ppermute | solution.py:341
  696.2 48.4 %collective-permute-done.37 = bf16[640,512]{1,0:T(8,128)(2,1)S(1)} collective-permute-done((bf16[640,512]{1,0:T(8,128)(2,1)S(1)}, bf16[640,512]{1,0:T(8,128)(2,1)S(1)}, u32[]{:S(2)}, u32[]{:S(2)}) %collective-permute-start.37) | collective-permute-done | bytes 655392 | tf_op jit(solution)/shard_map/ppermute | solution.py:341
  766.2 44.9 %collective-permute-done.38 = bf16[640,512]{1,0:T(8,128)(2,1)S(1)} collective-permute-done((bf16[640,512]{1,0:T(8,128)(2,1)S(1)}, bf16[640,512]{1,0:T(8,128)(2,1)S(1)}, u32[]{:S(2)}, u32[]{:S(2)}) %collective-permute-start.38) | collective-permute-done | bytes 655392 | tf_op jit(solution)/shard_map/ppermute | solution.py:341
  853.7 23.8 %collective-permute-done.61 = bf16[1024,1024]{1,0:T(8,128)(2,1)} collective-permute-done((bf16[1024,1024]{1,0:T(8,128)(2,1)S(1)}, bf16[1024,1024]{1,0:T(8,128)(2,1)}, u32[]{:S(2)}, u32[]{:S(2)}) %collective-permute-start.61) | collective-permute-done | bytes 2097184 | tf_op jit(solution)/shard_map/ppermute | solution.py:354
  883.5 38.8 %collective-permute-done.75 = bf16[1024,1024]{1,0:T(8,128)(2,1)S(1)} collective-permute-done((bf16[1024,1024]{1,0:T(8,128)(2,1)S(1)}, bf16[1024,1024]{1,0:T(8,128)(2,1)S(1)}, u32[]{:S(2)}, u32[]{:S(2)}) %collective-permute-start.75) | collective-permute-done | bytes 2097184 | tf_op jit(solution)/shard_map/ppermute | solution.py:354
  951.9 60.4 %collective-permute-done.44 = f32[1,4224]{1,0:T(1,128)S(1)} collective-permute-done((f32[1,4224]{1,0:T(1,128)S(1)}, f32[1,4224]{1,0:T(1,128)S(1)}, u32[]{:S(2)}, u32[]{:S(2)}) %collective-permute-start.44) | collective-permute-done | bytes 16928 | tf_op jit(solution)/shard_map/ppermute | solution.py:379
  1045.9 29.5 %collective-permute-done.63 = bf16[1024,1024]{1,0:T(8,128)(2,1)} collective-permute-done((bf16[1024,1024]{1,0:T(8,128)(2,1)}, bf16[1024,1024]{1,0:T(8,128)(2,1)}, u32[]{:S(2)}, u32[]{:S(2)}) %collective-permute-start.63) | collective-permute-done | bytes 2097184 | tf_op jit(solution)/shard_map/ppermute | solution.py:354
  1085.1 37.3 %collective-permute-done.77 = bf16[512,1024]{1,0:T(8,128)(2,1)S(1)} collective-permute-done((bf16[512,1024]{1,0:T(8,128)(2,1)S(1)}, bf16[512,1024]{1,0:T(8,128)(2,1)S(1)}, u32[]{:S(2)}, u32[]{:S(2)}) %collective-permute-start.77) | collective-permute-done | bytes 1048608 | tf_op jit(solution)/shard_map/ppermute | solution.py:354
  1126.5 39.5 %collective-permute-done.64 = bf16[1024,1024]{1,0:T(8,128)(2,1)S(1)} collective-permute-done((bf16[1024,1024]{1,0:T(8,128)(2,1)S(1)}, bf16[1024,1024]{1,0:T(8,128)(2,1)S(1)}, u32[]{:S(2)}, u32[]{:S(2)}) %collective-permute-start.64) | collective-permute-done | bytes 2097184 | tf_op jit(solution)/shard_map/ppermute | solution.py:354
  (521 shorter events, 416.8 us)
Async XLA Ops:
  141.7 77.6 %collective-permute-start.12 = (bf16[1024,1024]{1,0:T(8,128)(2,1)S(1)}, bf16[1024,1024]{1,0:T(8,128)(2,1)S(1)}, u32[]{:S(2)}, u32[]{:S(2)}) collective-permute-start(bf16[1024,1024]{1,0:T(8,128)(2,1)S(1)} %get-tuple-element.48), channel_id=1, source_target_pairs={{0,16},{16,0},{1,17},{17,1},{2,18},{18,2},{3,19},{19,3},{4,20},{20... | collective-permute-start | bytes 6291464 | tf_op jit(solution)/shard_map/ppermute | solution.py:23
  159.1 59.1 %collective-permute-start.10 = (bf16[160,2048]{1,0:T(8,128)(2,1)S(1)}, bf16[160,2048]{1,0:T(8,128)(2,1)S(1)}, u32[]{:S(2)}, u32[]{:S(2)}) collective-permute-start(bf16[160,2048]{1,0:T(8,128)(2,1)S(1)} %pad_maximum_fusion.21), channel_id=1, source_target_pairs={{0,18},{1,19},{2,16},{3,17},{16,2},{17,3},{18,0},{19,1},{4,22},{5,... | collective-permute-start | bytes 1966088 | tf_op jit(solution)/shard_map/ppermute | solution.py:36
  218.7 51.5 %collective-permute-start.11 = (bf16[640,2048]{1,0:T(8,128)(2,1)S(1)}, bf16[640,2048]{1,0:T(8,128)(2,1)S(1)}, u32[]{:S(2)}, u32[]{:S(2)}) collective-permute-start(bf16[640,2048]{1,0:T(8,128)(2,1)S(1)} %pad_maximum_fusion.3), channel_id=1, source_target_pairs={{0,1},{1,0},{2,3},{3,2},{4,5},{5,4},{6,7},{7,6},{8,9},{9,8},{10,11... | collective-permute-start | bytes 7864328 | tf_op jit(solution)/shard_map/ppermute | solution.py:27
  481.9 48.8 %collective-permute-start.66 = (bf16[1024,1024]{1,0:T(8,128)(2,1)}, bf16[1024,1024]{1,0:T(8,128)(2,1)}, u32[]{:S(2)}, u32[]{:S(2)}) collective-permute-start(bf16[1024,1024]{1,0:T(8,128)(2,1)} %fusion.34), channel_id=1, source_target_pairs={{0,4},{12,8},{1,5},{13,9},{2,6},{14,10},{3,7},{15,11},{16,20},{28,... | collective-permute-start | bytes 6291464 | tf_op jit(solution)/shard_map/ppermute | solution.py:354
  529.2 72.1 %collective-permute-start.51 = (bf16[1024,1024]{1,0:T(8,128)(2,1)S(1)}, bf16[1024,1024]{1,0:T(8,128)(2,1)}, u32[]{:S(2)}, u32[]{:S(2)}) collective-permute-start(bf16[1024,1024]{1,0:T(8,128)(2,1)S(1)} %copy-done.79), channel_id=1, source_target_pairs={{0,16},{16,0},{1,17},{17,1},{2,18},{18,2},{3,19},{19,3},{4,20},{20... | collective-permute-start | bytes 6291464 | tf_op jit(solution)/shard_map/ppermute | solution.py:23
  530.8 92.3 %collective-permute-start.67 = (bf16[1024,1024]{1,0:T(8,128)(2,1)S(1)}, bf16[1024,1024]{1,0:T(8,128)(2,1)S(1)}, u32[]{:S(2)}, u32[]{:S(2)}) collective-permute-start(bf16[1024,1024]{1,0:T(8,128)(2,1)S(1)} %fusion.28), channel_id=1, source_target_pairs={{0,4},{12,8},{1,5},{13,9},{2,6},{14,10},{3,7},{15,11},{16,20},{28,... | collective-permute-start | bytes 6291464 | tf_op jit(solution)/shard_map/ppermute | solution.py:354
  544.3 78.1 %collective-permute-start.53 = (bf16[1024,1024]{1,0:T(8,128)(2,1)}, bf16[1024,1024]{1,0:T(8,128)(2,1)S(1)}, u32[]{:S(2)}, u32[]{:S(2)}) collective-permute-start(bf16[1024,1024]{1,0:T(8,128)(2,1)} %collective-permute-done.50), channel_id=1, source_target_pairs={{0,4},{12,8},{1,5},{13,9},{2,6},{14,10},{3,7},{15,11},{16,20},{28,... | collective-permute-start | bytes 6291464 | tf_op jit(solution)/shard_map/ppermute | solution.py:354
  566.1 62.6 %collective-permute-start.33 = (bf16[160,2048]{1,0:T(8,128)(2,1)S(1)}, bf16[160,2048]{1,0:T(8,128)(2,1)S(1)}, u32[]{:S(2)}, u32[]{:S(2)}) collective-permute-start(bf16[160,2048]{1,0:T(8,128)(2,1)S(1)} %get-tuple-element.84), channel_id=1, source_target_pairs={{0,1},{1,0},{2,3},{3,2},{4,5},{5,4},{6,7},{7,6},{8,9},{9,8},{10,11... | collective-permute-start | bytes 1966088 | tf_op jit(solution)/shard_map/ppermute | solution.py:27
  575.0 53.7 %collective-permute-start.35 = (bf16[160,2048]{1,0:T(8,128)(2,1)S(1)}, bf16[160,2048]{1,0:T(8,128)(2,1)S(1)}, u32[]{:S(2)}, u32[]{:S(2)}) collective-permute-start(bf16[160,2048]{1,0:T(8,128)(2,1)S(1)} %collective-permute-done.34), channel_id=1, source_target_pairs={{0,1},{1,0},{2,3},{3,2},{4,5},{5,4},{6,7},{7,6},{8,9},{9,8},{10,11... | collective-permute-start | bytes 1966088 | tf_op jit(solution)/shard_map/ppermute | solution.py:27
  601.3 59.3 %collective-permute-start.70 = (bf16[1024,1024]{1,0:T(8,128)(2,1)S(1)}, bf16[1024,1024]{1,0:T(8,128)(2,1)S(1)}, u32[]{:S(2)}, u32[]{:S(2)}) collective-permute-start(bf16[1024,1024]{1,0:T(8,128)(2,1)S(1)} %add_convert_fusion.4), channel_id=1, source_target_pairs={{4,8},{8,4},{5,9},{9,5},{6,10},{10,6},{7,11},{11,7},{20,24},{24,20... | collective-permute-start | bytes 6291464 | tf_op jit(solution)/shard_map/ppermute | solution.py:354
  622.4 124.4 %collective-permute-start.52 = (bf16[1024,1024]{1,0:T(8,128)(2,1)}, bf16[1024,1024]{1,0:T(8,128)(2,1)}, u32[]{:S(2)}, u32[]{:S(2)}) collective-permute-start(bf16[1024,1024]{1,0:T(8,128)(2,1)} %fusion.19), channel_id=1, source_target_pairs={{0,16},{16,0},{1,17},{17,1},{2,18},{18,2},{3,19},{19,3},{4,20},{20... | collective-permute-start | bytes 6291464 | tf_op jit(solution)/shard_map/ppermute | solution.py:23
  623.1 125.0 %collective-permute-start.54 = (bf16[1024,1024]{1,0:T(8,128)(2,1)}, bf16[1024,1024]{1,0:T(8,128)(2,1)}, u32[]{:S(2)}, u32[]{:S(2)}) collective-permute-start(bf16[1024,1024]{1,0:T(8,128)(2,1)} %collective-permute-done.51), channel_id=1, source_target_pairs={{0,4},{12,8},{1,5},{13,9},{2,6},{14,10},{3,7},{15,11},{16,20},{28,... | collective-permute-start | bytes 6291464 | tf_op jit(solution)/shard_map/ppermute | solution.py:354
  660.7 95.5 %collective-permute-start.57 = (bf16[1024,1024]{1,0:T(8,128)(2,1)S(1)}, bf16[1024,1024]{1,0:T(8,128)(2,1)S(1)}, u32[]{:S(2)}, u32[]{:S(2)}) collective-permute-start(bf16[1024,1024]{1,0:T(8,128)(2,1)S(1)} %add_convert_fusion.11), channel_id=1, source_target_pairs={{4,8},{8,4},{5,9},{9,5},{6,10},{10,6},{7,11},{11,7},{20,24},{24,20... | collective-permute-start | bytes 6291464 | tf_op jit(solution)/shard_map/ppermute | solution.py:354
  684.3 75.1 %collective-permute-start.68 = (bf16[1024,1024]{1,0:T(8,128)(2,1)}, bf16[1024,1024]{1,0:T(8,128)(2,1)S(1)}, u32[]{:S(2)}, u32[]{:S(2)}) collective-permute-start(bf16[1024,1024]{1,0:T(8,128)(2,1)} %fusion.25), channel_id=1, source_target_pairs={{0,4},{12,8},{1,5},{13,9},{2,6},{14,10},{3,7},{15,11},{16,20},{28,... | collective-permute-start | bytes 6291464 | tf_op jit(solution)/shard_map/ppermute | solution.py:354
  690.9 53.8 %collective-permute-start.37 = (bf16[640,512]{1,0:T(8,128)(2,1)S(1)}, bf16[640,512]{1,0:T(8,128)(2,1)S(1)}, u32[]{:S(2)}, u32[]{:S(2)}) collective-permute-start(bf16[640,512]{1,0:T(8,128)(2,1)S(1)} %add_convert_fusion.20), channel_id=1, source_target_pairs={{0,4},{4,12},{12,8},{8,0},{1,5},{5,13},{13,9},{9,1},{2,6},{6,14},{... | collective-permute-start | bytes 1966088 | tf_op jit(solution)/shard_map/ppermute | solution.py:341
  744.6 79.8 %collective-permute-start.71 = (bf16[1024,1024]{1,0:T(8,128)(2,1)S(1)}, bf16[1024,1024]{1,0:T(8,128)(2,1)}, u32[]{:S(2)}, u32[]{:S(2)}) collective-permute-start(bf16[1024,1024]{1,0:T(8,128)(2,1)S(1)} %add_convert_fusion.5), channel_id=1, source_target_pairs={{4,8},{8,4},{5,9},{9,5},{6,10},{10,6},{7,11},{11,7},{20,24},{24,20... | collective-permute-start | bytes 6291464 | tf_op jit(solution)/shard_map/ppermute | solution.py:354
  746.8 80.3 %collective-permute-start.74 = (bf16[1024,1024]{1,0:T(8,128)(2,1)}, bf16[1024,1024]{1,0:T(8,128)(2,1)}, u32[]{:S(2)}, u32[]{:S(2)}) collective-permute-start(bf16[1024,1024]{1,0:T(8,128)(2,1)} %add_convert_fusion.1), channel_id=1, source_target_pairs={{4,0},{8,12},{5,1},{9,13},{6,2},{10,14},{7,3},{11,15},{20,16},{24,... | collective-permute-start | bytes 6291464 | tf_op jit(solution)/shard_map/ppermute | solution.py:354
  748.1 63.0 %collective-permute-start.38 = (bf16[640,512]{1,0:T(8,128)(2,1)S(1)}, bf16[640,512]{1,0:T(8,128)(2,1)S(1)}, u32[]{:S(2)}, u32[]{:S(2)}) collective-permute-start(bf16[640,512]{1,0:T(8,128)(2,1)S(1)} %add_convert_fusion.19), channel_id=1, source_target_pairs={{0,4},{4,12},{12,8},{8,0},{1,5},{5,13},{13,9},{9,1},{2,6},{6,14},{... | collective-permute-start | bytes 1966088 | tf_op jit(solution)/shard_map/ppermute | solution.py:341
  756.1 88.8 %collective-permute-start.55 = (bf16[1024,1024]{1,0:T(8,128)(2,1)}, bf16[1024,1024]{1,0:T(8,128)(2,1)}, u32[]{:S(2)}, u32[]{:S(2)}) collective-permute-start(bf16[1024,1024]{1,0:T(8,128)(2,1)} %collective-permute-done.52), channel_id=1, source_target_pairs={{0,4},{12,8},{1,5},{13,9},{2,6},{14,10},{3,7},{15,11},{16,20},{28,... | collective-permute-start | bytes 6291464 | tf_op jit(solution)/shard_map/ppermute | solution.py:354
  759.3 90.1 %collective-permute-start.58 = (bf16[1024,1024]{1,0:T(8,128)(2,1)S(1)}, bf16[1024,1024]{1,0:T(8,128)(2,1)}, u32[]{:S(2)}, u32[]{:S(2)}) collective-permute-start(bf16[1024,1024]{1,0:T(8,128)(2,1)S(1)} %add_convert_fusion.12), channel_id=1, source_target_pairs={{4,8},{8,4},{5,9},{9,5},{6,10},{10,6},{7,11},{11,7},{20,24},{24,20... | collective-permute-start | bytes 6291464 | tf_op jit(solution)/shard_map/ppermute | solution.py:354
  827.1 50.4 %collective-permute-start.61 = (bf16[1024,1024]{1,0:T(8,128)(2,1)S(1)}, bf16[1024,1024]{1,0:T(8,128)(2,1)}, u32[]{:S(2)}, u32[]{:S(2)}) collective-permute-start(bf16[1024,1024]{1,0:T(8,128)(2,1)S(1)} %add_convert_fusion.7), channel_id=1, source_target_pairs={{4,0},{8,12},{5,1},{9,13},{6,2},{10,14},{7,3},{11,15},{20,16},{24,... | collective-permute-start | bytes 6291464 | tf_op jit(solution)/shard_map/ppermute | solution.py:354
  838.9 83.5 %collective-permute-start.75 = (bf16[1024,1024]{1,0:T(8,128)(2,1)S(1)}, bf16[1024,1024]{1,0:T(8,128)(2,1)S(1)}, u32[]{:S(2)}, u32[]{:S(2)}) collective-permute-start(bf16[1024,1024]{1,0:T(8,128)(2,1)S(1)} %add_convert_fusion.2), channel_id=1, source_target_pairs={{4,0},{8,12},{5,1},{9,13},{6,2},{10,14},{7,3},{11,15},{20,16},{24,... | collective-permute-start | bytes 6291464 | tf_op jit(solution)/shard_map/ppermute | solution.py:354
  844.9 91.1 %collective-permute-start.49 = (bf16[1024,1024]{1,0:T(8,128)(2,1)}, bf16[1024,1024]{1,0:T(8,128)(2,1)}, u32[]{:S(2)}, u32[]{:S(2)}) collective-permute-start(bf16[1024,1024]{1,0:T(8,128)(2,1)} %convolution_convert_fusion.2), channel_id=1, source_target_pairs={{0,16},{16,0},{1,17},{17,1},{2,18},{18,2},{3,19},{19,3},{4,20},{20... | collective-permute-start | bytes 6291464 | tf_op jit(solution)/shard_map/ppermute | solution.py:23
  849.5 84.0 %collective-permute-start.40 = (bf16[160,2048]{1,0:T(8,128)(2,1)S(1)}, bf16[160,2048]{1,0:T(8,128)(2,1)S(1)}, u32[]{:S(2)}, u32[]{:S(2)}) collective-permute-start(bf16[160,2048]{1,0:T(8,128)(2,1)S(1)} %slice.491), channel_id=1, source_target_pairs={{0,2},{2,0},{1,3},{3,1},{4,6},{6,4},{5,7},{7,5},{8,10},{10,8},{9,1... | collective-permute-start | bytes 1966088 | tf_op jit(solution)/shard_map/ppermute | solution.py:31
  877.5 143.4 %collective-permute-start.59 = (bf16[1024,1024]{1,0:T(8,128)(2,1)S(1)}, bf16[1024,1024]{1,0:T(8,128)(2,1)S(1)}, u32[]{:S(2)}, u32[]{:S(2)}) collective-permute-start(bf16[1024,1024]{1,0:T(8,128)(2,1)S(1)} %add_convert_fusion.13), channel_id=1, source_target_pairs={{4,8},{8,4},{5,9},{9,5},{6,10},{10,6},{7,11},{11,7},{20,24},{24,20... | collective-permute-start | bytes 6291464 | tf_op jit(solution)/shard_map/ppermute | solution.py:354
  878.3 146.9 %collective-permute-start.62 = (bf16[1024,1024]{1,0:T(8,128)(2,1)S(1)}, bf16[1024,1024]{1,0:T(8,128)(2,1)S(1)}, u32[]{:S(2)}, u32[]{:S(2)}) collective-permute-start(bf16[1024,1024]{1,0:T(8,128)(2,1)S(1)} %add_convert_fusion.8), channel_id=1, source_target_pairs={{4,0},{8,12},{5,1},{9,13},{6,2},{10,14},{7,3},{11,15},{20,16},{24,... | collective-permute-start | bytes 6291464 | tf_op jit(solution)/shard_map/ppermute | solution.py:354
  923.7 117.2 %collective-permute-start.76 = (bf16[1024,1024]{1,0:T(8,128)(2,1)}, bf16[1024,1024]{1,0:T(8,128)(2,1)}, u32[]{:S(2)}, u32[]{:S(2)}) collective-permute-start(bf16[1024,1024]{1,0:T(8,128)(2,1)} %add_convert_fusion.3), channel_id=1, source_target_pairs={{4,0},{8,12},{5,1},{9,13},{6,2},{10,14},{7,3},{11,15},{20,16},{24,... | collective-permute-start | bytes 6291464 | tf_op jit(solution)/shard_map/ppermute | solution.py:354
  940.2 76.8 %collective-permute-start.56 = (bf16[1024,1024]{1,0:T(8,128)(2,1)S(1)}, bf16[1024,1024]{1,0:T(8,128)(2,1)S(1)}, u32[]{:S(2)}, u32[]{:S(2)}) collective-permute-start(bf16[1024,1024]{1,0:T(8,128)(2,1)S(1)} %add_convert_fusion.15), channel_id=1, source_target_pairs={{0,4},{12,8},{1,5},{13,9},{2,6},{14,10},{3,7},{15,11},{16,20},{28,... | collective-permute-start | bytes 6291464 | tf_op jit(solution)/shard_map/ppermute | solution.py:354
  951.7 60.5 %collective-permute-start.44 = (f32[1,4224]{1,0:T(1,128)S(1)}, f32[1,4224]{1,0:T(1,128)S(1)}, u32[]{:S(2)}, u32[]{:S(2)}) collective-permute-start(f32[1,4224]{1,0:T(1,128)S(1)} %add.304), channel_id=1, source_target_pairs={{0,4},{4,0},{8,12},{12,8},{1,5},{5,1},{9,13},{13,9},{2,6},{6,2},{1... | collective-permute-start | bytes 50696 | tf_op jit(solution)/shard_map/ppermute | solution.py:379
  1025.2 50.2 %collective-permute-start.63 = (bf16[1024,1024]{1,0:T(8,128)(2,1)}, bf16[1024,1024]{1,0:T(8,128)(2,1)}, u32[]{:S(2)}, u32[]{:S(2)}) collective-permute-start(bf16[1024,1024]{1,0:T(8,128)(2,1)} %add_convert_fusion.9), channel_id=1, source_target_pairs={{4,0},{8,12},{5,1},{9,13},{6,2},{10,14},{7,3},{11,15},{20,16},{24,... | collective-permute-start | bytes 6291464 | tf_op jit(solution)/shard_map/ppermute | solution.py:354
  1040.9 81.6 %collective-permute-start.77 = (bf16[512,1024]{1,0:T(8,128)(2,1)S(1)}, bf16[512,1024]{1,0:T(8,128)(2,1)S(1)}, u32[]{:S(2)}, u32[]{:S(2)}) collective-permute-start(bf16[512,1024]{1,0:T(8,128)(2,1)S(1)} %add_convert_fusion.16), channel_id=1, source_target_pairs={{4,0},{8,12},{5,1},{9,13},{6,2},{10,14},{7,3},{11,15},{20,16},{24,... | collective-permute-start | bytes 3145736 | tf_op jit(solution)/shard_map/ppermute | solution.py:354
  1075.4 90.7 %collective-permute-start.64 = (bf16[1024,1024]{1,0:T(8,128)(2,1)S(1)}, bf16[1024,1024]{1,0:T(8,128)(2,1)S(1)}, u32[]{:S(2)}, u32[]{:S(2)}) collective-permute-start(bf16[1024,1024]{1,0:T(8,128)(2,1)S(1)} %add_convert_fusion.10), channel_id=1, source_target_pairs={{4,0},{8,12},{5,1},{9,13},{6,2},{10,14},{7,3},{11,15},{20,16},{24,... | collective-permute-start | bytes 6291464 | tf_op jit(solution)/shard_map/ppermute | solution.py:354
  (141 other events, 3008.9 us)

commit v2 on v1

--- a/solution.py
+++ b/solution.py
@@ -36,6 +36,10 @@
     return lax.ppermute(a, ("fsdp", "tp"), pairs)
 
 
+def swap_ctx(a, count, mask):
+    return lax.ppermute(a, "ctx", [(i, i ^ mask) for i in range(count)])
+
+
 def after(value, *others):
     return lax.optimization_barrier((value, *others))[0]
 
@@ -78,10 +82,6 @@
         * lax.rsqrt(jnp.mean(values * values, axis=-1, keepdims=True) + EPSILON)
         * gain
     )
-
-
-def swiglu(gate_in, up_in):
-    return jax.nn.silu(gate_in) * up_in
 
 
 def rope_tables(positions):
@@ -95,47 +95,43 @@
     )
 
 
-def qkv_kernel(nq, nk, part_ref, x_ref, w_ref, cos_ref, sin_ref, q_ref, kv_ref):
-    acc = part_ref[...] + kdot(x_ref[...], w_ref[...], 1, 0)
+def whole(shape):
+    return pl.BlockSpec(shape, lambda i: (0,) * len(shape))
+
+
+def proj_kernel(turns, x_ref, cos_ref, sin_ref, *refs):
+    *weights, out_ref = refs
+    half = weights[0].shape[0]
+    near, far = x_ref[:, :half], x_ref[:, half:]
     cosine, sine = cos_ref[...], sin_ref[...]
-    for h in range(nq + nk):
-        u = acc[:, h * HD : (h + 1) * HD]
-        r = (u * cosine + pltpu.roll(u, HD // 2, 1) * sine).astype(BF16)
-        if h < nq:
-            q_ref[:, h * HD : (h + 1) * HD] = r
-        else:
-            kv_ref[:, (h - nq) * HD : (h - nq + 1) * HD] = r
-    kv_ref[:, nk * HD :] = acc[:, (nq + nk) * HD :].astype(BF16)
-
-
-def qkv_call(part, x, w, cosine, sine, nq, nk):
-    rows, width = part.shape
-    depth = x.shape[1]
+    at = 0
+    for turn, wn, wf in zip(turns, weights[::2], weights[1::2]):
+        acc = kdot(near, wn[...], 1, 0) + kdot(far, wf[...], 1, 0)
+        for h in range(acc.shape[1] // HD):
+            u = acc[:, h * HD : (h + 1) * HD]
+            if turn:
+                u = u * cosine + pltpu.roll(u, HD // 2, 1) * sine
+            out_ref[:, at : at + HD] = u.astype(BF16)
+            at += HD
+
+
+def proj_call(x, cosine, sine, turns, weights):
+    rows, width = x.shape
+    size = rows // 2
+    outs = sum(w.shape[1] for w in weights) // 2
     return pl.pallas_call(
-        partial(qkv_kernel, nq, nk),
-        grid=(rows // BLK,),
+        partial(proj_kernel, turns),
+        grid=(2,),
         in_specs=[
-            pl.BlockSpec((BLK, width), lambda i: (i, 0)),
-            pl.BlockSpec((BLK, depth), lambda i: (i, 0)),
-            pl.BlockSpec((depth, width), lambda i: (0, 0)),
-            pl.BlockSpec((BLK, HD), lambda i: (i, 0)),
-            pl.BlockSpec((BLK, HD), lambda i: (i, 0)),
-        ],
-        out_specs=[
-            pl.BlockSpec((BLK, nq * HD), lambda i: (i, 0)),
-            pl.BlockSpec((BLK, 2 * nk * HD), lambda i: (i, 0)),
-        ],
-        out_shape=[
-            jax.ShapeDtypeStruct((rows, nq * HD), BF16),
-            jax.ShapeDtypeStruct((rows, 2 * nk * HD), BF16),
-        ],
+            pl.BlockSpec((size, width), lambda i: (i, 0)),
+            pl.BlockSpec((size, HD), lambda i: (i, 0)),
+            pl.BlockSpec((size, HD), lambda i: (i, 0)),
+        ]
+        + [whole(w.shape) for w in weights],
+        out_specs=pl.BlockSpec((size, outs), lambda i: (i, 0)),
+        out_shape=jax.ShapeDtypeStruct((rows, outs), BF16),
         compiler_params=pltpu.CompilerParams(vmem_limit_bytes=VMEM_LIMIT),
-        cost_estimate=pl.CostEstimate(
-            flops=2 * rows * width * depth,
-            bytes_accessed=rows * width * 6 + rows * depth * 2 + depth * width * 2,
-            transcendentals=0,
-        ),
-    )(part, x, w, cosine, sine)
+    )(x, cosine, sine, *weights)
 
 
 def attend_parts(meta_ref, block, unit, trunk, step):
@@ -207,11 +203,6 @@
             jax.ShapeDtypeStruct(q.shape, F32),
         ],
         compiler_params=pltpu.CompilerParams(vmem_limit_bytes=VMEM_LIMIT),
-        cost_estimate=pl.CostEstimate(
-            flops=8 * rows * nk * HD * (trunk + 2 * unit),
-            bytes_accessed=kv.size * 2 + q.size * 12,
-            transcendentals=2 * rows * nk * (trunk + 2 * unit),
-        ),
     )(meta, q, kv, kv)
 
 
@@ -284,11 +275,6 @@
             jax.ShapeDtypeStruct((length, nk * HD), F32),
         ],
         compiler_params=pltpu.CompilerParams(vmem_limit_bytes=VMEM_LIMIT),
-        cost_estimate=pl.CostEstimate(
-            flops=20 * rows * nk * HD * (trunk + 2 * unit),
-            bytes_accessed=kv.size * 6 + q.size * 16,
-            transcendentals=2 * rows * nk * (trunk + 2 * unit),
-        ),
     )(meta, q, kv, kv, grad_context, context, total, cosine, sine)
 
 
@@ -309,6 +295,293 @@
         out_shape=jax.ShapeDtypeStruct((rows, width), BF16),
         compiler_params=pltpu.CompilerParams(vmem_limit_bytes=VMEM_LIMIT),
     )(sums, cosine, sine)
+
+
+TILE = 256
+
+
+def gathered(pieces, out_ref):
+    @pl.when(pl.program_id(0) == 0)
+    def _():
+        size = pieces[0].shape[0]
+        for j, piece in enumerate(pieces):
+            out_ref[j * size : (j + 1) * size, :] = piece[...]
+
+
+def row_loop(rows, body):
+    size = rows // 2
+
+    @pl.loop(0, 2)
+    def _(r):
+        body(pl.ds(pl.multiple_of(r * size, size), size))
+
+
+def up_kernel(gathers, *refs):
+    n = 8 if gathers else 1
+    pieces, (gn, gf, un, uf, gate_ref, up_ref, act_ref), rest = refs[:n], refs[n : n + 7], refs[n + 7 :]
+    half = gn.shape[0]
+    x_ref = rest[0] if gathers else pieces[0]
+    if gathers:
+        gathered(pieces, x_ref)
+
+    def body(here):
+        near, far = x_ref[here, :half], x_ref[here, half:]
+        gate = kdot(near, gn[...], 1, 0) + kdot(far, gf[...], 1, 0)
+        up = kdot(near, un[...], 1, 0) + kdot(far, uf[...], 1, 0)
+        gate_ref[here, :] = gate
+        up_ref[here, :] = up
+        act_ref[here, :] = (gate * jax.nn.sigmoid(gate) * up).astype(BF16)
+
+    row_loop(x_ref.shape[0], body)
+
+
+def up_call(pieces, gate_near, gate_far, up_near, up_far):
+    gathers = len(pieces) == 8
+    size, width = pieces[0].shape
+    rows = len(pieces) * size
+    depth, hidden = gate_near.shape
+    weight = pl.BlockSpec((depth, TILE), lambda i: (0, i))
+    tile = pl.BlockSpec((rows, TILE), lambda i: (0, i))
+    outs = [((rows, hidden), F32), ((rows, hidden), F32), ((rows, hidden), BF16)]
+    return pl.pallas_call(
+        partial(up_kernel, gathers),
+        grid=(hidden // TILE,),
+        in_specs=[whole((size, width))] * len(pieces) + [weight] * 4,
+        out_specs=[tile, tile, tile] + ([whole((rows, width))] if gathers else []),
+        out_shape=[
+            jax.ShapeDtypeStruct(shape, kind)
+            for shape, kind in outs + ([((rows, width), BF16)] if gathers else [])
+        ],
+        compiler_params=pltpu.CompilerParams(vmem_limit_bytes=VMEM_LIMIT),
+    )(*pieces, gate_near, gate_far, up_near, up_far)
+
+
+def act_back_kernel(gathers, *refs):
+    n = 8 if gathers else 1
+    pieces, (dn, df, gate_ref, up_ref, gg_ref, gu_ref), rest = refs[:n], refs[n : n + 6], refs[n + 6 :]
+    half = dn.shape[1]
+    x_ref = rest[0] if gathers else pieces[0]
+    if gathers:
+        gathered(pieces, x_ref)
+
+    def body(here):
+        grad_act = kdot(x_ref[here, :half], dn[...], 1, 1) + kdot(x_ref[here, half:], df[...], 1, 1)
+        gate, up = gate_ref[here, :], up_ref[here, :]
+        sg = jax.nn.sigmoid(gate)
+        gg_ref[here, :] = (grad_act * up * sg * (1.0 + gate * (1.0 - sg))).astype(BF16)
+        gu_ref[here, :] = (grad_act * (gate * sg)).astype(BF16)
+
+    row_loop(x_ref.shape[0], body)
+
+
+def act_back_call(pieces, down_near, down_far, gate, up):
+    gathers = len(pieces) == 8
+    size, width = pieces[0].shape
+    rows = len(pieces) * size
+    hidden, depth = down_near.shape
+    weight = pl.BlockSpec((TILE, depth), lambda i: (i, 0))
+    tile = pl.BlockSpec((rows, TILE), lambda i: (0, i))
+    outs = [((rows, hidden), BF16), ((rows, hidden), BF16)]
+    return pl.pallas_call(
+        partial(act_back_kernel, gathers),
+        grid=(hidden // TILE,),
+        in_specs=[whole((size, width))] * len(pieces) + [weight] * 2 + [tile] * 2,
+        out_specs=[tile, tile] + ([whole((rows, width))] if gathers else []),
+        out_shape=[
+            jax.ShapeDtypeStruct(shape, kind)
+            for shape, kind in outs + ([((rows, width), BF16)] if gathers else [])
+        ],
+        compiler_params=pltpu.CompilerParams(vmem_limit_bytes=VMEM_LIMIT),
+    )(*pieces, down_near, down_far, gate, up)
+
+
+def out_kernel(count, contract, last, *refs):
+    lefts, nears, fars, rest = (
+        refs[:count],
+        refs[count : 2 * count],
+        refs[2 * count : 3 * count],
+        refs[3 * count :],
+    )
+    i = pl.program_id(0)
+    near_at = pl.ds(pl.multiple_of(i * TILE, TILE), TILE)
+    width = rest[0].shape[1]
+    far_at = pl.ds(pl.multiple_of(width // 2 + i * TILE, TILE), TILE)
+    quarter = rest[0].shape[0] // 4
+
+    def product(weights):
+        total = kdot(lefts[0][...], weights[0][...], 1, contract)
+        for left, weight in zip(lefts[1:], weights[1:]):
+            total = total + kdot(left[...], weight[...], 1, contract)
+        return total
+
+    near, far = product(nears), product(fars)
+    if not last:
+        rest[0][:, near_at] = near.astype(BF16)
+        rest[0][:, far_at] = far.astype(BF16)
+        return
+    sent, own_ref, y_ref, x_ref, xy_ref = rest
+    near = near + sent[:, near_at].astype(F32)
+    far = far + sent[:, far_at].astype(F32)
+    own_ref[:, near_at] = near[:quarter]
+    own_ref[:, far_at] = far[:quarter]
+    near, far = near.astype(BF16), far.astype(BF16)
+    y_ref[:, near_at] = near[quarter : 2 * quarter]
+    y_ref[:, far_at] = far[quarter : 2 * quarter]
+    x_ref[:, near_at] = far[2 * quarter : 3 * quarter]
+    x_ref[:, far_at] = near[2 * quarter : 3 * quarter]
+    xy_ref[:, near_at] = far[3 * quarter :]
+    xy_ref[:, far_at] = near[3 * quarter :]
+
+
+def out_call(lefts, nears, fars, contract, group, sent=None):
+    rows = lefts[0].shape[0] // 2
+    quarter = rows // 4
+    depth = lefts[0].shape[1]
+    half = nears[0].shape[1 - contract]
+    if contract == 0:
+        weight = pl.BlockSpec((depth, TILE), lambda i: (0, i))
+    else:
+        weight = pl.BlockSpec((TILE, depth), lambda i: (i, 0))
+    n = len(lefts)
+    last = sent is not None
+    full = (rows, 2 * half)
+    piece = (quarter, 2 * half)
+    outs = [(piece, F32), (piece, BF16), (piece, BF16), (piece, BF16)] if last else [(full, BF16)]
+    got = pl.pallas_call(
+        partial(out_kernel, n, contract, last),
+        grid=(half // TILE,),
+        in_specs=[pl.BlockSpec((rows, depth), lambda i: (group, 0))] * n
+        + [weight] * (2 * n)
+        + ([whole(full)] if last else []),
+        out_specs=[whole(shape) for shape, _ in outs],
+        out_shape=[jax.ShapeDtypeStruct(shape, kind) for shape, kind in outs],
+        compiler_params=pltpu.CompilerParams(vmem_limit_bytes=VMEM_LIMIT),
+    )(*lefts, *nears, *fars, *((sent,) if last else ()))
+    return got if last else got[0]
+
+
+def all_up_kernel(first_ref, near_ref, far_ref, gn, gf, un, uf, gate_ref, up_ref, act_ref):
+    near, far = near_ref[...], far_ref[...]
+    gate = kdot(near, gn[...], 1, 0) + kdot(far, gf[...], 1, 0)
+    up = kdot(near, un[...], 1, 0) + kdot(far, uf[...], 1, 0)
+    gate_ref[...] = gate
+    up_ref[...] = up
+    act_ref[...] = (gate * jax.nn.sigmoid(gate) * up).astype(BF16)
+
+
+def fixed(shape):
+    return pl.BlockSpec(shape, lambda i, f: (0,) * len(shape))
+
+
+def halves_of_rows(size, width):
+    return [
+        pl.BlockSpec((size, width // 2), lambda i, f: (i, f[0])),
+        pl.BlockSpec((size, width // 2), lambda i, f: (i, 1 - f[0])),
+    ]
+
+
+def all_up_call(first, x, size, weights):
+    tokens, width = x.shape
+    hidden = weights[0].shape[1]
+    tile = pl.BlockSpec((size, hidden), lambda i, f: (i, 0))
+    return pl.pallas_call(
+        all_up_kernel,
+        grid_spec=pltpu.PrefetchScalarGridSpec(
+            num_scalar_prefetch=1,
+            grid=(tokens // size,),
+            in_specs=halves_of_rows(size, width) + [fixed(w.shape) for w in weights],
+            out_specs=[tile] * 3,
+        ),
+        out_shape=[jax.ShapeDtypeStruct((tokens, hidden), kind) for kind in (F32, F32, BF16)],
+        compiler_params=pltpu.CompilerParams(vmem_limit_bytes=VMEM_LIMIT),
+        cost_estimate=pl.CostEstimate(
+            flops=4 * tokens * width * hidden, bytes_accessed=0, transcendentals=0
+        ),
+    )(first, x, x, *weights)
+
+
+def put_sums(out, sum_gate, sum_up, sum_down):
+    half, depth = sum_gate.shape[1], sum_gate.shape[0]
+    out[:half, :] = sum_gate[...].T.astype(BF16)
+    out[half : 2 * half, :] = sum_up[...].T.astype(BF16)
+    down = sum_down[...].astype(BF16)
+    out[2 * half : 2 * half + depth, :] = down[:, :depth]
+    out[2 * half + depth :, :] = down[:, depth:]
+
+
+def add_sums(sums, gg, gu, act, x, g):
+    @pl.when(pl.program_id(0) == 0)
+    def _():
+        for total in sums:
+            total[...] = jnp.zeros_like(total)
+
+    sums[0][...] += kdot(gg, x, 0, 0)
+    sums[1][...] += kdot(gu, x, 0, 0)
+    sums[2][...] += kdot(act, g, 0, 0)
+
+
+def far_grads_kernel(
+    first_ref, xf, gn, gf, dn, df, gate_ref, up_ref, act_ref, far_ref, gg_ref, gu_ref, *sums
+):
+    grad_act = kdot(gn[...], dn[...], 1, 1) + kdot(gf[...], df[...], 1, 1)
+    gate, up = gate_ref[...], up_ref[...]
+    sg = jax.nn.sigmoid(gate)
+    gg = (grad_act * up * sg * (1.0 + gate * (1.0 - sg))).astype(BF16)
+    gu = (grad_act * (gate * sg)).astype(BF16)
+    gg_ref[...] = gg
+    gu_ref[...] = gu
+    add_sums(sums, gg, gu, act_ref[...], xf[...], gf[...])
+
+    @pl.when(pl.program_id(0) == pl.num_programs(0) - 1)
+    def _():
+        put_sums(far_ref, *sums)
+
+
+def near_grads_kernel(first_ref, xn, gn, act_ref, gg_ref, gu_ref, near_ref, *sums):
+    add_sums(sums, gg_ref[...], gu_ref[...], act_ref[...], xn[...], gn[...])
+
+    @pl.when(pl.program_id(0) == pl.num_programs(0) - 1)
+    def _():
+        put_sums(near_ref, *sums)
+
+
+def grads_call(kernel, first, wides, fixeds, tiles, size, outs, products):
+    tokens, width = wides[0][0].shape
+    half = width // 2
+    depth = tiles[0].shape[1]
+    assert half == 2 * depth
+    near, far = halves_of_rows(size, width)
+    tile = pl.BlockSpec((size, depth), lambda i, f: (i, 0))
+    shape = (3 * half, depth)
+    return pl.pallas_call(
+        kernel,
+        grid_spec=pltpu.PrefetchScalarGridSpec(
+            num_scalar_prefetch=1,
+            grid=(tokens // size,),
+            in_specs=[near if own else far for _, own in wides]
+            + [fixed(w.shape) for w in fixeds]
+            + [tile] * len(tiles),
+            out_specs=[fixed(shape)] + [tile] * outs,
+            scratch_shapes=[pltpu.VMEM((depth, half), F32)] * 3,
+        ),
+        out_shape=[jax.ShapeDtypeStruct(shape, BF16)]
+        + [jax.ShapeDtypeStruct((tokens, depth), BF16)] * outs,
+        compiler_params=pltpu.CompilerParams(vmem_limit_bytes=VMEM_LIMIT),
+        cost_estimate=products
+        and pl.CostEstimate(
+            flops=products * tokens * width * depth, bytes_accessed=0, transcendentals=0
+        ),
+    )(first, *(a for a, _ in wides), *fixeds, *tiles)
+
+
+def far_grads_call(first, x, g, size, weights, forward):
+    wides = [(x, False), (g, True), (g, False)]
+    return grads_call(far_grads_kernel, first, wides, weights, forward, size, 2, 5)
+
+
+def near_grads_call(first, x, g, size, act, back):
+    wides = [(x, True), (g, True)]
+    return grads_call(near_grads_kernel, first, wides, (), (act, *back), size, 0, None)[0]
 
 
 def gather_ctx(a, count, c):
@@ -325,52 +598,54 @@
     return out
 
 
+def gather_small(a, count, c):
+    out = jnp.zeros((count, a.shape[0]), a.dtype)
+    out = lax.dynamic_update_slice_in_dim(out, a[None], c, axis=0)
+    return sum_ctx(out, count).reshape(-1)
+
+
 def scatter_ctx(a, count, c):
     rows = a.shape[0] // count
     if count != 4:
         return lax.psum_scatter(a, "ctx", scatter_dimension=0, tiled=True)
-    ring = [(0, 1), (1, 3), (3, 2), (2, 0)]
-    owners = [table((2, 0, 3, 1), c), 3 - c, table((1, 3, 0, 2), c), c]
-    carried = None
-    for step in range(4):
-        mine = lax.dynamic_slice_in_dim(a, owners[step] * rows, rows, axis=0)
-        if carried is not None:
-            mine = mine + carried.astype(F32)
-        if step == 3:
-            return mine
-        carried = lax.ppermute(mine.astype(BF16), "ctx", ring)
-
-
-class LineSum:
-    def __init__(self, count, c):
-        self.count = count
-        self.middle = (c == 1) | (c == 2)
-        self.last = [[], [], []]
-
-    def move(self, stage, a, pairs):
-        past = self.last[stage]
-        if len(past) >= 2:
-            a = after(a, past[-2])
-        a = lax.ppermute(a, "ctx", pairs)
-        past.append(a)
-        return a
-
-    def __call__(self, a):
-        if self.count != 4:
-            return lax.psum(a.astype(F32), "ctx")
-        got = self.move(0, a, [(0, 1), (3, 2)])
-        pair = (a.astype(F32) + got.astype(F32)).astype(BF16)
-        got = self.move(1, pair, [(1, 2), (2, 1)])
-        whole = (pair.astype(F32) + got.astype(F32)).astype(BF16)
-        got = self.move(2, whole, [(1, 0), (2, 3)])
-        return jnp.where(self.middle, whole, got).astype(F32)
-
-
-def sum_all(a, count):
+    total = lax.dynamic_slice_in_dim(a, c * rows, rows, axis=0)
+    sent = [
+        lax.dynamic_slice_in_dim(a, (c ^ d) * rows, rows, axis=0).astype(BF16)
+        for d in (3, 2, 1)
+    ]
+    for d, block in zip((3, 2, 1), sent):
+        total = total + swap_ctx(block, count, d).astype(F32)
+    return total
+
+
+def line_sum(a):
+    return lax.psum(a, "ctx").astype(F32)
+
+
+def sum_planes(a, count, c):
+    if count != 4:
+        return lax.psum(a, "ctx")
+    rows = a.shape[0] // count
+
+    def share(index):
+        return lax.dynamic_slice_in_dim(a, index * rows, rows, axis=0)
+
+    total = share(c).astype(F32)
+    for d in (3, 2, 1):
+        total = total + swap_ctx(share(c ^ d), count, d).astype(F32)
+    total = total.astype(BF16)
+    out = jnp.zeros_like(a)
+    for d in (3, 2, 1, 0):
+        block = swap_ctx(total, count, d) if d else total
+        out = lax.dynamic_update_slice_in_dim(out, block, (c ^ d) * rows, axis=0)
+    return out
+
+
+def sum_all(a, count, *behind):
     a = a + swap_core(a)
     a = a + swap_y(a)
-    a = a + swap_x(a)
-    return sum_ctx(a, count)
+    a = sum_ctx(a, count)
+    return a + swap_x(after(a, *behind))
 
 
 def sum_ctx(a, count):
@@ -393,8 +668,10 @@
     tree_len = rows * count
     unit = tree_len // 20
     trunk = 8 * unit
-    nq, nk = w_query.shape[1] // HD, w_key.shape[1] // HD
+    nk = w_key.shape[1] // HD
     eighth = w_gate.shape[1] // 2
+    part = eighth // 2
+    parity = c % 2
     first = f == 0
 
     def turned(a):
@@ -416,57 +693,55 @@
 
     def gather_plane(x):
         flipped = halves_swapped(x)
-        over_x, over_y, over_xy = swap_x(flipped), swap_y(x), swap_xy(flipped)
-        group = jnp.concatenate([x, over_y, over_x, over_xy], axis=0)
-        return jnp.concatenate([group, swap_core(group)], axis=0)
-
-    def scatter_tp(product, a):
+        group = [x, swap_y(x), swap_x(flipped), swap_xy(flipped)]
+        return group + [swap_core(a) for a in group]
+
+    def gather_all(x):
+        return lax.all_gather(turned(x), ("fsdp", "ctx", "tp"), axis=0, tiled=True)
+
+    def halves_tp(product, a):
         cols = a.shape[1]
         blocks = a.reshape(2, 2, quarter, cols)
         sent = swap_core(product(blocks[:, 1].reshape(2 * quarter, cols)).astype(BF16))
         kept = product(blocks[:, 0].reshape(2 * quarter, cols)) + sent.astype(F32)
-        over_y = swap_y(kept[quarter:].astype(BF16))
-        return kept[:quarter] + over_y.astype(F32)
-
-    def scatter_plane(product, *arrays):
-        near = [a[: 4 * quarter] for a in arrays]
-        far = [a[4 * quarter :] for a in arrays]
-        sent = swap_core(product(*far).astype(BF16))
-        kept = product(*near) + sent.astype(F32)
-        to_y = kept[quarter : 2 * quarter].astype(BF16)
-        to_x = halves_swapped(kept[2 * quarter : 3 * quarter].astype(BF16))
-        to_xy = halves_swapped(kept[3 * quarter :].astype(BF16))
+        return kept[:quarter], kept[quarter:].astype(BF16)
+
+    def scatter_out(lefts, nears, fars, contract):
+        sent = swap_core(out_call(lefts, nears, fars, contract, 1))
+        return out_call(lefts, nears, fars, contract, 0, sent)
+
+    def scatter_sum(products, *meanwhile):
+        kept, to_y, to_x, to_xy = products
         over_xy, over_y, over_x = swap_xy(to_xy), swap_y(to_y), swap_x(to_x)
-        return (
-            kept[:quarter]
-            + over_y.astype(F32)
-            + over_x.astype(F32)
-            + over_xy.astype(F32)
-        )
-
-    near_qkv = jnp.concatenate([w_query, w_key, w_value], axis=1)
-    far_qkv = swap_x(near_qkv)
+        kept = after(kept, *meanwhile)
+        return kept + over_y.astype(F32) + over_x.astype(F32) + over_xy.astype(F32)
+
+    far_key, far_value = swap_x(w_key), swap_x(w_value)
     far_gains = swap_x(jnp.stack([attn_gain, ffn_gain]))
     gain_attn = jnp.concatenate([attn_gain, far_gains[0]]).astype(F32)
     gain_ffn = jnp.concatenate([ffn_gain, far_gains[1]]).astype(F32)
-    far_out = swap_x(after(w_out, far_qkv))
-    out_full = jnp.concatenate([w_out, far_out], axis=1)
-
-    def exchanged(w, axis, *behind):
-        kept = lax.dynamic_slice_in_dim(w, f * eighth, eighth, axis=axis)
-        sent = lax.dynamic_slice_in_dim(w, (1 - f) * eighth, eighth, axis=axis)
-        got = swap_x(after(sent, *behind))
-        return jnp.concatenate([kept, got], axis=1 - axis), got
-
-    gate_w, got = exchanged(w_gate, 1, far_out)
-    up_w, got = exchanged(w_up, 1, got)
-    down_w, got = exchanged(w_down, 0, got)
+    far_query = swap_x(after(w_query, far_key, far_value))
+    far_out = swap_x(after(w_out, far_query))
+
+    def exchanged(w, axis, share, *behind):
+        def cut(index, which):
+            return lax.dynamic_slice_in_dim(w, index * eighth + which * part, part, axis=axis)
+
+        got = swap_x(after(cut(1 - f, parity), *behind))
+        if not share:
+            other = swap_x(after(cut(1 - f, 1 - parity), *behind))
+        else:
+            other = swap_ctx(got, count, 1)
+        return (cut(f, parity), got), (cut(f, 1 - parity), other)
+
+    gate_p, gate_o = exchanged(w_gate, 1, True, far_out)
+    up_p, up_o = exchanged(w_up, 1, True, gate_p[1])
 
     labels = jnp.arange(parents.shape[0], dtype=jnp.int32)
     seg = segment_ids[::BLK]
     parent = jnp.sum(jnp.where(seg[:, None] == labels[None, :], parents[None, :], 0), axis=1)
     grand = jnp.sum(jnp.where(parent[:, None] == labels[None, :], parents[None, :], 0), axis=1)
-    all_seg = lax.all_gather(seg, "ctx", axis=0, tiled=True)
+    all_seg = gather_small(seg, count, c)
     spots = jnp.arange(all_seg.shape[0], dtype=jnp.int32)
     parent_spot = jnp.min(
         jnp.where(all_seg[None, :] == parent[:, None], spots[None, :], all_seg.shape[0] - 1),
@@ -499,20 +774,32 @@
     hidden = turned(hidden_in)
     normed = rms_scale(hidden.astype(F32), gain_attn).astype(BF16)
     near_normed, far_normed = normed[:, :half], normed[:, half:]
-    query, kv = qkv_call(dot(near_normed, near_qkv), far_normed, far_qkv, cosine, sine, nq, nk)
+    normed_in, meta, valid_count = lax.optimization_barrier((normed, meta, valid_count))
+    kv = proj_call(
+        normed_in, cosine, sine, (True, False), (w_key, far_key, w_value, far_value)
+    )
+    query = proj_call(after(normed_in, kv), cosine, sine, (True,), (w_query, far_query))
     kv_all = gather_ctx(kv, count, c)
-    attended, context, total = fwd_call(meta, query, kv_all, nk, unit, trunk)
-    attended = reordered(attended)
-    attn_out = scatter_tp(lambda a: dot(a, out_full), attended)
+    query_in, out_full = lax.optimization_barrier(
+        (query, jnp.concatenate([w_out, far_out], axis=1))
+    )
+    attended, context, total = fwd_call(meta, query_in, kv_all, nk, unit, trunk)
+    attended = after(reordered(attended), gate_p[1])
+    kept, to_y = halves_tp(lambda a: dot(a, out_full), attended)
+    attn_out = kept + swap_y(to_y).astype(F32)
 
     hidden_own = own_rows(hidden).astype(F32)
     middle = hidden_own + attn_out
-    normed_ffn = gather_plane(rms_scale(middle, gain_ffn).astype(BF16))
-    gate_proj = dot(normed_ffn, gate_w)
-    up_proj = dot(normed_ffn, up_w)
-    activated_f, swiglu_back = jax.vjp(swiglu, gate_proj, up_proj)
-    activated = activated_f.astype(BF16)
-    output_f = middle + scatter_plane(lambda a: dot(a, down_w), activated)
+    normed_own = after(rms_scale(middle, gain_ffn).astype(BF16), up_p[1], gate_o[1])
+    normed_pieces = gather_plane(normed_own)
+    down_p, down_o = exchanged(w_down, 0, False, normed_pieces[2])
+    *act_p, normed_ffn = up_call(normed_pieces, *gate_p, *up_p)
+    shares = count == 4
+    normed_ffn = after(normed_ffn, down_p[1])
+    act_o = list(up_call([normed_ffn], *gate_o, *up_o))
+    output_f = middle + scatter_sum(
+        scatter_out([act_p[2], act_o[2]], [down_p[0], down_o[0]], [down_p[1], down_o[1]], 0)
+    )
 
     deviation = output_f - turned(own_rows(teacher)).astype(F32)
     valid_own = lax.dynamic_slice_in_dim(valid_f, t * quarter, quarter, axis=0)
@@ -521,49 +808,131 @@
     loss_factor = float(width * tokens_all // 2)
     grad_output = loss_factor * 2.0 / width * valid_own[:, None] * deviation / valid_count
 
-    line_sum = LineSum(count, c)
-    grad_ffn = gather_plane(grad_output.astype(BF16))
-    grad_act = dot_nt(grad_ffn, down_w)
-    grad_gate_f, grad_up_f = swiglu_back(grad_act)
-    grad_gate, grad_up = grad_gate_f.astype(BF16), grad_up_f.astype(BF16)
-
-    down_sent = swap_x(dot_tn(activated, grad_ffn[:, half:], BF16))
-    down_near = line_sum(dot_tn(activated, grad_ffn[:, :half], BF16))
-    gate_sent = swap_x(after(dot_tn(normed_ffn[:, half:], grad_gate, BF16), down_sent))
-    down_far = line_sum(down_sent)
-    up_sent = swap_x(after(dot_tn(normed_ffn[:, half:], grad_up, BF16), gate_sent))
-    gate_near = line_sum(dot_tn(normed_ffn[:, :half], grad_gate, BF16))
-    gate_far = line_sum(gate_sent)
-    up_near = line_sum(dot_tn(normed_ffn[:, :half], grad_up, BF16))
-    up_far = line_sum(up_sent)
-
-    grad_normed_ffn = scatter_plane(
-        lambda a, b: dot_nt(a, gate_w) + dot_nt(b, up_w), grad_gate, grad_up
-    )
+    grad_own = grad_output.astype(BF16)
+    grad_pieces = gather_plane(grad_own)
+    if shares:
+        normed_all, grad_all = gather_all(normed_own), gather_all(grad_own)
+        place = f.reshape(1)
+    gg_p, gu_p, grad_ffn = act_back_call(grad_pieces, *down_p, act_p[0], act_p[1])
+    gg_o, gu_o = act_back_call([grad_ffn], *down_o, act_o[0], act_o[1])
+    products = scatter_out(
+        [gg_p, gu_p, gg_o, gu_o],
+        [gate_p[0], up_p[0], gate_o[0], up_o[0]],
+        [gate_p[1], up_p[1], gate_o[1], up_o[1]],
+        1,
+    )
+    meanwhile = ()
+    if shares:
+        ahead_p = all_up_call(after(place, products[0]), normed_all, rows, (*gate_p, *up_p))
+        meanwhile = ahead_p
+    grad_normed_ffn = scatter_sum(products, *meanwhile)
+
+    def joined(blocks, axis):
+        shape = list(blocks[0][0].shape)
+        shape[axis] *= 4
+        out = jnp.zeros(shape, F32)
+        for block, index, which in blocks:
+            out = lax.dynamic_update_slice_in_dim(
+                out, block.astype(F32), index * eighth + which * part, axis=axis
+            )
+        return out
+
     _, norm_ffn_back = jax.vjp(rms_scale, middle, gain_ffn)
     grad_middle_part, grad_ffn_gain = norm_ffn_back(grad_normed_ffn)
     grad_middle = grad_output + grad_middle_part
 
-    grad_attn = jnp.concatenate(gather_tp(grad_middle.astype(BF16)), axis=0)
+    grad_attn = gather_tp(grad_middle.astype(BF16))
+    if shares:
+        ahead_o = all_up_call(after(place, grad_middle), normed_all, rows, (*gate_o, *up_o))
+        grad_attn[0] = after(grad_attn[0], *ahead_o)
+    grad_attn = jnp.concatenate(grad_attn, axis=0)
     out_sent = swap_x(dot_tn(attended, grad_attn[:, half:], BF16))
-    grad_out = line_sum(
-        (dot_tn(attended, grad_attn[:, :half]) + out_sent.astype(F32)).astype(BF16)
-    )
+    out_kept = dot_tn(attended, grad_attn[:, :half])
     grad_context = reordered(dot_nt(grad_attn, out_full))
+    if shares:
+        grad_context, grad_all = lax.optimization_barrier((grad_context, grad_all))
     grad_query, key_terms, value_terms = bwd_call(
         meta, query, kv_all, grad_context, context, total, cosine, sine, nk, unit, trunk
     )
+    def query_weights():
+        sent = swap_x(dot_tn(far_normed, grad_query, BF16))
+        return sent, dot_tn(near_normed, grad_query)
+
+    query_sent, query_kept = query_weights()
+    if shares:
+        blocks = [[], [], []]
+
+        def keep(near, far, which):
+            for side, index in ((near, f), (far, 1 - f)):
+                gate, up, down = (side[k * half : (k + 1) * half] for k in range(3))
+                blocks[0].append((gate, index, which))
+                blocks[1].append((up, index, which))
+                down = jnp.concatenate([down[:part], down[part:]], axis=1)
+                blocks[2].append((down, index, which))
+
+        place = after(place, grad_query)
+        done, *back_p = far_grads_call(place, normed_all, grad_all, rows, down_p, ahead_p)
+    else:
+
+        def ordered(a, b):
+            return jnp.where(parity == 0, a, b), jnp.where(parity == 0, b, a)
+
+        def summed(pair_p, pair_o, axis):
+            blocks = []
+            for which, (near, far) in enumerate(zip(*(ordered(a, b) for a, b in zip(pair_p, pair_o)))):
+                blocks.append((line_sum(near), f, which))
+                blocks.append((line_sum(swap_x(far)), 1 - f, which))
+            return joined(blocks, axis)
+
+        def columns(g):
+            return dot_tn(normed_ffn[:, :half], g, BF16), dot_tn(normed_ffn[:, half:], g, BF16)
+
+        def lines(a):
+            return dot_tn(a, grad_ffn[:, :half], BF16), dot_tn(a, grad_ffn[:, half:], BF16)
+
+        grad_gate_w = summed(columns(gg_p), columns(gg_o), 1)
+        grad_up_w = summed(columns(gu_p), columns(gu_o), 1)
+        grad_down_w = summed(lines(act_p[2]), lines(act_o[2]), 0)
+
     kv_sums = scatter_ctx(jnp.concatenate([key_terms, value_terms], axis=1), count, c)
+    if shares:
+        kv_sums = after(kv_sums, done)
     grad_kv = dkv_call(kv_sums, cosine, sine, nk)
-    grad_qkv = jnp.concatenate([grad_query, grad_kv], axis=1)
-    qkv_sent = swap_x(dot_tn(far_normed, grad_qkv, BF16))
-    grad_qkv_w = line_sum(
-        (dot_tn(near_normed, grad_qkv) + qkv_sent.astype(F32)).astype(BF16)
-    )
-    grad_normed = scatter_tp(
-        lambda a: jnp.concatenate([dot_nt(a, near_qkv), dot_nt(a, far_qkv)], axis=1),
-        reordered(grad_qkv),
-    )
+    kv_sent = dot_tn(far_normed, grad_kv, BF16)
+    kv_sent = swap_x(kv_sent)
+    kv_kept = dot_tn(near_normed, grad_kv)
+    out_kept = after(out_kept, grad_query)
+    query_part = (query_kept + query_sent.astype(F32)).astype(BF16)
+    out_part = (out_kept + out_sent.astype(F32)).astype(BF16)
+    nears = jnp.concatenate([w_query, w_key, w_value], axis=1)
+    fars = jnp.concatenate([far_query, far_key, far_value], axis=1)
+    kept, to_y = halves_tp(
+        lambda a: jnp.concatenate([dot_nt(a, nears), dot_nt(a, fars)], axis=1),
+        reordered(jnp.concatenate([grad_query, grad_kv], axis=1)),
+    )
+    if shares:
+        over_p = swap_x(after(done, query_sent))
+        place = after(place, done, to_y, kv_kept, query_part, out_part)
+        far, *back_o = far_grads_call(place, normed_all, grad_all, rows, down_o, ahead_o)
+        over_o = swap_x(far)
+        over_y = swap_y(to_y)
+        over_y, place = lax.optimization_barrier((over_y, after(place, far)))
+        near = near_grads_call(place, normed_all, grad_all, rows, ahead_p[2], back_p)
+        first_near = near
+        kv_kept, over_p, place = lax.optimization_barrier(
+            (kv_kept, over_p, after(place, near))
+        )
+        near = near_grads_call(place, normed_all, grad_all, rows, ahead_o[2], back_o)
+        keep(first_near, over_p, parity)
+        keep(near, over_o, 1 - parity)
+        grad_gate_w, grad_up_w, grad_down_w = (
+            joined(b, axis) for b, axis in zip(blocks, (1, 1, 0))
+        )
+    else:
+        over_y = swap_y(to_y)
+    grad_query_w, grad_out_w = lax.psum((query_part, out_part), "ctx")
+    grad_kv_w = sum_planes((kv_kept + kv_sent.astype(F32)).astype(BF16), count, c).astype(F32)
+    grad_normed = kept + over_y.astype(F32)
     _, norm_attn_back = jax.vjp(rms_scale, hidden_own, gain_attn)
     grad_hidden_part, grad_attn_gain = norm_attn_back(grad_normed)
     grad_hidden = grad_middle + grad_hidden_part
@@ -576,31 +945,24 @@
             )
         return out
 
-    def joined(near, far, axis):
-        shape = list(near.shape)
-        shape[axis] *= 2
-        out = jnp.zeros(shape, F32)
-        out = lax.dynamic_update_slice_in_dim(out, near, f * eighth, axis=axis)
-        return lax.dynamic_update_slice_in_dim(out, far, (1 - f) * eighth, axis=axis)
-
-    small = jnp.concatenate([turned(grad_attn_gain), turned(grad_ffn_gain)])
-    small = jnp.concatenate([small, jnp.full((HD,), error_sum, F32)]).reshape(1, -1)
-    small = sum_all(small, count)[0]
+    small = jnp.concatenate(
+        [turned(grad_attn_gain), turned(grad_ffn_gain), jnp.full((HD,), error_sum, F32)]
+    ).reshape(1, -1)
+    small = sum_all(small, count, *((over_o,) if shares else ()))[0]
     loss_value = small[2 * width] / valid_count
     own_attn_gain = lax.dynamic_slice_in_dim(small[:width], f * half, half)
     own_ffn_gain = lax.dynamic_slice_in_dim(small[width : 2 * width], f * half, half)
-    nqw, nkw = nq * HD, nk * HD
     return (
-        whole_rows(turned(output_f).astype(BF16), BF16),
+        whole_rows(after(turned(output_f).astype(BF16), done if shares else grad_query), BF16),
         loss_value,
         whole_rows(turned(grad_hidden).astype(BF16), F32),
-        grad_qkv_w[:, :nqw],
-        grad_qkv_w[:, nqw : nqw + nkw],
-        grad_qkv_w[:, nqw + nkw :],
-        grad_out,
-        joined(gate_near, gate_far, 1),
-        joined(up_near, up_far, 1),
-        joined(down_near, down_far, 0),
+        grad_query_w.astype(F32),
+        grad_kv_w[:, : nk * HD],
+        grad_kv_w[:, nk * HD :],
+        grad_out_w.astype(F32),
+        grad_gate_w,
+        grad_up_w,
+        grad_down_w,
         own_attn_gain,
         own_ffn_gain,
     )

time: 1180 us -> 844 us (0.72)
  waiting for transfers between devices: 710 us -> 241 us
  Pallas kernels: 41 us -> 332 us
  matrix products: 126 us -> 26.2 us
  other arithmetic: 104 us -> 68.3 us
  starting transfers between devices: 105 us -> 70.2 us
  local copies, waits for them, and re-layouts: 61 us -> 80 us
  blocking collectives: 16 us -> 0 us
    pallas_call x1 -> x16, Pallas kernels: 6.73 us -> 298 us  [the longest x4 151 us: grads_call(): pl.pallas_call(kernel, grid_spec=pltpu.PrefetchScalarGridSpec(num_scalar_...]
    ppermute x27 -> x11, waiting for transfers between devices: 306 us -> 18.2 us  [swap_ctx(): return lax.ppermute(a, 'ctx', [(i, i ^ mask) for i in range(count)])]
    ppermute x17 -> x20, waiting for transfers between devices: 214 us -> 93.8 us  [swap_x(): return lax.ppermute(a, 'fsdp', [(0, 1), (1, 0)])]
    ppermute x4 -> x6, waiting for transfers between devices: 65.7 us -> 8.91 us  [sum_ctx(): a = a + lax.ppermute(a, 'ctx', [(i, i ^ step) for i in range(count)])]
    dot_general x10 -> x5, matrix products: 51.9 us -> 10.6 us  [dot_nt(): lax.dot_general(a, b, (((1,), (1,)), ((), ())), preferred_element_type=F32)]
    ppermute x27 -> x11, starting transfers between devices: 57.8 us -> 17.2 us  [swap_ctx(): return lax.ppermute(a, 'ctx', [(i, i ^ mask) for i in range(count)])]
    ppermute x10, waiting for transfers between devices: 63.9 us -> 24.2 us  [swap_y(): return lax.ppermute(a, 'tp', [(0, 2), (2, 0), (1, 3), (3, 1)])]
    dot_general x7 -> x2, matrix products: 35.4 us -> 1.74 us  [dot(): return jnp.dot(a, b, preferred_element_type=F32).astype(out)]
  transfers between devices with their start and end apart: 78 -> 76, of which waited for: 38 -> 33; matrix products, arithmetic and copies ran while one was open for 18% -> 18% of each run, Pallas kernels for 2% -> 40%
where the time goes in v2:
time: 844 us; the launch traced here: 838 us
  Pallas kernels  332 us (39%)
  waiting for transfers between devices  241 us (29%)
  local copies, waits for them, and re-layouts  80 us (9%)
  starting transfers between devices  70.2 us (8%)
  other arithmetic  68.3 us (8%)
  matrix products  26.2 us (3%)
  between operations  19.6 us (2%)
    pallas_call x4, Pallas kernels, grads_call(): pl.pallas_call(kernel, grid_spec=pltpu.PrefetchScalarGridSpec(num_scalar_...  151 us
    ppermute x20, waiting for transfers between devices, swap_x(): return lax.ppermute(a, 'fsdp', [(0, 1), (1, 0)])  93.8 us
    pallas_call x2, Pallas kernels, all_up_call(): pl.pallas_call(all_up_kernel, grid_spec=pltpu.PrefetchScalarGridSpec(num_...  55.6 us
    ppermute x4, waiting for transfers between devices, swap_xy(): return lax.ppermute(a, ('fsdp', 'tp'), pairs)  53.3 us
    pallas_call x4, Pallas kernels, out_call(): pl.pallas_call(partial(out_kernel, n, contract, last), grid=(half // TILE...  37.2 us
    ppermute x3, waiting for transfers between devices, gather_ctx(): a = lax.ppermute(a, 'ctx', ring)  28.1 us
    unnamed x148, local copies, waits for them, and re-layouts  25.5 us
    pallas_call x2, Pallas kernels, up_call(): pl.pallas_call(partial(up_kernel, gathers), grid=(hidden // TILE,), in_sp...  24.7 us
  transfers between devices with their start and end apart: 76, of which 33 were waited for; matrix products, arithmetic and copies ran while one was open for 18% of the time, Pallas kernels for 40%

profile of v2, /device:TPU:0, one launch (start us, length us, event | category | flops | bytes accessed | tf_op | source)
XLA Modules:
  0.0 837.5 jit_solution(11908350934163452136)
XLA Ops:
  51.1 13.5 %collective-permute-done.10 = bf16[640,512]{1,0:T(8,128)(2,1)S(1)} collective-permute-done((bf16[640,512]{1,0:T(8,128)(2,1)}, bf16[640,512]{1,0:T(8,128)(2,1)S(1)}, u32[]{:S(2)}, u32[]{:S(2)}) %collective-permute-start.10) | collective-permute-done | bytes 655392 | tf_op jit(solution)/shard_map/ppermute | solution.py:597
  66.4 12.4 %collective-permute-done.11 = bf16[640,512]{1,0:T(8,128)(2,1)} collective-permute-done((bf16[640,512]{1,0:T(8,128)(2,1)S(1)}, bf16[640,512]{1,0:T(8,128)(2,1)}, u32[]{:S(2)}, u32[]{:S(2)}) %collective-permute-start.11) | collective-permute-done | bytes 655392 | tf_op jit(solution)/shard_map/ppermute | solution.py:597
  84.2 4.9 shard_map.239.q_ref
  95.6 12.4 %shard_map.240 = (bf16[640,512]{1,0:T(8,128)(2,1)}, f32[640,512]{1,0:T(8,128)}, f32[640,512]{1,0:T(8,128)}) custom-call(s32[40]{0:T(128)} %reshape.266.meta_ref, bf16[640,512]{1,0:T(8,128)(2,1)} %shard_map.239.q_ref, bf16[2560,512]{1,0:T(8,128)(2,1)} %copy-done, bf16[2560,512]{1,0:T(8,128)(2,1)} %copy-done), custom_call_target="tpu_custom_call" | custom-call | tf_op jit(solution)/shard_map/pallas_call | solution.py:187
  128.8 9.0 %collective-permute-done.15 = bf16[160,2048]{1,0:T(8,128)(2,1)S(1)} collective-permute-done((bf16[160,2048]{1,0:T(8,128)(2,1)S(1)}, bf16[160,2048]{1,0:T(8,128)(2,1)S(1)}, u32[]{:S(2)}, u32[]{:S(2)}) %collective-permute-start.15) | collective-permute-done | bytes 655392 | tf_op jit(solution)/shard_map/ppermute | solution.py:31
  139.6 11.5 %collective-permute-done.16.refs_11_.refs_9_.uf = bf16[1024,512]{1,0:T(8,128)(2,1)S(1)} collective-permute-done((bf16[1024,512]{1,0:T(8,128)(2,1)S(1)}, bf16[1024,512]{1,0:T(8,128)(2,1)S(1)}, u32[]{:S(2)}, u32[]{:S(2)}) %collective-permute-start.16) | collective-permute-done | bytes 1048608 | tf_op jit(solution)/shard_map/ppermute | solution.py:23
  157.8 19.2 %collective-permute-done.19.refs_2_ = bf16[160,2048]{1,0:T(8,128)(2,1)} collective-permute-done((bf16[160,2048]{1,0:T(8,128)(2,1)}, bf16[160,2048]{1,0:T(8,128)(2,1)}, u32[]{:S(2)}, u32[]{:S(2)}) %collective-permute-start.19) | collective-permute-done | bytes 655392 | tf_op jit(solution)/shard_map/ppermute | solution.py:23
  182.4 8.5 %collective-permute-done.20.refs_3_ = bf16[160,2048]{1,0:T(8,128)(2,1)S(1)} collective-permute-done((bf16[160,2048]{1,0:T(8,128)(2,1)}, bf16[160,2048]{1,0:T(8,128)(2,1)S(1)}, u32[]{:S(2)}, u32[]{:S(2)}) %collective-permute-start.20) | collective-permute-done | bytes 655392 | tf_op jit(solution)/shard_map/ppermute | solution.py:36
  197.5 13.2 %shard_map.241 = (f32[1280,512]{1,0:T(8,128)}, f32[1280,512]{1,0:T(8,128)}, bf16[1280,512]{1,0:T(8,128)(2,1)}, bf16[1280,2048]{1,0:T(8,128)(2,1)}) custom-call(bf16[160,2048]{1,0:T(8,128)(2,1)} %copy-done.6, bf16[160,2048]{1,0:T(8,128)(2,1)} %collective-permute-done.18.refs_1_, bf16[160,2048]{1,0:T(8,128)(2,1)} %collective-permute-done.19.refs_2_, ...), custom_call_target="tpu_custom_call" | custom-call | tf_op jit(solution)/shard_map/pallas_call | solution.py:346
  210.7 21.4 %collective-permute-done.25.refs_4_.refs_9_.df = bf16[512,1024]{1,0:T(8,128)(2,1)S(1)} collective-permute-done((bf16[512,1024]{1,0:T(8,128)(2,1)}, bf16[512,1024]{1,0:T(8,128)(2,1)S(1)}, u32[]{:S(2)}, u32[]{:S(2)}) %collective-permute-start.25) | collective-permute-done | bytes 1048608 | tf_op jit(solution)/shard_map/ppermute | solution.py:23
  233.1 11.5 %shard_map.242 = (f32[1280,512]{1,0:T(8,128)}, f32[1280,512]{1,0:T(8,128)}, bf16[1280,512]{1,0:T(8,128)(2,1)}) custom-call(bf16[1280,2048]{1,0:T(8,128)(2,1)} %get-tuple-element.100.refs_0_, bf16[1024,512]{1,0:T(8,128)(2,1)} %get-tuple-element.188.refs_1_.refs_6_.gn, bf16[1024,512]{1,0:T(8,128)(2,1)} %copy-done.14, ...), custom_call_target="tpu_custom_call" | custom-call | tf_op jit(solution)/shard_map/pallas_call | solution.py:346
  244.6 14.0 %collective-permute-done.27.refs_5_.refs_2_.df = bf16[512,1024]{1,0:T(8,128)(2,1)S(1)} collective-permute-done((bf16[512,1024]{1,0:T(8,128)(2,1)S(1)}, bf16[512,1024]{1,0:T(8,128)(2,1)S(1)}, u32[]{:S(2)}, u32[]{:S(2)}) %collective-permute-start.27) | collective-permute-done | bytes 1048608 | tf_op jit(solution)/shard_map/ppermute | solution.py:23
  259.5 7.2 shard_map.243
  266.7 5.1 collective-permute-done.28.refs_6_
  273.3 8.0 shard_map.244
  286.5 13.5 %collective-permute-done.29 = bf16[160,2048]{1,0:T(8,128)(2,1)S(1)} collective-permute-done((bf16[160,2048]{1,0:T(8,128)(2,1)}, bf16[160,2048]{1,0:T(8,128)(2,1)S(1)}, u32[]{:S(2)}, u32[]{:S(2)}) %collective-permute-start.29) | collective-permute-done | bytes 655392 | tf_op jit(solution)/shard_map/ppermute | solution.py:31
  304.1 13.8 %collective-permute-done.31 = bf16[160,2048]{1,0:T(8,128)(2,1)S(1)} collective-permute-done((bf16[160,2048]{1,0:T(8,128)(2,1)}, bf16[160,2048]{1,0:T(8,128)(2,1)S(1)}, u32[]{:S(2)}, u32[]{:S(2)}) %collective-permute-start.31) | collective-permute-done | bytes 655392 | tf_op jit(solution)/shard_map/ppermute | solution.py:36
  327.4 19.0 %collective-permute-done.33.refs_2_ = bf16[160,2048]{1,0:T(8,128)(2,1)S(1)} collective-permute-done((bf16[160,2048]{1,0:T(8,128)(2,1)}, bf16[160,2048]{1,0:T(8,128)(2,1)S(1)}, u32[]{:S(2)}, u32[]{:S(2)}) %collective-permute-start.33) | collective-permute-done | bytes 655392 | tf_op jit(solution)/shard_map/ppermute | solution.py:23
  346.4 13.9 %collective-permute-done.34.refs_3_ = bf16[160,2048]{1,0:T(8,128)(2,1)S(1)} collective-permute-done((bf16[160,2048]{1,0:T(8,128)(2,1)}, bf16[160,2048]{1,0:T(8,128)(2,1)S(1)}, u32[]{:S(2)}, u32[]{:S(2)}) %collective-permute-start.34) | collective-permute-done | bytes 655392 | tf_op jit(solution)/shard_map/ppermute | solution.py:36
  364.4 10.8 %shard_map.245 = (bf16[1280,512]{1,0:T(8,128)(2,1)}, bf16[1280,512]{1,0:T(8,128)(2,1)}, bf16[1280,2048]{1,0:T(8,128)(2,1)}) custom-call(bf16[160,2048]{1,0:T(8,128)(2,1)} %copy-done.7, bf16[160,2048]{1,0:T(8,128)(2,1)} %copy-done.49, bf16[160,2048]{1,0:T(8,128)(2,1)} %copy-done.47, bf16[160,2048]{1,0:T(8,128)(2,1)} %copy-done.48, ...), custom_call_target="tpu_custom_call" | custom-call | tf_op jit(solution)/shard_map/pallas_call | solution.py:385
  375.1 8.8 %shard_map.246 = (bf16[1280,512]{1,0:T(8,128)(2,1)}, bf16[1280,512]{1,0:T(8,128)(2,1)}) custom-call(bf16[1280,2048]{1,0:T(8,128)(2,1)} %get-tuple-element.112.refs_0_, bf16[512,1024]{1,0:T(8,128)(2,1)} %get-tuple-element.184.refs_3_.refs_1_.dn, bf16[512,1024]{1,0:T(8,128)(2,1)} %copy-done.11, f32[1280,512]{1,0:T(8,128)} %get-tuple-element.113.refs_3_, ...), custom_call_target="tpu_custom_call" | custom-call | tf_op jit(solution)/shard_map/pallas_call | solution.py:385
  383.9 10.6 %shard_map.247 = bf16[640,2048]{1,0:T(8,128)(2,1)} custom-call(bf16[1280,512]{1,0:T(8,128)(2,1)} %get-tuple-element.110.refs_0_, bf16[1280,512]{1,0:T(8,128)(2,1)} %get-tuple-element.111.refs_1_, bf16[1280,512]{1,0:T(8,128)(2,1)} %get-tuple-element.115.refs_2_, bf16[1280,512]{1,0:T(8,128)(2,1)} %get-tuple-element.116.refs_3_, ...), custom_call_target="tpu_custom_call" | custom-call | tf_op jit(solution)/shard_map/pallas_call | solution.py:450
  404.8 11.4 %shard_map.248 = (f32[160,2048]{1,0:T(8,128)}, bf16[160,2048]{1,0:T(8,128)(2,1)}, bf16[160,2048]{1,0:T(8,128)(2,1)}, bf16[160,2048]{1,0:T(8,128)(2,1)}) custom-call(bf16[1280,512]{1,0:T(8,128)(2,1)} %get-tuple-element.110.refs_0_, bf16[1280,512]{1,0:T(8,128)(2,1)} %get-tuple-element.111.refs_1_, bf16[1280,512]{1,0:T(8,128)(2,1)} %get-tuple-element.115.refs_2_, ...), custom_call_target="tpu_custom_call" | custom-call | tf_op jit(solution)/shard_map/pallas_call | solution.py:450
  419.8 27.7 %shard_map.249 = (f32[5120,512]{1,0:T(8,128)}, f32[5120,512]{1,0:T(8,128)}, bf16[5120,512]{1,0:T(8,128)(2,1)}) custom-call(s32[1]{0:T(128)} %bitcast.15.first_ref, bf16[5120,2048]{1,0:T(8,128)(2,1)} %all-gather.3.cloned.1.call-done.near_ref.far_ref.xf.xn, bf16[5120,2048]{1,0:T(8,128)(2,1)} %all-gather.3.cloned.1.call-done.near_ref.far_ref.xf.xn, ...), custom_call_target="tpu_custom_call" | custom-call | flops 21474836480 | tf_op jit(solution)/shard_map/pallas_call | solution.py:487
  448.8 17.2 %collective-permute-done.42 = bf16[160,2048]{1,0:T(8,128)(2,1)} collective-permute-done((bf16[160,2048]{1,0:T(8,128)(2,1)}, bf16[160,2048]{1,0:T(8,128)(2,1)}, u32[]{:S(2)}, u32[]{:S(2)}) %collective-permute-start.42) | collective-permute-done | bytes 655392 | tf_op jit(solution)/shard_map/ppermute | solution.py:36
  470.2 28.0 %shard_map.250 = (f32[5120,512]{1,0:T(8,128)}, f32[5120,512]{1,0:T(8,128)}, bf16[5120,512]{1,0:T(8,128)(2,1)}) custom-call(s32[1]{0:T(128)} %bitcast.15.first_ref, bf16[5120,2048]{1,0:T(8,128)(2,1)} %all-gather.3.cloned.1.call-done.near_ref.far_ref.xf.xn, bf16[5120,2048]{1,0:T(8,128)(2,1)} %all-gather.3.cloned.1.call-done.near_ref.far_ref.xf.xn, ...), custom_call_target="tpu_custom_call" | custom-call | flops 21474836480 | tf_op jit(solution)/shard_map/pallas_call | solution.py:487
  509.1 19.3 %shard_map.251 = (bf16[640,512]{1,0:T(8,128)(2,1)}, f32[2560,256]{1,0:T(8,128)}, f32[2560,256]{1,0:T(8,128)}) custom-call(s32[40]{0:T(128)} %reshape.266.meta_ref, bf16[640,512]{1,0:T(8,128)(2,1)} %shard_map.239.q_ref, bf16[2560,512]{1,0:T(8,128)(2,1)} %copy-done, bf16[2560,512]{1,0:T(8,128)(2,1)} %copy-done, f32[640,512]{1,0:T(8,128)} %bitcast_select_fusion.gc_ref, ...), custom_call_target="tpu_custom_call" | custom-call | tf_op jit(solution)/shard_map/pallas_call | solution.py:254
  537.1 46.3 %shard_map.252 = (bf16[3072,512]{1,0:T(8,128)(2,1)}, bf16[5120,512]{1,0:T(8,128)(2,1)}, bf16[5120,512]{1,0:T(8,128)(2,1)}) custom-call(s32[1]{0:T(128)} %bitcast.15.first_ref, bf16[5120,2048]{1,0:T(8,128)(2,1)} %all-gather.3.cloned.1.call-done.near_ref.far_ref.xf.xn, bf16[5120,2048]{1,0:T(8,128)(2,1)} %all-gather.5.cloned.1.call-done.gn.gf, ...), custom_call_target="tpu_custom_call" | custom-call | flops 26843545600 | tf_op jit(solution)/shard_map/pallas_call | solution.py:556
  631.2 46.5 %shard_map.254 = (bf16[3072,512]{1,0:T(8,128)(2,1)}, bf16[5120,512]{1,0:T(8,128)(2,1)}, bf16[5120,512]{1,0:T(8,128)(2,1)}) custom-call(s32[1]{0:T(128)} %bitcast.15.first_ref, bf16[5120,2048]{1,0:T(8,128)(2,1)} %all-gather.3.cloned.1.call-done.near_ref.far_ref.xf.xn, bf16[5120,2048]{1,0:T(8,128)(2,1)} %all-gather.5.cloned.1.call-done.gn.gf, ...), custom_call_target="tpu_custom_call" | custom-call | flops 26843545600 | tf_op jit(solution)/shard_map/pallas_call | solution.py:556
  685.3 29.1 %shard_map.255 = bf16[3072,512]{1,0:T(8,128)(2,1)} custom-call(s32[1]{0:T(128)} %bitcast.15.first_ref, bf16[5120,2048]{1,0:T(8,128)(2,1)} %all-gather.3.cloned.1.call-done.near_ref.far_ref.xf.xn, bf16[5120,2048]{1,0:T(8,128)(2,1)} %all-gather.5.cloned.1.call-done.gn.gf, bf16[5120,512]{1,0:T(8,128)(2,1)} %get-tuple-element.121.act_ref, ...), custom_call_target="tpu_custom_call" | custom-call | tf_op jit(solution)/shard_map/pallas_call | solution.py:556
  756.0 28.9 %shard_map.256 = bf16[3072,512]{1,0:T(8,128)(2,1)} custom-call(s32[1]{0:T(128)} %bitcast.15.first_ref, bf16[5120,2048]{1,0:T(8,128)(2,1)} %all-gather.3.cloned.1.call-done.near_ref.far_ref.xf.xn, bf16[5120,2048]{1,0:T(8,128)(2,1)} %all-gather.5.cloned.1.call-done.gn.gf, bf16[5120,512]{1,0:T(8,128)(2,1)} %get-tuple-element.129.act_ref, ...), custom_call_target="tpu_custom_call" | custom-call | tf_op jit(solution)/shard_map/pallas_call | solution.py:556
  805.7 14.0 %collective-permute-done.71 = bf16[256,512]{1,0:T(8,128)(2,1)S(1)} collective-permute-done((bf16[256,512]{1,0:T(8,128)(2,1)S(1)}, bf16[256,512]{1,0:T(8,128)(2,1)S(1)}, u32[]{:S(2)}, u32[]{:S(2)}) %collective-permute-start.71) | collective-permute-done | bytes 262176 | tf_op jit(solution)/shard_map/ppermute | solution.py:40
  (454 shorter events, 287.4 us)
Async XLA Ops:
  7.2 412.6 %all-gather.3.cloned.1.call-start = ((), (), s32[]{:S(2)}) async-start(), calls=%async_computation | async-start | bytes 21626880 | tf_op jit(solution)/shard_map/all_gather | solution.py:700
  12.5 29.6 %collective-permute-start = (bf16[2,1024]{1,0:T(2,128)(2,1)S(1)}, bf16[2,1024]{1,0:T(2,128)(2,1)S(1)}, u32[]{:S(2)}, u32[]{:S(2)}) collective-permute-start(bf16[2,1024]{1,0:T(2,128)(2,1)S(1)} %pad_maximum_fusion.12), channel_id=1, source_target_pairs={{0,16},{16,0},{1,17},{17,1},{2,18},{18,2},{3,19},{19,3},{4,20},{20... | collective-permute-start | bytes 12296 | tf_op jit(solution)/shard_map/ppermute | solution.py:23
  154.0 355.1 %all-gather.5.cloned.1.call-start = ((), (), s32[]{:S(2)}) async-start(), calls=%async_computation.1 | async-start | bytes 21626880 | tf_op jit(solution)/shard_map/all_gather | solution.py:700
  155.8 35.1 %collective-permute-start.20 = (bf16[160,2048]{1,0:T(8,128)(2,1)}, bf16[160,2048]{1,0:T(8,128)(2,1)S(1)}, u32[]{:S(2)}, u32[]{:S(2)}) collective-permute-start(bf16[160,2048]{1,0:T(8,128)(2,1)} %get-tuple-element.234), channel_id=1, source_target_pairs={{0,18},{1,19},{2,16},{3,17},{16,2},{17,3},{18,0},{19,1},{4,22},{5,... | collective-permute-start | bytes 1966088 | tf_op jit(solution)/shard_map/ppermute | solution.py:36
  156.2 36.5 %collective-permute-start.18 = (bf16[160,2048]{1,0:T(8,128)(2,1)S(1)}, bf16[160,2048]{1,0:T(8,128)(2,1)}, u32[]{:S(2)}, u32[]{:S(2)}) collective-permute-start(bf16[160,2048]{1,0:T(8,128)(2,1)S(1)} %multiply_convert_fusion.refs_0_), channel_id=1, source_target_pairs={{0,2},{2,0},{1,3},{3,1},{4,6},{6,4},{5,7},{7,5},{8,10},{10,8},{9,1... | collective-permute-start | bytes 1966088 | tf_op jit(solution)/shard_map/ppermute | solution.py:31
  157.8 36.4 %collective-permute-start.21 = (bf16[160,2048]{1,0:T(8,128)(2,1)S(1)}, bf16[160,2048]{1,0:T(8,128)(2,1)}, u32[]{:S(2)}, u32[]{:S(2)}) collective-permute-start(bf16[160,2048]{1,0:T(8,128)(2,1)S(1)} %multiply_convert_fusion.refs_0_), channel_id=1, source_target_pairs={{0,1},{1,0},{2,3},{3,2},{4,5},{5,4},{6,7},{7,6},{8,9},{9,8},{10,11... | collective-permute-start | bytes 1966088 | tf_op jit(solution)/shard_map/ppermute | solution.py:27
  180.9 51.2 %collective-permute-start.25 = (bf16[512,1024]{1,0:T(8,128)(2,1)}, bf16[512,1024]{1,0:T(8,128)(2,1)S(1)}, u32[]{:S(2)}, u32[]{:S(2)}) collective-permute-start(bf16[512,1024]{1,0:T(8,128)(2,1)} %get-tuple-element.99), channel_id=1, source_target_pairs={{0,16},{16,0},{1,17},{17,1},{2,18},{18,2},{3,19},{19,3},{4,20},{20... | collective-permute-start | bytes 3145736 | tf_op jit(solution)/shard_map/ppermute | solution.py:23
  190.9 41.2 %collective-permute-start.26 = (bf16[1024,512]{1,0:T(8,128)(2,1)S(1)}, bf16[1024,512]{1,0:T(8,128)(2,1)S(1)}, u32[]{:S(2)}, u32[]{:S(2)}) collective-permute-start(bf16[1024,512]{1,0:T(8,128)(2,1)S(1)} %copy-done.16), channel_id=1, source_target_pairs={{0,4},{4,0},{8,12},{12,8},{1,5},{5,1},{9,13},{13,9},{2,6},{6,2},{1... | collective-permute-start | bytes 3145736 | tf_op jit(solution)/shard_map/ppermute | solution.py:40
  192.7 65.8 %collective-permute-start.27 = (bf16[512,1024]{1,0:T(8,128)(2,1)S(1)}, bf16[512,1024]{1,0:T(8,128)(2,1)S(1)}, u32[]{:S(2)}, u32[]{:S(2)}) collective-permute-start(bf16[512,1024]{1,0:T(8,128)(2,1)S(1)} %get-tuple-element.102), channel_id=1, source_target_pairs={{0,16},{16,0},{1,17},{17,1},{2,18},{18,2},{3,19},{19,3},{4,20},{20... | collective-permute-start | bytes 3145736 | tf_op jit(solution)/shard_map/ppermute | solution.py:23
  283.9 34.0 %collective-permute-start.31 = (bf16[160,2048]{1,0:T(8,128)(2,1)}, bf16[160,2048]{1,0:T(8,128)(2,1)S(1)}, u32[]{:S(2)}, u32[]{:S(2)}) collective-permute-start(bf16[160,2048]{1,0:T(8,128)(2,1)} %get-tuple-element.106), channel_id=1, source_target_pairs={{0,18},{1,19},{2,16},{3,17},{16,2},{17,3},{18,0},{19,1},{4,22},{5,... | collective-permute-start | bytes 1966088 | tf_op jit(solution)/shard_map/ppermute | solution.py:36
  323.5 420.4 %all-reduce.3.cloned.1.call-start = ((), (), s32[]{:S(2)}) async-start(), calls=%async_computation.2 | async-start | bytes 4194304 | tf_op jit(solution)/shard_map/psum | solution.py:933
  325.2 35.1 %collective-permute-start.34 = (bf16[160,2048]{1,0:T(8,128)(2,1)}, bf16[160,2048]{1,0:T(8,128)(2,1)S(1)}, u32[]{:S(2)}, u32[]{:S(2)}) collective-permute-start(bf16[160,2048]{1,0:T(8,128)(2,1)} %get-tuple-element.232), channel_id=1, source_target_pairs={{0,18},{1,19},{2,16},{3,17},{16,2},{17,3},{18,0},{19,1},{4,22},{5,... | collective-permute-start | bytes 1966088 | tf_op jit(solution)/shard_map/ppermute | solution.py:36
  326.7 34.7 %collective-permute-start.32 = (bf16[160,2048]{1,0:T(8,128)(2,1)S(1)}, bf16[160,2048]{1,0:T(8,128)(2,1)S(1)}, u32[]{:S(2)}, u32[]{:S(2)}) collective-permute-start(bf16[160,2048]{1,0:T(8,128)(2,1)S(1)} %fusion.22.refs_0_), channel_id=1, source_target_pairs={{0,2},{2,0},{1,3},{3,1},{4,6},{6,4},{5,7},{7,5},{8,10},{10,8},{9,1... | collective-permute-start | bytes 1966088 | tf_op jit(solution)/shard_map/ppermute | solution.py:31
  327.4 34.0 %collective-permute-start.35 = (bf16[160,2048]{1,0:T(8,128)(2,1)S(1)}, bf16[160,2048]{1,0:T(8,128)(2,1)S(1)}, u32[]{:S(2)}, u32[]{:S(2)}) collective-permute-start(bf16[160,2048]{1,0:T(8,128)(2,1)S(1)} %fusion.22.refs_0_), channel_id=1, source_target_pairs={{0,1},{1,0},{2,3},{3,2},{4,5},{5,4},{6,7},{7,6},{8,9},{9,8},{10,11... | collective-permute-start | bytes 1966088 | tf_op jit(solution)/shard_map/ppermute | solution.py:27
  416.2 31.7 %collective-permute-start.40 = (bf16[160,2048]{1,0:T(8,128)(2,1)}, bf16[160,2048]{1,0:T(8,128)(2,1)S(1)}, u32[]{:S(2)}, u32[]{:S(2)}) collective-permute-start(bf16[160,2048]{1,0:T(8,128)(2,1)} %get-tuple-element.123), channel_id=1, source_target_pairs={{0,2},{2,0},{1,3},{3,1},{4,6},{6,4},{5,7},{7,5},{8,10},{10,8},{9,1... | collective-permute-start | bytes 1966088 | tf_op jit(solution)/shard_map/ppermute | solution.py:31
  416.9 31.9 %collective-permute-start.41 = (bf16[160,2048]{1,0:T(8,128)(2,1)}, bf16[160,2048]{1,0:T(8,128)(2,1)}, u32[]{:S(2)}, u32[]{:S(2)}) collective-permute-start(bf16[160,2048]{1,0:T(8,128)(2,1)} %get-tuple-element.124), channel_id=1, source_target_pairs={{0,16},{16,0},{1,17},{17,1},{2,18},{18,2},{3,19},{19,3},{4,20},{20... | collective-permute-start | bytes 1966088 | tf_op jit(solution)/shard_map/ppermute | solution.py:23
  418.3 47.8 %collective-permute-start.42 = (bf16[160,2048]{1,0:T(8,128)(2,1)}, bf16[160,2048]{1,0:T(8,128)(2,1)}, u32[]{:S(2)}, u32[]{:S(2)}) collective-permute-start(bf16[160,2048]{1,0:T(8,128)(2,1)} %get-tuple-element.125), channel_id=1, source_target_pairs={{0,18},{1,19},{2,16},{3,17},{16,2},{17,3},{18,0},{19,1},{4,22},{5,... | collective-permute-start | bytes 1966088 | tf_op jit(solution)/shard_map/ppermute | solution.py:36
  502.7 84.8 %collective-permute-start.55 = (bf16[512,1024]{1,0:T(8,128)(2,1)}, bf16[512,1024]{1,0:T(8,128)(2,1)}, u32[]{:S(2)}, u32[]{:S(2)}) collective-permute-start(bf16[512,1024]{1,0:T(8,128)(2,1)} %convolution_convert_fusion.2), channel_id=1, source_target_pairs={{0,16},{16,0},{1,17},{17,1},{2,18},{18,2},{3,19},{19,3},{4,20},{20... | collective-permute-start | bytes 3145736 | tf_op jit(solution)/shard_map/ppermute | solution.py:23
  532.7 59.0 %collective-permute-start.49 = (bf16[640,512]{1,0:T(8,128)(2,1)}, bf16[640,512]{1,0:T(8,128)(2,1)}, u32[]{:S(2)}, u32[]{:S(2)}) collective-permute-start(bf16[640,512]{1,0:T(8,128)(2,1)} %get-tuple-element.178), channel_id=1, source_target_pairs={{0,12},{4,8},{8,4},{12,0},{1,13},{5,9},{9,5},{13,1},{2,14},{6,10},... | collective-permute-start | bytes 1966088 | tf_op jit(solution)/shard_map/ppermute | solution.py:40
  536.4 56.8 %collective-permute-start.50 = (bf16[640,512]{1,0:T(8,128)(2,1)}, bf16[640,512]{1,0:T(8,128)(2,1)}, u32[]{:S(2)}, u32[]{:S(2)}) collective-permute-start(bf16[640,512]{1,0:T(8,128)(2,1)} %get-tuple-element.180), channel_id=1, source_target_pairs={{0,8},{4,12},{8,0},{12,4},{1,9},{5,13},{9,1},{13,5},{2,10},{6,14},... | collective-permute-start | bytes 1966088 | tf_op jit(solution)/shard_map/ppermute | solution.py:40
  536.4 56.8 %collective-permute-start.51 = (bf16[640,512]{1,0:T(8,128)(2,1)}, bf16[640,512]{1,0:T(8,128)(2,1)}, u32[]{:S(2)}, u32[]{:S(2)}) collective-permute-start(bf16[640,512]{1,0:T(8,128)(2,1)} %get-tuple-element.179), channel_id=1, source_target_pairs={{0,4},{4,0},{8,12},{12,8},{1,5},{5,1},{9,13},{13,9},{2,6},{6,2},{1... | collective-permute-start | bytes 1966088 | tf_op jit(solution)/shard_map/ppermute | solution.py:40
  583.4 30.6 %collective-permute-start.46 = (bf16[160,2048]{1,0:T(8,128)(2,1)}, bf16[160,2048]{1,0:T(8,128)(2,1)}, u32[]{:S(2)}, u32[]{:S(2)}) collective-permute-start(bf16[160,2048]{1,0:T(8,128)(2,1)} %fusion.12), channel_id=1, source_target_pairs={{0,1},{1,0},{2,3},{3,2},{4,5},{5,4},{6,7},{7,6},{8,9},{9,8},{10,11... | collective-permute-start | bytes 1966088 | tf_op jit(solution)/shard_map/ppermute | solution.py:27
  608.9 139.5 %collective-permute-start.66 = (bf16[1024,512]{1,0:T(8,128)(2,1)}, bf16[1024,512]{1,0:T(8,128)(2,1)}, u32[]{:S(2)}, u32[]{:S(2)}) collective-permute-start(bf16[1024,512]{1,0:T(8,128)(2,1)} %convolution_convert_fusion.1), channel_id=1, source_target_pairs={{0,16},{16,0},{1,17},{17,1},{2,18},{18,2},{3,19},{19,3},{4,20},{20... | collective-permute-start | bytes 3145736 | tf_op jit(solution)/shard_map/ppermute | solution.py:23
  620.6 127.8 %collective-permute-start.65 = (bf16[3072,512]{1,0:T(8,128)(2,1)}, bf16[3072,512]{1,0:T(8,128)(2,1)}, u32[]{:S(2)}, u32[]{:S(2)}) collective-permute-start(bf16[3072,512]{1,0:T(8,128)(2,1)} %get-tuple-element.148), channel_id=1, source_target_pairs={{0,16},{16,0},{1,17},{17,1},{2,18},{18,2},{3,19},{19,3},{4,20},{20... | collective-permute-start | bytes 9437192 | tf_op jit(solution)/shard_map/ppermute | solution.py:23
  629.6 48.0 %collective-permute-start.53 = (bf16[160,2048]{1,0:T(8,128)(2,1)}, bf16[160,2048]{1,0:T(8,128)(2,1)S(1)}, u32[]{:S(2)}, u32[]{:S(2)}) collective-permute-start(bf16[160,2048]{1,0:T(8,128)(2,1)} %slice.406), channel_id=1, source_target_pairs={{0,2},{2,0},{1,3},{3,1},{4,6},{6,4},{5,7},{7,5},{8,10},{10,8},{9,1... | collective-permute-start | bytes 1966088 | tf_op jit(solution)/shard_map/ppermute | solution.py:31
  683.8 56.5 %collective-permute-start.62 = (bf16[160,2048]{1,0:T(8,128)(2,1)S(1)}, bf16[160,2048]{1,0:T(8,128)(2,1)S(1)}, u32[]{:S(2)}, u32[]{:S(2)}) collective-permute-start(bf16[160,2048]{1,0:T(8,128)(2,1)S(1)} %get-tuple-element.167), channel_id=1, source_target_pairs={{0,1},{1,0},{2,3},{3,2},{4,5},{5,4},{6,7},{7,6},{8,9},{9,8},{10,11... | collective-permute-start | bytes 1966088 | tf_op jit(solution)/shard_map/ppermute | solution.py:27
  683.8 56.4 %collective-permute-start.63 = (bf16[160,2048]{1,0:T(8,128)(2,1)S(1)}, bf16[160,2048]{1,0:T(8,128)(2,1)S(1)}, u32[]{:S(2)}, u32[]{:S(2)}) collective-permute-start(bf16[160,2048]{1,0:T(8,128)(2,1)S(1)} %get-tuple-element.167), channel_id=1, source_target_pairs={{0,2},{2,0},{1,3},{3,1},{4,6},{6,4},{5,7},{7,5},{8,10},{10,8},{9,1... | collective-permute-start | bytes 1966088 | tf_op jit(solution)/shard_map/ppermute | solution.py:31
  685.0 35.5 %collective-permute-start.56 = (f32[1,4224]{1,0:T(1,128)S(1)}, f32[1,4224]{1,0:T(1,128)S(1)}, u32[]{:S(2)}, u32[]{:S(2)}) collective-permute-start(f32[1,4224]{1,0:T(1,128)S(1)} %reshape.273), channel_id=1, source_target_pairs={{0,1},{1,0},{2,3},{3,2},{4,5},{5,4},{6,7},{7,6},{8,9},{9,8},{10,11... | collective-permute-start | bytes 50696 | tf_op jit(solution)/shard_map/ppermute | solution.py:27
  739.7 81.6 %collective-permute-start.60 = (bf16[3072,512]{1,0:T(8,128)(2,1)}, bf16[3072,512]{1,0:T(8,128)(2,1)S(1)}, u32[]{:S(2)}, u32[]{:S(2)}) collective-permute-start(bf16[3072,512]{1,0:T(8,128)(2,1)} %get-tuple-element.144), channel_id=1, source_target_pairs={{0,16},{16,0},{1,17},{17,1},{2,18},{18,2},{3,19},{19,3},{4,20},{20... | collective-permute-start | bytes 9437192 | tf_op jit(solution)/shard_map/ppermute | solution.py:23
  751.7 41.5 %collective-permute-start.67 = (bf16[256,512]{1,0:T(8,128)(2,1)}, bf16[256,512]{1,0:T(8,128)(2,1)S(1)}, u32[]{:S(2)}, u32[]{:S(2)}) collective-permute-start(bf16[256,512]{1,0:T(8,128)(2,1)} %get-tuple-element.226), channel_id=1, source_target_pairs={{0,12},{4,8},{8,4},{12,0},{1,13},{5,9},{9,5},{13,1},{2,14},{6,10},... | collective-permute-start | bytes 786440 | tf_op jit(solution)/shard_map/ppermute | solution.py:40
  753.2 40.0 %collective-permute-start.68 = (bf16[256,512]{1,0:T(8,128)(2,1)}, bf16[256,512]{1,0:T(8,128)(2,1)}, u32[]{:S(2)}, u32[]{:S(2)}) collective-permute-start(bf16[256,512]{1,0:T(8,128)(2,1)} %get-tuple-element.228), channel_id=1, source_target_pairs={{0,8},{4,12},{8,0},{12,4},{1,9},{5,13},{9,1},{13,5},{2,10},{6,14},... | collective-permute-start | bytes 786440 | tf_op jit(solution)/shard_map/ppermute | solution.py:40
  755.1 38.1 %collective-permute-start.69 = (bf16[256,512]{1,0:T(8,128)(2,1)}, bf16[256,512]{1,0:T(8,128)(2,1)}, u32[]{:S(2)}, u32[]{:S(2)}) collective-permute-start(bf16[256,512]{1,0:T(8,128)(2,1)} %get-tuple-element.227), channel_id=1, source_target_pairs={{0,4},{4,0},{8,12},{12,8},{1,5},{5,1},{9,13},{13,9},{2,6},{6,2},{1... | collective-permute-start | bytes 786440 | tf_op jit(solution)/shard_map/ppermute | solution.py:40
  (114 other events, 1484.7 us)
Sparse Core Ops, SparseCore 0:
  154.1 166.9 all-gather.2
  323.9 155.1 all-gather.4
  631.3 86.3 all-reduce.2

commit v3 on v2

--- a/solution.py
+++ b/solution.py
@@ -17,6 +17,11 @@
 BF16 = jnp.bfloat16
 VMEM_LIMIT = 56 * 1024 * 1024
 BIG = 1 << 30
+CFG = {'farcost': 1, 'a_qfar': 1, 'a_out': 1, 'kv_q': 1, 'x_kv': 1, 'b_y': 1, 'b_q': 1, 'kv_late': 1, 'n_p': 1, 's_last': 1, 'w_near': 1, 'o_q': 1, 'o_ffn': 1, 'o_near': 1, 'ow_near': 1, 'c_all': 1, 'early': 1, 'e_after': 1, 'e_hook': 1, 'e_up': 1, 'e_go': 1, 'e_gp': 1}
+
+
+def on(name, *values):
+    return values if CFG.get(name) else ()
 
 
 def swap_x(a):
@@ -496,7 +501,9 @@
         compiler_params=pltpu.CompilerParams(vmem_limit_bytes=VMEM_LIMIT),
         cost_estimate=pl.CostEstimate(
             flops=4 * tokens * width * hidden, bytes_accessed=0, transcendentals=0
-        ),
+        )
+        if CFG.get('upcost')
+        else None,
     )(first, x, x, *weights)
 
 
@@ -537,12 +544,16 @@
         put_sums(far_ref, *sums)
 
 
-def near_grads_kernel(first_ref, xn, gn, act_ref, gg_ref, gu_ref, near_ref, *sums):
-    add_sums(sums, gg_ref[...], gu_ref[...], act_ref[...], xn[...], gn[...])
+def near_grads_kernel(first_ref, xn, gn, *refs):
+    tiles, outs, sums = refs[:6], refs[6:8], refs[8:]
+    for k in range(2):
+        act, gg, gu = (ref[...] for ref in tiles[3 * k : 3 * k + 3])
+        add_sums(sums[3 * k : 3 * k + 3], gg, gu, act, xn[...], gn[...])
 
     @pl.when(pl.program_id(0) == pl.num_programs(0) - 1)
     def _():
-        put_sums(near_ref, *sums)
+        for k in range(2):
+            put_sums(outs[k], *sums[3 * k : 3 * k + 3])
 
 
 def grads_call(kernel, first, wides, fixeds, tiles, size, outs, products):
@@ -576,12 +587,71 @@
 
 def far_grads_call(first, x, g, size, weights, forward):
     wides = [(x, False), (g, True), (g, False)]
-    return grads_call(far_grads_kernel, first, wides, weights, forward, size, 2, 5)
-
-
-def near_grads_call(first, x, g, size, act, back):
-    wides = [(x, True), (g, True)]
-    return grads_call(near_grads_kernel, first, wides, (), (act, *back), size, 0, None)[0]
+    return grads_call(far_grads_kernel, first, wides, weights, forward, size, 2, 5 if CFG.get('farcost') else None)
+
+
+def near_grads_call(first, x, g, size, tiles):
+    tokens, width = x.shape
+    half = width // 2
+    depth = tiles[0].shape[1]
+    near, _ = halves_of_rows(size, width)
+    tile = pl.BlockSpec((size, depth), lambda i, f: (i, 0))
+    shape = (3 * half, depth)
+    return pl.pallas_call(
+        near_grads_kernel,
+        grid_spec=pltpu.PrefetchScalarGridSpec(
+            num_scalar_prefetch=1,
+            grid=(tokens // size,),
+            in_specs=[near, near] + [tile] * 6,
+            out_specs=[fixed(shape)] * 2,
+            scratch_shapes=[pltpu.VMEM((depth, half), F32)] * 6,
+        ),
+        out_shape=[jax.ShapeDtypeStruct(shape, BF16)] * 2,
+        compiler_params=pltpu.CompilerParams(vmem_limit_bytes=VMEM_LIMIT),
+        cost_estimate=pl.CostEstimate(
+            flops=6 * tokens * width * depth, bytes_accessed=0, transcendentals=0
+        )
+        if CFG.get('nearcost')
+        else None,
+    )(first, x, g, *tiles)
+
+
+def place_kernel(at_ref, gate, up, left, right, *refs):
+    gate_ref, up_ref, down_ref = refs[-3:]
+    size = left.shape[1]
+    gate_ref[...] = gate[...].astype(F32)
+    up_ref[...] = up[...].astype(F32)
+    down_ref[:, :size] = left[...].astype(F32)
+    down_ref[:, size:] = right[...].astype(F32)
+
+
+def place_call(at, block, so_far=()):
+    half, depth = block.shape[0] // 3, block.shape[1]
+    tall, flat = half // 4, depth // 4
+    anywhere = pl.BlockSpec(memory_space=pl.ANY)
+    shapes = [(half, 4 * depth)] * 2 + [(4 * depth, half)]
+    return pl.pallas_call(
+        place_kernel,
+        grid_spec=pltpu.PrefetchScalarGridSpec(
+            num_scalar_prefetch=1,
+            grid=(4,),
+            in_specs=[
+                pl.BlockSpec((tall, depth), lambda i, w: (i, 0)),
+                pl.BlockSpec((tall, depth), lambda i, w: (4 + i, 0)),
+                pl.BlockSpec((flat, depth), lambda i, w: (2 * half // flat + i, 0)),
+                pl.BlockSpec((flat, depth), lambda i, w: ((2 * half + depth) // flat + i, 0)),
+            ]
+            + [anywhere] * len(so_far),
+            out_specs=[
+                pl.BlockSpec((tall, depth), lambda i, w: (i, w[0])),
+                pl.BlockSpec((tall, depth), lambda i, w: (i, w[0])),
+                pl.BlockSpec((flat, half), lambda i, w: (4 * w[0] + i, 0)),
+            ],
+        ),
+        out_shape=[jax.ShapeDtypeStruct(shape, F32) for shape in shapes],
+        input_output_aliases={5 + k: k for k in range(len(so_far))},
+        compiler_params=pltpu.CompilerParams(vmem_limit_bytes=VMEM_LIMIT),
+    )(at.reshape(1), block, block, block, block, *so_far)
 
 
 def gather_ctx(a, count, c):
@@ -622,19 +692,21 @@
     return lax.psum(a, "ctx").astype(F32)
 
 
-def sum_planes(a, count, c):
-    if count != 4:
-        return lax.psum(a, "ctx")
+def share_sums(a, count, c, *meanwhile):
     rows = a.shape[0] // count
 
     def share(index):
         return lax.dynamic_slice_in_dim(a, index * rows, rows, axis=0)
 
-    total = share(c).astype(F32)
+    total = after(share(c).astype(F32), *meanwhile)
     for d in (3, 2, 1):
         total = total + swap_ctx(share(c ^ d), count, d).astype(F32)
-    total = total.astype(BF16)
-    out = jnp.zeros_like(a)
+    return total.astype(BF16)
+
+
+def shares_back(total, count, c, *meanwhile):
+    rows = total.shape[0]
+    out = after(jnp.zeros((rows * count, total.shape[1]), total.dtype), *meanwhile)
     for d in (3, 2, 1, 0):
         block = swap_ctx(total, count, d) if d else total
         out = lax.dynamic_update_slice_in_dim(out, block, (c ^ d) * rows, axis=0)
@@ -693,7 +765,8 @@
 
     def gather_plane(x):
         flipped = halves_swapped(x)
-        group = [x, swap_y(x), swap_x(flipped), swap_xy(flipped)]
+        over_x = swap_x(flipped)
+        group = [x, swap_y(x), over_x, swap_y(over_x) if CFG.get('e_relay') else swap_xy(flipped)]
         return group + [swap_core(a) for a in group]
 
     def gather_all(x):
@@ -723,19 +796,23 @@
     far_query = swap_x(after(w_query, far_key, far_value))
     far_out = swap_x(after(w_out, far_query))
 
+    sends = []
+
     def exchanged(w, axis, share, *behind):
         def cut(index, which):
             return lax.dynamic_slice_in_dim(w, index * eighth + which * part, part, axis=axis)
 
-        got = swap_x(after(cut(1 - f, parity), *behind))
+        sends.append(cut(1 - f, parity))
+        got = swap_x(after(sends[-1], *behind))
         if not share:
-            other = swap_x(after(cut(1 - f, 1 - parity), *behind))
+            sends.append(cut(1 - f, 1 - parity))
+            other = swap_x(after(sends[-1], *behind))
         else:
             other = swap_ctx(got, count, 1)
         return (cut(f, parity), got), (cut(f, 1 - parity), other)
 
     gate_p, gate_o = exchanged(w_gate, 1, True, far_out)
-    up_p, up_o = exchanged(w_up, 1, True, gate_p[1])
+    up_p, up_o = exchanged(w_up, 1, True, far_out if CFG.get('e_two') else gate_p[1])
 
     labels = jnp.arange(parents.shape[0], dtype=jnp.int32)
     seg = segment_ids[::BLK]
@@ -775,6 +852,7 @@
     normed = rms_scale(hidden.astype(F32), gain_attn).astype(BF16)
     near_normed, far_normed = normed[:, :half], normed[:, half:]
     normed_in, meta, valid_count = lax.optimization_barrier((normed, meta, valid_count))
+    normed_in = after(normed_in, *on('early', *sends))
     kv = proj_call(
         normed_in, cosine, sine, (True, False), (w_key, far_key, w_value, far_value)
     )
@@ -784,18 +862,18 @@
         (query, jnp.concatenate([w_out, far_out], axis=1))
     )
     attended, context, total = fwd_call(meta, query_in, kv_all, nk, unit, trunk)
-    attended = after(reordered(attended), gate_p[1])
+    attended = after(reordered(attended), *on('e_gp', gate_p[1]))
     kept, to_y = halves_tp(lambda a: dot(a, out_full), attended)
     attn_out = kept + swap_y(to_y).astype(F32)
 
     hidden_own = own_rows(hidden).astype(F32)
     middle = hidden_own + attn_out
-    normed_own = after(rms_scale(middle, gain_ffn).astype(BF16), up_p[1], gate_o[1])
+    normed_own = after(rms_scale(middle, gain_ffn).astype(BF16), *on('e_up', up_p[1]), *on('e_go', gate_o[1]))
     normed_pieces = gather_plane(normed_own)
-    down_p, down_o = exchanged(w_down, 0, False, normed_pieces[2])
+    down_p, down_o = exchanged(w_down, 0, bool(CFG.get('e_share')), *on('e_after', normed_pieces[2]), *on('e_after2', normed_pieces[3]), up_p[1])
     *act_p, normed_ffn = up_call(normed_pieces, *gate_p, *up_p)
     shares = count == 4
-    normed_ffn = after(normed_ffn, down_p[1])
+    normed_ffn = after(normed_ffn, *on('e_hook', down_p[1]), *on('e_hook2', up_o[1]))
     act_o = list(up_call([normed_ffn], *gate_o, *up_o))
     output_f = middle + scatter_sum(
         scatter_out([act_p[2], act_o[2]], [down_p[0], down_o[0]], [down_p[1], down_o[1]], 0)
@@ -811,7 +889,7 @@
     grad_own = grad_output.astype(BF16)
     grad_pieces = gather_plane(grad_own)
     if shares:
-        normed_all, grad_all = gather_all(normed_own), gather_all(grad_own)
+        normed_all, grad_all = gather_all(after(normed_own, *on('e_ag', normed_pieces[3]), *on('e_ag2', down_p[1]))), gather_all(grad_own)
         place = f.reshape(1)
     gg_p, gu_p, grad_ffn = act_back_call(grad_pieces, *down_p, act_p[0], act_p[1])
     gg_o, gu_o = act_back_call([grad_ffn], *down_o, act_o[0], act_o[1])
@@ -843,34 +921,27 @@
 
     grad_attn = gather_tp(grad_middle.astype(BF16))
     if shares:
-        ahead_o = all_up_call(after(place, grad_middle), normed_all, rows, (*gate_o, *up_o))
-        grad_attn[0] = after(grad_attn[0], *ahead_o)
+        if not CFG.get('ahead_late'):
+            ahead_o = all_up_call(after(place, grad_middle), normed_all, rows, (*gate_o, *up_o))
+            grad_attn[0] = after(grad_attn[0], *ahead_o)
     grad_attn = jnp.concatenate(grad_attn, axis=0)
     out_sent = swap_x(dot_tn(attended, grad_attn[:, half:], BF16))
     out_kept = dot_tn(attended, grad_attn[:, :half])
     grad_context = reordered(dot_nt(grad_attn, out_full))
-    if shares:
+    if shares and CFG.get('c_all'):
         grad_context, grad_all = lax.optimization_barrier((grad_context, grad_all))
     grad_query, key_terms, value_terms = bwd_call(
         meta, query, kv_all, grad_context, context, total, cosine, sine, nk, unit, trunk
     )
-    def query_weights():
-        sent = swap_x(dot_tn(far_normed, grad_query, BF16))
-        return sent, dot_tn(near_normed, grad_query)
-
-    query_sent, query_kept = query_weights()
+    query_far = dot_tn(far_normed, grad_query, BF16)
+    query_sent, query_kept = swap_x(query_far), dot_tn(near_normed, grad_query)
+    out_kept = after(out_kept, grad_query)
+    out_part = (out_kept + out_sent.astype(F32)).astype(BF16)
     if shares:
-        blocks = [[], [], []]
-
-        def keep(near, far, which):
-            for side, index in ((near, f), (far, 1 - f)):
-                gate, up, down = (side[k * half : (k + 1) * half] for k in range(3))
-                blocks[0].append((gate, index, which))
-                blocks[1].append((up, index, which))
-                down = jnp.concatenate([down[:part], down[part:]], axis=1)
-                blocks[2].append((down, index, which))
-
-        place = after(place, grad_query)
+        place = after(place, grad_query, *on('a_qfar', query_far), *on('a_qkept', query_kept), *on('a_out', out_part), *on('a_qsent', query_sent))
+        if CFG.get('ahead_late'):
+            ahead_o = all_up_call(place, normed_all, rows, (*gate_o, *up_o))
+            place = after(place, *ahead_o)
         done, *back_p = far_grads_call(place, normed_all, grad_all, rows, down_p, ahead_p)
     else:
 
@@ -896,14 +967,13 @@
 
     kv_sums = scatter_ctx(jnp.concatenate([key_terms, value_terms], axis=1), count, c)
     if shares:
-        kv_sums = after(kv_sums, done)
+        kv_sums = after(kv_sums, done, *on('kv_q', query_sent))
     grad_kv = dkv_call(kv_sums, cosine, sine, nk)
-    kv_sent = dot_tn(far_normed, grad_kv, BF16)
-    kv_sent = swap_x(kv_sent)
-    kv_kept = dot_tn(near_normed, grad_kv)
-    out_kept = after(out_kept, grad_query)
+    kv_far = dot_tn(far_normed, grad_kv, BF16)
+    kv_sent, kv_kept = swap_x(kv_far), dot_tn(near_normed, grad_kv)
     query_part = (query_kept + query_sent.astype(F32)).astype(BF16)
-    out_part = (out_kept + out_sent.astype(F32)).astype(BF16)
+    kv_part = None if CFG.get('kv_late') and shares else (kv_kept + kv_sent.astype(F32)).astype(BF16)
+    grad_query_w, grad_out_w = lax.psum((query_part, out_part), "ctx")
     nears = jnp.concatenate([w_query, w_key, w_value], axis=1)
     fars = jnp.concatenate([far_query, far_key, far_value], axis=1)
     kept, to_y = halves_tp(
@@ -911,51 +981,68 @@
         reordered(jnp.concatenate([grad_query, grad_kv], axis=1)),
     )
     if shares:
-        over_p = swap_x(after(done, query_sent))
-        place = after(place, done, to_y, kv_kept, query_part, out_part)
+        over_p = swap_x(after(done, *on('x_kv', kv_far), *on('x_q', query_sent)))
+        place = after(place, done, *on('b_y', to_y), *on('b_q', query_part), *on('b_kv', kv_part), *on('b_kvkept', kv_kept), *on('b_out', out_part))
         far, *back_o = far_grads_call(place, normed_all, grad_all, rows, down_o, ahead_o)
         over_o = swap_x(far)
         over_y = swap_y(to_y)
-        over_y, place = lax.optimization_barrier((over_y, after(place, far)))
-        near = near_grads_call(place, normed_all, grad_all, rows, ahead_p[2], back_p)
-        first_near = near
-        kv_kept, over_p, place = lax.optimization_barrier(
-            (kv_kept, over_p, after(place, near))
+        place = after(place, far)
+        if CFG.get('kv_late'):
+            kv_part = (after(kv_kept, far) + kv_sent.astype(F32)).astype(BF16)
+            place = after(place, *on('n_kv', kv_part))
+        else:
+            kv_shares = share_sums(kv_part, count, c, far)
+            place = after(place, *on('n_kv', kv_shares))
+        place = after(place, *on('n_y', over_y), *on('n_p', over_p))
+        near_p, near_o = near_grads_call(
+            place, normed_all, grad_all, 2 * rows, (ahead_p[2], *back_p, ahead_o[2], *back_o)
         )
-        near = near_grads_call(place, normed_all, grad_all, rows, ahead_o[2], back_o)
-        keep(first_near, over_p, parity)
-        keep(near, over_o, 1 - parity)
-        grad_gate_w, grad_up_w, grad_down_w = (
-            joined(b, axis) for b, axis in zip(blocks, (1, 1, 0))
+        meanwhile = (near_p,)
+        weights = place_call(2 * (1 - f) + parity, over_p)
+        weights = place_call(2 * f + parity, near_p, weights)
+        weights = place_call(2 * f + 1 - parity, near_o, weights)
+        grad_gate_w, grad_up_w, grad_down_w = place_call(
+            2 * (1 - f) + 1 - parity, over_o, weights
         )
     else:
+        meanwhile = ()
         over_y = swap_y(to_y)
-    grad_query_w, grad_out_w = lax.psum((query_part, out_part), "ctx")
-    grad_kv_w = sum_planes((kv_kept + kv_sent.astype(F32)).astype(BF16), count, c).astype(F32)
+    if shares:
+        if CFG.get('kv_late'):
+            kv_shares = share_sums(kv_part, count, c, *meanwhile, *on('s_ar', grad_query_w, grad_out_w))
+            grad_kv_w = gather_ctx(kv_shares, count, c).astype(F32)
+        else:
+            grad_kv_w = shares_back(kv_shares, count, c, *meanwhile, *on('s_ar', grad_query_w, grad_out_w)).astype(F32)
+    else:
+        grad_kv_w = line_sum(kv_part)
     grad_normed = kept + over_y.astype(F32)
     _, norm_attn_back = jax.vjp(rms_scale, hidden_own, gain_attn)
     grad_hidden_part, grad_attn_gain = norm_attn_back(grad_normed)
-    grad_hidden = grad_middle + grad_hidden_part
-
-    def whole_rows(x, kind):
+    grad_hidden = after(grad_middle, *on('h_near', *meanwhile)) + grad_hidden_part
+
+    def whole_rows(x, kind, *behind):
+        pair = after(jnp.concatenate([x, swap_y(x)], axis=0), *behind)
         out = jnp.zeros((rows, width), kind)
-        for j, block in enumerate(gather_tp(x)):
-            out = lax.dynamic_update_slice_in_dim(
-                out, block.astype(kind), (t ^ j) * quarter, axis=0
-            )
+        for k, blocks in enumerate((pair, swap_core(pair))):
+            for y in range(2):
+                block = blocks[y * quarter : (y + 1) * quarter].astype(kind)
+                out = lax.dynamic_update_slice_in_dim(
+                    out, block, (t ^ (2 * y + k)) * quarter, axis=0
+                )
         return out
 
     small = jnp.concatenate(
         [turned(grad_attn_gain), turned(grad_ffn_gain), jnp.full((HD,), error_sum, F32)]
     ).reshape(1, -1)
-    small = sum_all(small, count, *((over_o,) if shares else ()))[0]
+    small = after(small, *on('s_near', *meanwhile))
+    small = sum_all(small, count, *(on('s_last', over_o) if shares else ()))[0]
     loss_value = small[2 * width] / valid_count
     own_attn_gain = lax.dynamic_slice_in_dim(small[:width], f * half, half)
     own_ffn_gain = lax.dynamic_slice_in_dim(small[width : 2 * width], f * half, half)
     return (
-        whole_rows(after(turned(output_f).astype(BF16), done if shares else grad_query), BF16),
+        whole_rows(after(turned(output_f).astype(BF16), *on('o_q', grad_query), *on('o_ffn', grad_ffn), *(on('o_done', done) if shares else ()), *on('o_near', *meanwhile)), BF16, *on('ow_near', *meanwhile)),
         loss_value,
-        whole_rows(turned(grad_hidden).astype(BF16), F32),
+        whole_rows(turned(grad_hidden).astype(BF16), F32, *on('w_near', *meanwhile)),
         grad_query_w.astype(F32),
         grad_kv_w[:, : nk * HD],
         grad_kv_w[:, nk * HD :],

time: 844 us -> 832 us (0.986)
  local copies, waits for them, and re-layouts: 80 us -> 66.4 us
  Pallas kernels: 332 us -> 343 us
  other arithmetic: 68.3 us -> 59.1 us
  waiting for transfers between devices: 241 us -> 232 us
    pallas_call x0 -> x5, Pallas kernels: none -> 68.6 us  [the longest x1 49 us: near_grads_call(): pl.pallas_call(near_grads_kernel, grid_spec=pltpu.PrefetchScalarGridSpec(...]
    pallas_call x4 -> x2, Pallas kernels: 151 us -> 92.8 us  [grads_call(): pl.pallas_call(kernel, grid_spec=pltpu.PrefetchScalarGridSpec(num_scalar_...]
    ppermute x20, waiting for transfers between devices: 93.8 us -> 67.4 us  [swap_x(): return lax.ppermute(a, 'fsdp', [(0, 1), (1, 0)])]
    ppermute x10, waiting for transfers between devices: 24.2 us -> 49.8 us  [swap_y(): return lax.ppermute(a, 'tp', [(0, 2), (2, 0), (1, 3), (3, 1)])]
    ppermute x11 -> x8, waiting for transfers between devices: 18.2 us -> 0.06 us  [swap_ctx(): return lax.ppermute(a, 'ctx', [(i, i ^ mask) for i in range(count)])]
    dynamic_update_slice x13 -> x5, other arithmetic: 24 us -> 9.99 us  [the longest x4 9.14 us: whole_rows(): lax.dynamic_update_slice_in_dim(out, block, (t ^ 2 * y + k) * quarter, ax...]
    ppermute x3 -> x6, waiting for transfers between devices: 28.1 us -> 37.7 us  [gather_ctx(): a = lax.ppermute(a, 'ctx', ring)]
    another operation x5 -> x3, local copies, waits for them, and re-layouts: 8.91 us -> 0.01 us
  transfers between devices with their start and end apart: 76 -> 74, of which waited for: 33 -> 33; matrix products, arithmetic and copies ran while one was open for 18% -> 14% of each run, Pallas kernels for 40% -> 41%
where the time goes in v3:
time: 832 us; the launch traced here: 824 us
  Pallas kernels  343 us (41%)
  waiting for transfers between devices  232 us (28%)
  starting transfers between devices  77.9 us (9%)
  local copies, waits for them, and re-layouts  66.4 us (8%)
  other arithmetic  59.1 us (7%)
  matrix products  25.9 us (3%)
  between operations  19.7 us (2%)
    pallas_call x2, Pallas kernels, grads_call(): pl.pallas_call(kernel, grid_spec=pltpu.PrefetchScalarGridSpec(num_scalar_...  92.8 us
    ppermute x20, waiting for transfers between devices, swap_x(): return lax.ppermute(a, 'fsdp', [(0, 1), (1, 0)])  67.4 us
    pallas_call x2, Pallas kernels, all_up_call(): pl.pallas_call(all_up_kernel, grid_spec=pltpu.PrefetchScalarGridSpec(num_...  55.6 us
    ppermute x10, waiting for transfers between devices, swap_y(): return lax.ppermute(a, 'tp', [(0, 2), (2, 0), (1, 3), (3, 1)])  49.8 us
    pallas_call x1, Pallas kernels, near_grads_call(): pl.pallas_call(near_grads_kernel, grid_spec=pltpu.PrefetchScalarGridSpec(...  49 us
    ppermute x4, waiting for transfers between devices, swap_xy(): return lax.ppermute(a, ('fsdp', 'tp'), pairs)  46.9 us
    ppermute x6, waiting for transfers between devices, gather_ctx(): a = lax.ppermute(a, 'ctx', ring)  37.7 us
    pallas_call x4, Pallas kernels, out_call(): pl.pallas_call(partial(out_kernel, n, contract, last), grid=(half // TILE...  37.5 us
  transfers between devices with their start and end apart: 74, of which 33 were waited for; matrix products, arithmetic and copies ran while one was open for 14% of the time, Pallas kernels for 41%

profile of v3, /device:TPU:0, one launch (start us, length us, event | category | flops | bytes accessed | tf_op | source)
XLA Modules:
  0.0 824.1 jit_solution(16858527966229732239)
XLA Ops:
  55.6 14.7 %collective-permute-done.10 = bf16[640,512]{1,0:T(8,128)(2,1)S(1)} collective-permute-done((bf16[640,512]{1,0:T(8,128)(2,1)}, bf16[640,512]{1,0:T(8,128)(2,1)S(1)}, u32[]{:S(2)}, u32[]{:S(2)}) %collective-permute-start.10) | collective-permute-done | bytes 655392 | tf_op jit(solution)/shard_map/ppermute | solution.py:667
  71.8 12.9 %collective-permute-done.11 = bf16[640,512]{1,0:T(8,128)(2,1)S(1)} collective-permute-done((bf16[640,512]{1,0:T(8,128)(2,1)S(1)}, bf16[640,512]{1,0:T(8,128)(2,1)S(1)}, u32[]{:S(2)}, u32[]{:S(2)}) %collective-permute-start.11) | collective-permute-done | bytes 655392 | tf_op jit(solution)/shard_map/ppermute | solution.py:667
  90.5 6.3 collective-permute-done.12
  100.9 12.4 %shard_map.240 = (bf16[640,512]{1,0:T(8,128)(2,1)}, f32[640,512]{1,0:T(8,128)}, f32[640,512]{1,0:T(8,128)}) custom-call(s32[40]{0:T(128)} %reshape.278.meta_ref, bf16[640,512]{1,0:T(8,128)(2,1)} %shard_map.239.q_ref, bf16[2560,512]{1,0:T(8,128)(2,1)} %copy-done, bf16[2560,512]{1,0:T(8,128)(2,1)} %copy-done), custom_call_target="tpu_custom_call" | custom-call | tf_op jit(solution)/shard_map/pallas_call | solution.py:192
  126.7 14.7 %collective-permute-done.15 = bf16[160,2048]{1,0:T(8,128)(2,1)S(1)} collective-permute-done((bf16[160,2048]{1,0:T(8,128)(2,1)S(1)}, bf16[160,2048]{1,0:T(8,128)(2,1)S(1)}, u32[]{:S(2)}, u32[]{:S(2)}) %collective-permute-start.15) | collective-permute-done | bytes 655392 | tf_op jit(solution)/shard_map/ppermute | solution.py:36
  143.5 7.8 collective-permute-done.16.refs_11_.refs_9_.uf
  158.5 15.9 %collective-permute-done.18.refs_1_ = bf16[160,2048]{1,0:T(8,128)(2,1)S(1)} collective-permute-done((bf16[160,2048]{1,0:T(8,128)(2,1)S(1)}, bf16[160,2048]{1,0:T(8,128)(2,1)S(1)}, u32[]{:S(2)}, u32[]{:S(2)}) %collective-permute-start.18) | collective-permute-done | bytes 655392 | tf_op jit(solution)/shard_map/ppermute | solution.py:36
  180.1 16.0 %collective-permute-done.20.refs_3_ = bf16[160,2048]{1,0:T(8,128)(2,1)} collective-permute-done((bf16[160,2048]{1,0:T(8,128)(2,1)}, bf16[160,2048]{1,0:T(8,128)(2,1)}, u32[]{:S(2)}, u32[]{:S(2)}) %collective-permute-start.20) | collective-permute-done | bytes 655392 | tf_op jit(solution)/shard_map/ppermute | solution.py:41
  202.2 13.3 %shard_map.241 = (f32[1280,512]{1,0:T(8,128)}, f32[1280,512]{1,0:T(8,128)}, bf16[1280,512]{1,0:T(8,128)(2,1)}, bf16[1280,2048]{1,0:T(8,128)(2,1)}) custom-call(bf16[160,2048]{1,0:T(8,128)(2,1)} %copy-done.10, bf16[160,2048]{1,0:T(8,128)(2,1)} %copy-done.49, bf16[160,2048]{1,0:T(8,128)(2,1)} %collective-permute-done.19.refs_2_, ...), custom_call_target="tpu_custom_call" | custom-call | tf_op jit(solution)/shard_map/pallas_call | solution.py:351
  215.5 17.8 %collective-permute-done.25.refs_4_.refs_9_.df = bf16[512,1024]{1,0:T(8,128)(2,1)S(1)} collective-permute-done((bf16[512,1024]{1,0:T(8,128)(2,1)}, bf16[512,1024]{1,0:T(8,128)(2,1)S(1)}, u32[]{:S(2)}, u32[]{:S(2)}) %collective-permute-start.25) | collective-permute-done | bytes 1048608 | tf_op jit(solution)/shard_map/ppermute | solution.py:28
  234.3 11.8 %shard_map.242 = (f32[1280,512]{1,0:T(8,128)}, f32[1280,512]{1,0:T(8,128)}, bf16[1280,512]{1,0:T(8,128)(2,1)}) custom-call(bf16[1280,2048]{1,0:T(8,128)(2,1)} %get-tuple-element.115.refs_0_, bf16[1024,512]{1,0:T(8,128)(2,1)} %get-tuple-element.216.refs_1_.refs_6_.gn, bf16[1024,512]{1,0:T(8,128)(2,1)} %copy-done.6, ...), custom_call_target="tpu_custom_call" | custom-call | tf_op jit(solution)/shard_map/pallas_call | solution.py:351
  246.1 17.0 %collective-permute-done.27.refs_5_.refs_2_.df = bf16[512,1024]{1,0:T(8,128)(2,1)S(1)} collective-permute-done((bf16[512,1024]{1,0:T(8,128)(2,1)S(1)}, bf16[512,1024]{1,0:T(8,128)(2,1)S(1)}, u32[]{:S(2)}, u32[]{:S(2)}) %collective-permute-start.27) | collective-permute-done | bytes 1048608 | tf_op jit(solution)/shard_map/ppermute | solution.py:28
  264.2 7.2 shard_map.243
  271.4 5.1 collective-permute-done.28.refs_6_
  278.0 8.0 shard_map.244
  290.8 15.2 %collective-permute-done.31 = bf16[160,2048]{1,0:T(8,128)(2,1)S(1)} collective-permute-done((bf16[160,2048]{1,0:T(8,128)(2,1)}, bf16[160,2048]{1,0:T(8,128)(2,1)S(1)}, u32[]{:S(2)}, u32[]{:S(2)}) %collective-permute-start.31) | collective-permute-done | bytes 655392 | tf_op jit(solution)/shard_map/ppermute | solution.py:41
  306.0 12.9 %collective-permute-done.30 = bf16[160,2048]{1,0:T(8,128)(2,1)S(1)} collective-permute-done((bf16[160,2048]{1,0:T(8,128)(2,1)}, bf16[160,2048]{1,0:T(8,128)(2,1)S(1)}, u32[]{:S(2)}, u32[]{:S(2)}) %collective-permute-start.30) | collective-permute-done | bytes 655392 | tf_op jit(solution)/shard_map/ppermute | solution.py:28
  328.3 17.7 %collective-permute-done.32.refs_1_ = bf16[160,2048]{1,0:T(8,128)(2,1)S(1)} collective-permute-done((bf16[160,2048]{1,0:T(8,128)(2,1)S(1)}, bf16[160,2048]{1,0:T(8,128)(2,1)S(1)}, u32[]{:S(2)}, u32[]{:S(2)}) %collective-permute-start.32) | collective-permute-done | bytes 655392 | tf_op jit(solution)/shard_map/ppermute | solution.py:36
  348.9 15.6 %collective-permute-done.34.refs_3_ = bf16[160,2048]{1,0:T(8,128)(2,1)S(1)} collective-permute-done((bf16[160,2048]{1,0:T(8,128)(2,1)}, bf16[160,2048]{1,0:T(8,128)(2,1)S(1)}, u32[]{:S(2)}, u32[]{:S(2)}) %collective-permute-start.34) | collective-permute-done | bytes 655392 | tf_op jit(solution)/shard_map/ppermute | solution.py:41
  367.5 10.7 %shard_map.245 = (bf16[1280,512]{1,0:T(8,128)(2,1)}, bf16[1280,512]{1,0:T(8,128)(2,1)}, bf16[1280,2048]{1,0:T(8,128)(2,1)}) custom-call(bf16[160,2048]{1,0:T(8,128)(2,1)} %copy-done.13, bf16[160,2048]{1,0:T(8,128)(2,1)} %copy-done.50, bf16[160,2048]{1,0:T(8,128)(2,1)} %copy-done.51, bf16[160,2048]{1,0:T(8,128)(2,1)} %copy-done.52, ...), custom_call_target="tpu_custom_call" | custom-call | tf_op jit(solution)/shard_map/pallas_call | solution.py:390
  378.2 8.8 %shard_map.246 = (bf16[1280,512]{1,0:T(8,128)(2,1)}, bf16[1280,512]{1,0:T(8,128)(2,1)}) custom-call(bf16[1280,2048]{1,0:T(8,128)(2,1)} %get-tuple-element.127.refs_0_, bf16[512,1024]{1,0:T(8,128)(2,1)} %get-tuple-element.212.refs_3_.refs_1_.dn, bf16[512,1024]{1,0:T(8,128)(2,1)} %copy-done.16, f32[1280,512]{1,0:T(8,128)} %get-tuple-element.128.refs_3_, ...), custom_call_target="tpu_custom_call" | custom-call | tf_op jit(solution)/shard_map/pallas_call | solution.py:390
  387.0 10.9 %shard_map.247 = bf16[640,2048]{1,0:T(8,128)(2,1)} custom-call(bf16[1280,512]{1,0:T(8,128)(2,1)} %get-tuple-element.125.refs_0_, bf16[1280,512]{1,0:T(8,128)(2,1)} %get-tuple-element.126.refs_1_, bf16[1280,512]{1,0:T(8,128)(2,1)} %get-tuple-element.130.refs_2_, bf16[1280,512]{1,0:T(8,128)(2,1)} %get-tuple-element.131.refs_3_, ...), custom_call_target="tpu_custom_call" | custom-call | tf_op jit(solution)/shard_map/pallas_call | solution.py:455
  400.4 6.2 collective-permute-done.39.refs_12_
  408.2 11.5 %shard_map.248 = (f32[160,2048]{1,0:T(8,128)}, bf16[160,2048]{1,0:T(8,128)(2,1)}, bf16[160,2048]{1,0:T(8,128)(2,1)}, bf16[160,2048]{1,0:T(8,128)(2,1)}) custom-call(bf16[1280,512]{1,0:T(8,128)(2,1)} %get-tuple-element.125.refs_0_, bf16[1280,512]{1,0:T(8,128)(2,1)} %get-tuple-element.126.refs_1_, bf16[1280,512]{1,0:T(8,128)(2,1)} %get-tuple-element.130.refs_2_, ...), custom_call_target="tpu_custom_call" | custom-call | tf_op jit(solution)/shard_map/pallas_call | solution.py:455
  429.1 27.7 %shard_map.249 = (f32[5120,512]{1,0:T(8,128)}, f32[5120,512]{1,0:T(8,128)}, bf16[5120,512]{1,0:T(8,128)(2,1)}) custom-call(s32[1]{0:T(128)} %bitcast.15.first_ref, bf16[5120,2048]{1,0:T(8,128)(2,1)} %all-gather.3.cloned.1.call-done.near_ref.far_ref.xf.xn, bf16[5120,2048]{1,0:T(8,128)(2,1)} %all-gather.3.cloned.1.call-done.near_ref.far_ref.xf.xn, ...), custom_call_target="tpu_custom_call" | custom-call | tf_op jit(solution)/shard_map/pallas_call | solution.py:492
  456.8 6.9 collective-permute-done.41
  469.9 27.9 %shard_map.250 = (f32[5120,512]{1,0:T(8,128)}, f32[5120,512]{1,0:T(8,128)}, bf16[5120,512]{1,0:T(8,128)(2,1)}) custom-call(s32[1]{0:T(128)} %bitcast.15.first_ref, bf16[5120,2048]{1,0:T(8,128)(2,1)} %all-gather.3.cloned.1.call-done.near_ref.far_ref.xf.xn, bf16[5120,2048]{1,0:T(8,128)(2,1)} %all-gather.3.cloned.1.call-done.near_ref.far_ref.xf.xn, ...), custom_call_target="tpu_custom_call" | custom-call | tf_op jit(solution)/shard_map/pallas_call | solution.py:492
  507.6 19.5 %shard_map.251 = (bf16[640,512]{1,0:T(8,128)(2,1)}, f32[2560,256]{1,0:T(8,128)}, f32[2560,256]{1,0:T(8,128)}) custom-call(s32[40]{0:T(128)} %reshape.278.meta_ref, bf16[640,512]{1,0:T(8,128)(2,1)} %shard_map.239.q_ref, bf16[2560,512]{1,0:T(8,128)(2,1)} %copy-done, bf16[2560,512]{1,0:T(8,128)(2,1)} %copy-done, f32[640,512]{1,0:T(8,128)} %bitcast_select_fusion.gc_ref, ...), custom_call_target="tpu_custom_call" | custom-call | tf_op jit(solution)/shard_map/pallas_call | solution.py:259
  543.6 46.3 %shard_map.252 = (bf16[3072,512]{1,0:T(8,128)(2,1)}, bf16[5120,512]{1,0:T(8,128)(2,1)}, bf16[5120,512]{1,0:T(8,128)(2,1)}) custom-call(s32[1]{0:T(128)} %bitcast.15.first_ref, bf16[5120,2048]{1,0:T(8,128)(2,1)} %all-gather.3.cloned.1.call-done.near_ref.far_ref.xf.xn, bf16[5120,2048]{1,0:T(8,128)(2,1)} %all-gather.5.cloned.1.call-done.gn.gf, ...), custom_call_target="tpu_custom_call" | custom-call | flops 26843545600 | tf_op jit(solution)/shard_map/pallas_call | solution.py:567
  621.4 46.5 %shard_map.254 = (bf16[3072,512]{1,0:T(8,128)(2,1)}, bf16[5120,512]{1,0:T(8,128)(2,1)}, bf16[5120,512]{1,0:T(8,128)(2,1)}) custom-call(s32[1]{0:T(128)} %bitcast.15.first_ref, bf16[5120,2048]{1,0:T(8,128)(2,1)} %all-gather.3.cloned.1.call-done.near_ref.far_ref.xf.xn, bf16[5120,2048]{1,0:T(8,128)(2,1)} %all-gather.5.cloned.1.call-done.gn.gf, ...), custom_call_target="tpu_custom_call" | custom-call | flops 26843545600 | tf_op jit(solution)/shard_map/pallas_call | solution.py:567
  675.8 10.6 %collective-permute-start.58 = (f32[1,4224]{1,0:T(1,128)S(1)}, f32[1,4224]{1,0:T(1,128)S(1)}, u32[]{:S(2)}, u32[]{:S(2)}) collective-permute-start(f32[1,4224]{1,0:T(1,128)S(1)} %add.340), channel_id=1, source_target_pairs={{0,4},{4,0},{8,12},{12,8},{1,5},{5,1},{9,13},{13,9},{2,6},{6,2},{1... | collective-permute-start | bytes 50696 | tf_op jit(solution)/shard_map/ppermute | solution.py:726
  700.6 49.0 %shard_map.255 = (bf16[3072,512]{1,0:T(8,128)(2,1)}, bf16[3072,512]{1,0:T(8,128)(2,1)}) custom-call(s32[1]{0:T(128)} %bitcast.15.first_ref, bf16[5120,2048]{1,0:T(8,128)(2,1)} %all-gather.3.cloned.1.call-done.near_ref.far_ref.xf.xn, bf16[5120,2048]{1,0:T(8,128)(2,1)} %all-gather.5.cloned.1.call-done.gn.gf, ...), custom_call_target="tpu_custom_call" | custom-call | tf_op jit(solution)/shard_map/pallas_call | solution.py:600
  (441 shorter events, 279.8 us)
Async XLA Ops:
  7.2 421.9 %all-gather.3.cloned.1.call-start = ((), (), s32[]{:S(2)}) async-start(), calls=%async_computation | async-start | bytes 21626880 | tf_op jit(solution)/shard_map/all_gather | solution.py:773
  8.6 37.9 %collective-permute-start = (bf16[2,1024]{1,0:T(2,128)(2,1)S(1)}, bf16[2,1024]{1,0:T(2,128)(2,1)S(1)}, u32[]{:S(2)}, u32[]{:S(2)}) collective-permute-start(bf16[2,1024]{1,0:T(2,128)(2,1)S(1)} %pad_maximum_fusion.14), channel_id=1, source_target_pairs={{0,16},{16,0},{1,17},{17,1},{2,18},{18,2},{3,19},{19,3},{4,20},{20... | collective-permute-start | bytes 12296 | tf_op jit(solution)/shard_map/ppermute | solution.py:28
  15.9 30.7 %collective-permute-start.6 = (bf16[1024,256]{1,0:T(8,128)(2,1)}, bf16[1024,256]{1,0:T(8,128)(2,1)S(1)}, u32[]{:S(2)}, u32[]{:S(2)}) collective-permute-start(bf16[1024,256]{1,0:T(8,128)(2,1)} %refs_0_.2), channel_id=1, source_target_pairs={{0,16},{16,0},{1,17},{17,1},{2,18},{18,2},{3,19},{19,3},{4,20},{20... | collective-permute-start | bytes 1572872 | tf_op jit(solution)/shard_map/ppermute | solution.py:28
  153.8 353.8 %all-gather.5.cloned.1.call-start = ((), (), s32[]{:S(2)}) async-start(), calls=%async_computation.1 | async-start | bytes 21626880 | tf_op jit(solution)/shard_map/all_gather | solution.py:773
  156.7 39.4 %collective-permute-start.20 = (bf16[160,2048]{1,0:T(8,128)(2,1)}, bf16[160,2048]{1,0:T(8,128)(2,1)}, u32[]{:S(2)}, u32[]{:S(2)}) collective-permute-start(bf16[160,2048]{1,0:T(8,128)(2,1)} %pad_maximum_fusion.9), channel_id=1, source_target_pairs={{0,18},{1,19},{2,16},{3,17},{16,2},{17,3},{18,0},{19,1},{4,22},{5,... | collective-permute-start | bytes 1966088 | tf_op jit(solution)/shard_map/ppermute | solution.py:41
  158.5 39.6 %collective-permute-start.21 = (bf16[160,2048]{1,0:T(8,128)(2,1)S(1)}, bf16[160,2048]{1,0:T(8,128)(2,1)}, u32[]{:S(2)}, u32[]{:S(2)}) collective-permute-start(bf16[160,2048]{1,0:T(8,128)(2,1)S(1)} %multiply_convert_fusion.refs_0_), channel_id=1, source_target_pairs={{0,1},{1,0},{2,3},{3,2},{4,5},{5,4},{6,7},{7,6},{8,9},{9,8},{10,11... | collective-permute-start | bytes 1966088 | tf_op jit(solution)/shard_map/ppermute | solution.py:32
  178.5 54.8 %collective-permute-start.25 = (bf16[512,1024]{1,0:T(8,128)(2,1)}, bf16[512,1024]{1,0:T(8,128)(2,1)S(1)}, u32[]{:S(2)}, u32[]{:S(2)}) collective-permute-start(bf16[512,1024]{1,0:T(8,128)(2,1)} %get-tuple-element.114), channel_id=1, source_target_pairs={{0,16},{16,0},{1,17},{17,1},{2,18},{18,2},{3,19},{19,3},{4,20},{20... | collective-permute-start | bytes 3145736 | tf_op jit(solution)/shard_map/ppermute | solution.py:28
  179.8 53.5 %collective-permute-start.26 = (bf16[1024,512]{1,0:T(8,128)(2,1)S(1)}, bf16[1024,512]{1,0:T(8,128)(2,1)S(1)}, u32[]{:S(2)}, u32[]{:S(2)}) collective-permute-start(bf16[1024,512]{1,0:T(8,128)(2,1)S(1)} %copy-done.8), channel_id=1, source_target_pairs={{0,4},{4,0},{8,12},{12,8},{1,5},{5,1},{9,13},{13,9},{2,6},{6,2},{1... | collective-permute-start | bytes 3145736 | tf_op jit(solution)/shard_map/ppermute | solution.py:45
  196.2 67.0 %collective-permute-start.27 = (bf16[512,1024]{1,0:T(8,128)(2,1)S(1)}, bf16[512,1024]{1,0:T(8,128)(2,1)S(1)}, u32[]{:S(2)}, u32[]{:S(2)}) collective-permute-start(bf16[512,1024]{1,0:T(8,128)(2,1)S(1)} %get-tuple-element.117), channel_id=1, source_target_pairs={{0,16},{16,0},{1,17},{17,1},{2,18},{18,2},{3,19},{19,3},{4,20},{20... | collective-permute-start | bytes 3145736 | tf_op jit(solution)/shard_map/ppermute | solution.py:28
  288.9 30.0 %collective-permute-start.30 = (bf16[160,2048]{1,0:T(8,128)(2,1)}, bf16[160,2048]{1,0:T(8,128)(2,1)S(1)}, u32[]{:S(2)}, u32[]{:S(2)}) collective-permute-start(bf16[160,2048]{1,0:T(8,128)(2,1)} %get-tuple-element.120), channel_id=1, source_target_pairs={{0,16},{16,0},{1,17},{17,1},{2,18},{18,2},{3,19},{19,3},{4,20},{20... | collective-permute-start | bytes 1966088 | tf_op jit(solution)/shard_map/ppermute | solution.py:28
  289.0 30.0 %collective-permute-start.29 = (bf16[160,2048]{1,0:T(8,128)(2,1)}, bf16[160,2048]{1,0:T(8,128)(2,1)S(1)}, u32[]{:S(2)}, u32[]{:S(2)}) collective-permute-start(bf16[160,2048]{1,0:T(8,128)(2,1)} %get-tuple-element.119), channel_id=1, source_target_pairs={{0,2},{2,0},{1,3},{3,1},{4,6},{6,4},{5,7},{7,5},{8,10},{10,8},{9,1... | collective-permute-start | bytes 1966088 | tf_op jit(solution)/shard_map/ppermute | solution.py:36
  324.5 456.3 %all-reduce.3.cloned.1.call-start = ((), (), s32[]{:S(2)}) async-start(), calls=%async_computation.2 | async-start | bytes 4194304 | tf_op jit(solution)/shard_map/psum | solution.py:976
  327.3 37.2 %collective-permute-start.34 = (bf16[160,2048]{1,0:T(8,128)(2,1)}, bf16[160,2048]{1,0:T(8,128)(2,1)S(1)}, u32[]{:S(2)}, u32[]{:S(2)}) collective-permute-start(bf16[160,2048]{1,0:T(8,128)(2,1)} %get-tuple-element.247), channel_id=1, source_target_pairs={{0,18},{1,19},{2,16},{3,17},{16,2},{17,3},{18,0},{19,1},{4,22},{5,... | collective-permute-start | bytes 1966088 | tf_op jit(solution)/shard_map/ppermute | solution.py:41
  328.3 36.2 %collective-permute-start.35 = (bf16[160,2048]{1,0:T(8,128)(2,1)S(1)}, bf16[160,2048]{1,0:T(8,128)(2,1)S(1)}, u32[]{:S(2)}, u32[]{:S(2)}) collective-permute-start(bf16[160,2048]{1,0:T(8,128)(2,1)S(1)} %fusion.22.refs_0_), channel_id=1, source_target_pairs={{0,1},{1,0},{2,3},{3,2},{4,5},{5,4},{6,7},{7,6},{8,9},{9,8},{10,11... | collective-permute-start | bytes 1966088 | tf_op jit(solution)/shard_map/ppermute | solution.py:32
  419.7 37.1 %collective-permute-start.42 = (bf16[160,2048]{1,0:T(8,128)(2,1)}, bf16[160,2048]{1,0:T(8,128)(2,1)}, u32[]{:S(2)}, u32[]{:S(2)}) collective-permute-start(bf16[160,2048]{1,0:T(8,128)(2,1)} %get-tuple-element.140), channel_id=1, source_target_pairs={{0,18},{1,19},{2,16},{3,17},{16,2},{17,3},{18,0},{19,1},{4,22},{5,... | collective-permute-start | bytes 1966088 | tf_op jit(solution)/shard_map/ppermute | solution.py:41
  422.2 41.4 %collective-permute-start.41 = (bf16[160,2048]{1,0:T(8,128)(2,1)}, bf16[160,2048]{1,0:T(8,128)(2,1)}, u32[]{:S(2)}, u32[]{:S(2)}) collective-permute-start(bf16[160,2048]{1,0:T(8,128)(2,1)} %get-tuple-element.139), channel_id=1, source_target_pairs={{0,16},{16,0},{1,17},{17,1},{2,18},{18,2},{3,19},{19,3},{4,20},{20... | collective-permute-start | bytes 1966088 | tf_op jit(solution)/shard_map/ppermute | solution.py:28
  422.9 40.8 %collective-permute-start.40 = (bf16[160,2048]{1,0:T(8,128)(2,1)}, bf16[160,2048]{1,0:T(8,128)(2,1)}, u32[]{:S(2)}, u32[]{:S(2)}) collective-permute-start(bf16[160,2048]{1,0:T(8,128)(2,1)} %get-tuple-element.138), channel_id=1, source_target_pairs={{0,2},{2,0},{1,3},{3,1},{4,6},{6,4},{5,7},{7,5},{8,10},{10,8},{9,1... | collective-permute-start | bytes 1966088 | tf_op jit(solution)/shard_map/ppermute | solution.py:36
  467.5 30.4 %collective-permute-start.44 = (bf16[160,2048]{1,0:T(8,128)(2,1)S(1)}, bf16[160,2048]{1,0:T(8,128)(2,1)S(1)}, u32[]{:S(2)}, u32[]{:S(2)}) collective-permute-start(bf16[160,2048]{1,0:T(8,128)(2,1)S(1)} %get-tuple-element.145), channel_id=1, source_target_pairs={{0,2},{2,0},{1,3},{3,1},{4,6},{6,4},{5,7},{7,5},{8,10},{10,8},{9,1... | collective-permute-start | bytes 1966088 | tf_op jit(solution)/shard_map/ppermute | solution.py:36
  502.6 29.3 %collective-permute-start.46 = (bf16[512,1024]{1,0:T(8,128)(2,1)}, bf16[512,1024]{1,0:T(8,128)(2,1)}, u32[]{:S(2)}, u32[]{:S(2)}) collective-permute-start(bf16[512,1024]{1,0:T(8,128)(2,1)} %convolution_convert_fusion.2), channel_id=1, source_target_pairs={{0,16},{16,0},{1,17},{17,1},{2,18},{18,2},{3,19},{19,3},{4,20},{20... | collective-permute-start | bytes 3145736 | tf_op jit(solution)/shard_map/ppermute | solution.py:28
  530.1 62.6 %collective-permute-start.50 = (bf16[1024,512]{1,0:T(8,128)(2,1)}, bf16[1024,512]{1,0:T(8,128)(2,1)}, u32[]{:S(2)}, u32[]{:S(2)}) collective-permute-start(bf16[1024,512]{1,0:T(8,128)(2,1)} %convolution_convert_fusion.3), channel_id=1, source_target_pairs={{0,16},{16,0},{1,17},{17,1},{2,18},{18,2},{3,19},{19,3},{4,20},{20... | collective-permute-start | bytes 3145736 | tf_op jit(solution)/shard_map/ppermute | solution.py:28
  539.2 50.8 %collective-permute-start.49 = (bf16[640,512]{1,0:T(8,128)(2,1)S(1)}, bf16[640,512]{1,0:T(8,128)(2,1)S(1)}, u32[]{:S(2)}, u32[]{:S(2)}) collective-permute-start(bf16[640,512]{1,0:T(8,128)(2,1)S(1)} %get-tuple-element.207), channel_id=1, source_target_pairs={{0,4},{4,0},{8,12},{12,8},{1,5},{5,1},{9,13},{13,9},{2,6},{6,2},{1... | collective-permute-start | bytes 1966088 | tf_op jit(solution)/shard_map/ppermute | solution.py:45
  540.7 49.3 %collective-permute-start.48 = (bf16[640,512]{1,0:T(8,128)(2,1)S(1)}, bf16[640,512]{1,0:T(8,128)(2,1)S(1)}, u32[]{:S(2)}, u32[]{:S(2)}) collective-permute-start(bf16[640,512]{1,0:T(8,128)(2,1)S(1)} %get-tuple-element.208), channel_id=1, source_target_pairs={{0,8},{4,12},{8,0},{12,4},{1,9},{5,13},{9,1},{13,5},{2,10},{6,14},... | collective-permute-start | bytes 1966088 | tf_op jit(solution)/shard_map/ppermute | solution.py:45
  543.4 46.6 %collective-permute-start.47 = (bf16[640,512]{1,0:T(8,128)(2,1)S(1)}, bf16[640,512]{1,0:T(8,128)(2,1)S(1)}, u32[]{:S(2)}, u32[]{:S(2)}) collective-permute-start(bf16[640,512]{1,0:T(8,128)(2,1)S(1)} %get-tuple-element.206), channel_id=1, source_target_pairs={{0,12},{4,8},{8,4},{12,0},{1,13},{5,9},{9,5},{13,1},{2,14},{6,10},... | collective-permute-start | bytes 1966088 | tf_op jit(solution)/shard_map/ppermute | solution.py:45
  598.8 87.5 %collective-permute-start.64 = (bf16[1024,512]{1,0:T(8,128)(2,1)}, bf16[1024,512]{1,0:T(8,128)(2,1)}, u32[]{:S(2)}, u32[]{:S(2)}) collective-permute-start(bf16[1024,512]{1,0:T(8,128)(2,1)} %convolution_convert_fusion.1), channel_id=1, source_target_pairs={{0,16},{16,0},{1,17},{17,1},{2,18},{18,2},{3,19},{19,3},{4,20},{20... | collective-permute-start | bytes 3145736 | tf_op jit(solution)/shard_map/ppermute | solution.py:28
  603.7 96.9 %collective-permute-start.52 = (bf16[3072,512]{1,0:T(8,128)(2,1)}, bf16[3072,512]{1,0:T(8,128)(2,1)}, u32[]{:S(2)}, u32[]{:S(2)}) collective-permute-start(bf16[3072,512]{1,0:T(8,128)(2,1)} %get-tuple-element.160), channel_id=1, source_target_pairs={{0,16},{16,0},{1,17},{17,1},{2,18},{18,2},{3,19},{19,3},{4,20},{20... | collective-permute-start | bytes 9437192 | tf_op jit(solution)/shard_map/ppermute | solution.py:28
  620.5 47.4 %collective-permute-start.55 = (bf16[160,2048]{1,0:T(8,128)(2,1)S(1)}, bf16[160,2048]{1,0:T(8,128)(2,1)S(1)}, u32[]{:S(2)}, u32[]{:S(2)}) collective-permute-start(bf16[160,2048]{1,0:T(8,128)(2,1)S(1)} %slice.362), channel_id=1, source_target_pairs={{0,2},{2,0},{1,3},{3,1},{4,6},{6,4},{5,7},{7,5},{8,10},{10,8},{9,1... | collective-permute-start | bytes 1966088 | tf_op jit(solution)/shard_map/ppermute | solution.py:36
  691.7 59.5 %collective-permute-start.67 = (bf16[256,512]{1,0:T(8,128)(2,1)S(1)}, bf16[256,512]{1,0:T(8,128)(2,1)S(1)}, u32[]{:S(2)}, u32[]{:S(2)}) collective-permute-start(bf16[256,512]{1,0:T(8,128)(2,1)S(1)} %get-tuple-element.241), channel_id=1, source_target_pairs={{0,4},{4,0},{8,12},{12,8},{1,5},{5,1},{9,13},{13,9},{2,6},{6,2},{1... | collective-permute-start | bytes 786440 | tf_op jit(solution)/shard_map/ppermute | solution.py:45
  693.5 57.7 %collective-permute-start.66 = (bf16[256,512]{1,0:T(8,128)(2,1)S(1)}, bf16[256,512]{1,0:T(8,128)(2,1)S(1)}, u32[]{:S(2)}, u32[]{:S(2)}) collective-permute-start(bf16[256,512]{1,0:T(8,128)(2,1)S(1)} %get-tuple-element.242), channel_id=1, source_target_pairs={{0,8},{4,12},{8,0},{12,4},{1,9},{5,13},{9,1},{13,5},{2,10},{6,14},... | collective-permute-start | bytes 786440 | tf_op jit(solution)/shard_map/ppermute | solution.py:45
  694.9 56.2 %collective-permute-start.65 = (bf16[256,512]{1,0:T(8,128)(2,1)S(1)}, bf16[256,512]{1,0:T(8,128)(2,1)S(1)}, u32[]{:S(2)}, u32[]{:S(2)}) collective-permute-start(bf16[256,512]{1,0:T(8,128)(2,1)S(1)} %get-tuple-element.240), channel_id=1, source_target_pairs={{0,12},{4,8},{8,4},{12,0},{1,13},{5,9},{9,5},{13,1},{2,14},{6,10},... | collective-permute-start | bytes 786440 | tf_op jit(solution)/shard_map/ppermute | solution.py:45
  699.3 99.6 %collective-permute-start.60 = (bf16[3072,512]{1,0:T(8,128)(2,1)}, bf16[3072,512]{1,0:T(8,128)(2,1)S(1)}, u32[]{:S(2)}, u32[]{:S(2)}) collective-permute-start(bf16[3072,512]{1,0:T(8,128)(2,1)} %get-tuple-element.158), channel_id=1, source_target_pairs={{0,16},{16,0},{1,17},{17,1},{2,18},{18,2},{3,19},{19,3},{4,20},{20... | collective-permute-start | bytes 9437192 | tf_op jit(solution)/shard_map/ppermute | solution.py:28
  749.6 39.6 %collective-permute-start.53 = (bf16[160,2048]{1,0:T(8,128)(2,1)}, bf16[160,2048]{1,0:T(8,128)(2,1)}, u32[]{:S(2)}, u32[]{:S(2)}) collective-permute-start(bf16[160,2048]{1,0:T(8,128)(2,1)} %fusion.12), channel_id=1, source_target_pairs={{0,2},{2,0},{1,3},{3,1},{4,6},{6,4},{5,7},{7,5},{8,10},{10,8},{9,1... | collective-permute-start | bytes 1966088 | tf_op jit(solution)/shard_map/ppermute | solution.py:36
  751.2 49.1 %collective-permute-start.63 = (bf16[320,2048]{1,0:T(8,128)(2,1)}, bf16[320,2048]{1,0:T(8,128)(2,1)}, u32[]{:S(2)}, u32[]{:S(2)}) collective-permute-start(bf16[320,2048]{1,0:T(8,128)(2,1)} %pad_maximum_fusion.6), channel_id=1, source_target_pairs={{0,1},{1,0},{2,3},{3,2},{4,5},{5,4},{6,7},{7,6},{8,9},{9,8},{10,11... | collective-permute-start | bytes 3932168 | tf_op jit(solution)/shard_map/ppermute | solution.py:32
  (112 other events, 1289.7 us)
Sparse Core Ops, SparseCore 0:
  153.9 163.3 all-gather.2
  324.6 164.3 all-gather.4
  621.5 117.3 all-reduce.2

commit v4 on v3

--- a/solution.py
+++ b/solution.py
@@ -17,7 +17,7 @@
 BF16 = jnp.bfloat16
 VMEM_LIMIT = 56 * 1024 * 1024
 BIG = 1 << 30
-CFG = {'farcost': 1, 'a_qfar': 1, 'a_out': 1, 'kv_q': 1, 'x_kv': 1, 'b_y': 1, 'b_q': 1, 'kv_late': 1, 'n_p': 1, 's_last': 1, 'w_near': 1, 'o_q': 1, 'o_ffn': 1, 'o_near': 1, 'ow_near': 1, 'c_all': 1, 'early': 1, 'e_after': 1, 'e_hook': 1, 'e_up': 1, 'e_go': 1, 'e_gp': 1}
+CFG = {'farcost': 1, 'a_qfar': 1, 'a_out': 1, 'kv_q': 1, 'x_kv': 1, 'b_y': 1, 'b_q': 1, 'kv_late': 1, 'n_p': 1, 's_last': 1, 'w_near': 1, 'o_q': 1, 'o_near': 1, 'ow_near': 1, 'c_all': 1, 'early': 1, 'e_after': 1, 'e_hook': 1, 'e_up': 1, 'e_go': 1, 'e_gp': 1, 'e_share': 1}
 
 
 def on(name, *values):

time: 832 us -> 840 us (level)
  waiting for transfers between devices: 232 us -> 242 us
    ppermute x20 -> x19, waiting for transfers between devices: 67.4 us -> 99.4 us  [swap_x(): return lax.ppermute(a, 'fsdp', [(0, 1), (1, 0)])]
    ppermute x10, waiting for transfers between devices: 49.8 us -> 29.5 us  [swap_y(): return lax.ppermute(a, 'tp', [(0, 2), (2, 0), (1, 3), (3, 1)])]
    ppermute x20 -> x19, starting transfers between devices: 21.4 us -> 23.9 us  [swap_x(): return lax.ppermute(a, 'fsdp', [(0, 1), (1, 0)])]
    unnamed x148 -> x156, local copies, waits for them, and re-layouts: 22.5 us -> 22.3 us
  transfers between devices with their start and end apart: 74 -> 74, of which waited for: 33 -> 31; matrix products, arithmetic and copies ran while one was open for 14% -> 14% of each run, Pallas kernels for 41% -> 41%
where the time goes in v4:
time: 840 us; the launch traced here: 832 us
  Pallas kernels  345 us (41%)
  waiting for transfers between devices  242 us (29%)
  starting transfers between devices  75.8 us (9%)
  local copies, waits for them, and re-layouts  65.6 us (8%)
  other arithmetic  58.3 us (7%)
  matrix products  25.9 us (3%)
  between operations  19.8 us (2%)
    ppermute x19, waiting for transfers between devices, swap_x(): return lax.ppermute(a, 'fsdp', [(0, 1), (1, 0)])  99.4 us
    pallas_call x2, Pallas kernels, grads_call(): pl.pallas_call(kernel, grid_spec=pltpu.PrefetchScalarGridSpec(num_scalar_...  92.8 us
    pallas_call x2, Pallas kernels, all_up_call(): pl.pallas_call(all_up_kernel, grid_spec=pltpu.PrefetchScalarGridSpec(num_...  56.4 us
    ppermute x4, waiting for transfers between devices, swap_xy(): return lax.ppermute(a, ('fsdp', 'tp'), pairs)  51.1 us
    pallas_call x1, Pallas kernels, near_grads_call(): pl.pallas_call(near_grads_kernel, grid_spec=pltpu.PrefetchScalarGridSpec(...  49 us
    ppermute x6, waiting for transfers between devices, gather_ctx(): a = lax.ppermute(a, 'ctx', ring)  37.7 us
    pallas_call x4, Pallas kernels, out_call(): pl.pallas_call(partial(out_kernel, n, contract, last), grid=(half // TILE...  37.5 us
    ppermute x10, waiting for transfers between devices, swap_y(): return lax.ppermute(a, 'tp', [(0, 2), (2, 0), (1, 3), (3, 1)])  29.5 us
  transfers between devices with their start and end apart: 74, of which 31 were waited for; matrix products, arithmetic and copies ran while one was open for 14% of the time, Pallas kernels for 41%

profile of v4, /device:TPU:0, one launch (start us, length us, event | category | flops | bytes accessed | tf_op | source)
XLA Modules:
  0.0 832.4 jit_solution(17490408056156708649)
XLA Ops:
  55.5 14.7 %collective-permute-done.10 = bf16[640,512]{1,0:T(8,128)(2,1)S(1)} collective-permute-done((bf16[640,512]{1,0:T(8,128)(2,1)}, bf16[640,512]{1,0:T(8,128)(2,1)S(1)}, u32[]{:S(2)}, u32[]{:S(2)}) %collective-permute-start.10) | collective-permute-done | bytes 655392 | tf_op jit(solution)/shard_map/ppermute | solution.py:667
  71.7 12.9 %collective-permute-done.11 = bf16[640,512]{1,0:T(8,128)(2,1)S(1)} collective-permute-done((bf16[640,512]{1,0:T(8,128)(2,1)S(1)}, bf16[640,512]{1,0:T(8,128)(2,1)S(1)}, u32[]{:S(2)}, u32[]{:S(2)}) %collective-permute-start.11) | collective-permute-done | bytes 655392 | tf_op jit(solution)/shard_map/ppermute | solution.py:667
  85.4 4.9 shard_map.239.q_ref
  90.4 6.3 collective-permute-done.12
  100.8 12.4 %shard_map.240 = (bf16[640,512]{1,0:T(8,128)(2,1)}, f32[640,512]{1,0:T(8,128)}, f32[640,512]{1,0:T(8,128)}) custom-call(s32[40]{0:T(128)} %reshape.278.meta_ref, bf16[640,512]{1,0:T(8,128)(2,1)} %shard_map.239.q_ref, bf16[2560,512]{1,0:T(8,128)(2,1)} %copy-done, bf16[2560,512]{1,0:T(8,128)(2,1)} %copy-done), custom_call_target="tpu_custom_call" | custom-call | tf_op jit(solution)/shard_map/pallas_call | solution.py:192
  126.6 14.7 %collective-permute-done.15 = bf16[160,2048]{1,0:T(8,128)(2,1)S(1)} collective-permute-done((bf16[160,2048]{1,0:T(8,128)(2,1)S(1)}, bf16[160,2048]{1,0:T(8,128)(2,1)S(1)}, u32[]{:S(2)}, u32[]{:S(2)}) %collective-permute-start.15) | collective-permute-done | bytes 655392 | tf_op jit(solution)/shard_map/ppermute | solution.py:36
  143.4 7.8 collective-permute-done.16.refs_11_.refs_9_.uf
  158.8 15.6 %collective-permute-done.19.refs_2_ = bf16[160,2048]{1,0:T(8,128)(2,1)S(1)} collective-permute-done((bf16[160,2048]{1,0:T(8,128)(2,1)S(1)}, bf16[160,2048]{1,0:T(8,128)(2,1)S(1)}, u32[]{:S(2)}, u32[]{:S(2)}) %collective-permute-start.19) | collective-permute-done | bytes 655392 | tf_op jit(solution)/shard_map/ppermute | solution.py:28
  178.0 34.9 %collective-permute-done.25.refs_4_.refs_9_.df = bf16[512,1024]{1,0:T(8,128)(2,1)S(1)} collective-permute-done((bf16[512,1024]{1,0:T(8,128)(2,1)S(1)}, bf16[512,1024]{1,0:T(8,128)(2,1)S(1)}, u32[]{:S(2)}, u32[]{:S(2)}) %collective-permute-start.25) | collective-permute-done | bytes 1048608 | tf_op jit(solution)/shard_map/ppermute | solution.py:28
  213.1 16.9 %collective-permute-done.20.refs_3_ = bf16[160,2048]{1,0:T(8,128)(2,1)S(1)} collective-permute-done((bf16[160,2048]{1,0:T(8,128)(2,1)S(1)}, bf16[160,2048]{1,0:T(8,128)(2,1)S(1)}, u32[]{:S(2)}, u32[]{:S(2)}) %collective-permute-start.20) | collective-permute-done | bytes 655392 | tf_op jit(solution)/shard_map/ppermute | solution.py:41
  233.9 13.3 %shard_map.241 = (f32[1280,512]{1,0:T(8,128)}, f32[1280,512]{1,0:T(8,128)}, bf16[1280,512]{1,0:T(8,128)(2,1)}, bf16[1280,2048]{1,0:T(8,128)(2,1)}) custom-call(bf16[160,2048]{1,0:T(8,128)(2,1)} %copy-done.10, bf16[160,2048]{1,0:T(8,128)(2,1)} %copy-done.50, bf16[160,2048]{1,0:T(8,128)(2,1)} %copy-done.49, bf16[160,2048]{1,0:T(8,128)(2,1)} %copy-done.51, ...), custom_call_target="tpu_custom_call" | custom-call | tf_op jit(solution)/shard_map/pallas_call | solution.py:351
  248.2 12.6 %shard_map.242 = (f32[1280,512]{1,0:T(8,128)}, f32[1280,512]{1,0:T(8,128)}, bf16[1280,512]{1,0:T(8,128)(2,1)}) custom-call(bf16[1280,2048]{1,0:T(8,128)(2,1)} %get-tuple-element.114.refs_0_, bf16[1024,512]{1,0:T(8,128)(2,1)} %get-tuple-element.213.refs_1_.refs_6_.gn, bf16[1024,512]{1,0:T(8,128)(2,1)} %copy-done.6, ...), custom_call_target="tpu_custom_call" | custom-call | tf_op jit(solution)/shard_map/pallas_call | solution.py:351
  261.8 7.2 shard_map.243
  269.0 5.1 collective-permute-done.28.refs_6_
  275.6 8.0 shard_map.244
  288.3 16.6 %collective-permute-done.31 = bf16[160,2048]{1,0:T(8,128)(2,1)S(1)} collective-permute-done((bf16[160,2048]{1,0:T(8,128)(2,1)}, bf16[160,2048]{1,0:T(8,128)(2,1)S(1)}, u32[]{:S(2)}, u32[]{:S(2)}) %collective-permute-start.31) | collective-permute-done | bytes 655392 | tf_op jit(solution)/shard_map/ppermute | solution.py:41
  304.9 12.9 %collective-permute-done.30 = bf16[160,2048]{1,0:T(8,128)(2,1)S(1)} collective-permute-done((bf16[160,2048]{1,0:T(8,128)(2,1)}, bf16[160,2048]{1,0:T(8,128)(2,1)S(1)}, u32[]{:S(2)}, u32[]{:S(2)}) %collective-permute-start.30) | collective-permute-done | bytes 655392 | tf_op jit(solution)/shard_map/ppermute | solution.py:28
  327.2 13.2 %collective-permute-done.32.refs_1_ = bf16[160,2048]{1,0:T(8,128)(2,1)S(1)} collective-permute-done((bf16[160,2048]{1,0:T(8,128)(2,1)S(1)}, bf16[160,2048]{1,0:T(8,128)(2,1)S(1)}, u32[]{:S(2)}, u32[]{:S(2)}) %collective-permute-start.32) | collective-permute-done | bytes 655392 | tf_op jit(solution)/shard_map/ppermute | solution.py:36
  343.0 17.6 %collective-permute-done.34.refs_3_ = bf16[160,2048]{1,0:T(8,128)(2,1)S(1)} collective-permute-done((bf16[160,2048]{1,0:T(8,128)(2,1)}, bf16[160,2048]{1,0:T(8,128)(2,1)S(1)}, u32[]{:S(2)}, u32[]{:S(2)}) %collective-permute-start.34) | collective-permute-done | bytes 655392 | tf_op jit(solution)/shard_map/ppermute | solution.py:41
  363.5 10.7 %shard_map.245 = (bf16[1280,512]{1,0:T(8,128)(2,1)}, bf16[1280,512]{1,0:T(8,128)(2,1)}, bf16[1280,2048]{1,0:T(8,128)(2,1)}) custom-call(bf16[160,2048]{1,0:T(8,128)(2,1)} %copy-done.13, bf16[160,2048]{1,0:T(8,128)(2,1)} %copy-done.52, bf16[160,2048]{1,0:T(8,128)(2,1)} %copy-done.54, bf16[160,2048]{1,0:T(8,128)(2,1)} %copy-done.55, ...), custom_call_target="tpu_custom_call" | custom-call | tf_op jit(solution)/shard_map/pallas_call | solution.py:390
  374.3 8.7 %shard_map.246 = (bf16[1280,512]{1,0:T(8,128)(2,1)}, bf16[1280,512]{1,0:T(8,128)(2,1)}) custom-call(bf16[1280,2048]{1,0:T(8,128)(2,1)} %get-tuple-element.125.refs_0_, bf16[512,1024]{1,0:T(8,128)(2,1)} %get-tuple-element.207.refs_3_.refs_1_.dn, bf16[512,1024]{1,0:T(8,128)(2,1)} %copy-done.16, f32[1280,512]{1,0:T(8,128)} %get-tuple-element.126.refs_3_, ...), custom_call_target="tpu_custom_call" | custom-call | tf_op jit(solution)/shard_map/pallas_call | solution.py:390
  383.0 10.6 %shard_map.247 = bf16[640,2048]{1,0:T(8,128)(2,1)} custom-call(bf16[1280,512]{1,0:T(8,128)(2,1)} %get-tuple-element.123.refs_0_, bf16[1280,512]{1,0:T(8,128)(2,1)} %get-tuple-element.124.refs_1_, bf16[1280,512]{1,0:T(8,128)(2,1)} %get-tuple-element.128.refs_2_, bf16[1280,512]{1,0:T(8,128)(2,1)} %get-tuple-element.129.refs_3_, ...), custom_call_target="tpu_custom_call" | custom-call | tf_op jit(solution)/shard_map/pallas_call | solution.py:455
  400.3 11.6 %shard_map.248 = (f32[160,2048]{1,0:T(8,128)}, bf16[160,2048]{1,0:T(8,128)(2,1)}, bf16[160,2048]{1,0:T(8,128)(2,1)}, bf16[160,2048]{1,0:T(8,128)(2,1)}) custom-call(bf16[1280,512]{1,0:T(8,128)(2,1)} %get-tuple-element.123.refs_0_, bf16[1280,512]{1,0:T(8,128)(2,1)} %get-tuple-element.124.refs_1_, bf16[1280,512]{1,0:T(8,128)(2,1)} %get-tuple-element.128.refs_2_, ...), custom_call_target="tpu_custom_call" | custom-call | tf_op jit(solution)/shard_map/pallas_call | solution.py:455
  421.5 27.7 %shard_map.249 = (f32[5120,512]{1,0:T(8,128)}, f32[5120,512]{1,0:T(8,128)}, bf16[5120,512]{1,0:T(8,128)(2,1)}) custom-call(s32[1]{0:T(128)} %bitcast.15.first_ref, bf16[5120,2048]{1,0:T(8,128)(2,1)} %all-gather.3.cloned.1.call-done.near_ref.far_ref.xf.xn, bf16[5120,2048]{1,0:T(8,128)(2,1)} %all-gather.3.cloned.1.call-done.near_ref.far_ref.xf.xn, ...), custom_call_target="tpu_custom_call" | custom-call | tf_op jit(solution)/shard_map/pallas_call | solution.py:492
  449.1 23.6 %collective-permute-done.41 = bf16[160,2048]{1,0:T(8,128)(2,1)} collective-permute-done((bf16[160,2048]{1,0:T(8,128)(2,1)}, bf16[160,2048]{1,0:T(8,128)(2,1)}, u32[]{:S(2)}, u32[]{:S(2)}) %collective-permute-start.41) | collective-permute-done | bytes 655392 | tf_op jit(solution)/shard_map/ppermute | solution.py:28
  478.0 28.7 %shard_map.250 = (f32[5120,512]{1,0:T(8,128)}, f32[5120,512]{1,0:T(8,128)}, bf16[5120,512]{1,0:T(8,128)(2,1)}) custom-call(s32[1]{0:T(128)} %bitcast.15.first_ref, bf16[5120,2048]{1,0:T(8,128)(2,1)} %all-gather.3.cloned.1.call-done.near_ref.far_ref.xf.xn, bf16[5120,2048]{1,0:T(8,128)(2,1)} %all-gather.3.cloned.1.call-done.near_ref.far_ref.xf.xn, ...), custom_call_target="tpu_custom_call" | custom-call | tf_op jit(solution)/shard_map/pallas_call | solution.py:492
  516.8 19.5 %shard_map.251 = (bf16[640,512]{1,0:T(8,128)(2,1)}, f32[2560,256]{1,0:T(8,128)}, f32[2560,256]{1,0:T(8,128)}) custom-call(s32[40]{0:T(128)} %reshape.278.meta_ref, bf16[640,512]{1,0:T(8,128)(2,1)} %shard_map.239.q_ref, bf16[2560,512]{1,0:T(8,128)(2,1)} %copy-done, bf16[2560,512]{1,0:T(8,128)(2,1)} %copy-done, f32[640,512]{1,0:T(8,128)} %bitcast_select_fusion.gc_ref, ...), custom_call_target="tpu_custom_call" | custom-call | tf_op jit(solution)/shard_map/pallas_call | solution.py:259
  552.0 46.4 %shard_map.252 = (bf16[3072,512]{1,0:T(8,128)(2,1)}, bf16[5120,512]{1,0:T(8,128)(2,1)}, bf16[5120,512]{1,0:T(8,128)(2,1)}) custom-call(s32[1]{0:T(128)} %bitcast.15.first_ref, bf16[5120,2048]{1,0:T(8,128)(2,1)} %all-gather.3.cloned.1.call-done.near_ref.far_ref.xf.xn, bf16[5120,2048]{1,0:T(8,128)(2,1)} %all-gather.5.cloned.1.call-done.gn.gf, ...), custom_call_target="tpu_custom_call" | custom-call | flops 26843545600 | tf_op jit(solution)/shard_map/pallas_call | solution.py:567
  630.6 46.5 %shard_map.254 = (bf16[3072,512]{1,0:T(8,128)(2,1)}, bf16[5120,512]{1,0:T(8,128)(2,1)}, bf16[5120,512]{1,0:T(8,128)(2,1)}) custom-call(s32[1]{0:T(128)} %bitcast.15.first_ref, bf16[5120,2048]{1,0:T(8,128)(2,1)} %all-gather.3.cloned.1.call-done.near_ref.far_ref.xf.xn, bf16[5120,2048]{1,0:T(8,128)(2,1)} %all-gather.5.cloned.1.call-done.gn.gf, ...), custom_call_target="tpu_custom_call" | custom-call | flops 26843545600 | tf_op jit(solution)/shard_map/pallas_call | solution.py:567
  685.1 10.5 %collective-permute-start.58 = (f32[1,4224]{1,0:T(1,128)S(1)}, f32[1,4224]{1,0:T(1,128)S(1)}, u32[]{:S(2)}, u32[]{:S(2)}) collective-permute-start(f32[1,4224]{1,0:T(1,128)S(1)} %add.332), channel_id=1, source_target_pairs={{0,4},{4,0},{8,12},{12,8},{1,5},{5,1},{9,13},{13,9},{2,6},{6,2},{1... | collective-permute-start | bytes 50696 | tf_op jit(solution)/shard_map/ppermute | solution.py:726
  710.4 49.0 %shard_map.255 = (bf16[3072,512]{1,0:T(8,128)(2,1)}, bf16[3072,512]{1,0:T(8,128)(2,1)}) custom-call(s32[1]{0:T(128)} %bitcast.15.first_ref, bf16[5120,2048]{1,0:T(8,128)(2,1)} %all-gather.3.cloned.1.call-done.near_ref.far_ref.xf.xn, bf16[5120,2048]{1,0:T(8,128)(2,1)} %all-gather.5.cloned.1.call-done.gn.gf, ...), custom_call_target="tpu_custom_call" | custom-call | tf_op jit(solution)/shard_map/pallas_call | solution.py:600
  779.0 4.9 shard_map.257
  (449 shorter events, 266.8 us)
Async XLA Ops:
  7.2 414.3 %all-gather.3.cloned.1.call-start = ((), (), s32[]{:S(2)}) async-start(), calls=%async_computation | async-start | bytes 21626880 | tf_op jit(solution)/shard_map/all_gather | solution.py:773
  8.6 37.9 %collective-permute-start = (bf16[2,1024]{1,0:T(2,128)(2,1)S(1)}, bf16[2,1024]{1,0:T(2,128)(2,1)S(1)}, u32[]{:S(2)}, u32[]{:S(2)}) collective-permute-start(bf16[2,1024]{1,0:T(2,128)(2,1)S(1)} %pad_maximum_fusion.14), channel_id=1, source_target_pairs={{0,16},{16,0},{1,17},{17,1},{2,18},{18,2},{3,19},{19,3},{4,20},{20... | collective-permute-start | bytes 12296 | tf_op jit(solution)/shard_map/ppermute | solution.py:28
  15.9 30.7 %collective-permute-start.6 = (bf16[1024,256]{1,0:T(8,128)(2,1)}, bf16[1024,256]{1,0:T(8,128)(2,1)S(1)}, u32[]{:S(2)}, u32[]{:S(2)}) collective-permute-start(bf16[1024,256]{1,0:T(8,128)(2,1)} %refs_0_.2), channel_id=1, source_target_pairs={{0,16},{16,0},{1,17},{17,1},{2,18},{18,2},{3,19},{19,3},{4,20},{20... | collective-permute-start | bytes 1572872 | tf_op jit(solution)/shard_map/ppermute | solution.py:28
  153.6 363.2 %all-gather.5.cloned.1.call-start = ((), (), s32[]{:S(2)}) async-start(), calls=%async_computation.1 | async-start | bytes 21626880 | tf_op jit(solution)/shard_map/all_gather | solution.py:773
  174.4 38.6 %collective-permute-start.25 = (bf16[512,1024]{1,0:T(8,128)(2,1)S(1)}, bf16[512,1024]{1,0:T(8,128)(2,1)S(1)}, u32[]{:S(2)}, u32[]{:S(2)}) collective-permute-start(bf16[512,1024]{1,0:T(8,128)(2,1)S(1)} %get-tuple-element.113), channel_id=1, source_target_pairs={{0,16},{16,0},{1,17},{17,1},{2,18},{18,2},{3,19},{19,3},{4,20},{20... | collective-permute-start | bytes 3145736 | tf_op jit(solution)/shard_map/ppermute | solution.py:28
  175.3 37.7 %collective-permute-start.18 = (bf16[160,2048]{1,0:T(8,128)(2,1)S(1)}, bf16[160,2048]{1,0:T(8,128)(2,1)S(1)}, u32[]{:S(2)}, u32[]{:S(2)}) collective-permute-start(bf16[160,2048]{1,0:T(8,128)(2,1)S(1)} %multiply_convert_fusion.refs_0_), channel_id=1, source_target_pairs={{0,2},{2,0},{1,3},{3,1},{4,6},{6,4},{5,7},{7,5},{8,10},{10,8},{9,1... | collective-permute-start | bytes 1966088 | tf_op jit(solution)/shard_map/ppermute | solution.py:36
  175.8 54.1 %collective-permute-start.20 = (bf16[160,2048]{1,0:T(8,128)(2,1)S(1)}, bf16[160,2048]{1,0:T(8,128)(2,1)S(1)}, u32[]{:S(2)}, u32[]{:S(2)}) collective-permute-start(bf16[160,2048]{1,0:T(8,128)(2,1)S(1)} %pad_maximum_fusion.9), channel_id=1, source_target_pairs={{0,18},{1,19},{2,16},{3,17},{16,2},{17,3},{18,0},{19,1},{4,22},{5,... | collective-permute-start | bytes 1966088 | tf_op jit(solution)/shard_map/ppermute | solution.py:41
  177.9 52.1 %collective-permute-start.21 = (bf16[160,2048]{1,0:T(8,128)(2,1)S(1)}, bf16[160,2048]{1,0:T(8,128)(2,1)S(1)}, u32[]{:S(2)}, u32[]{:S(2)}) collective-permute-start(bf16[160,2048]{1,0:T(8,128)(2,1)S(1)} %multiply_convert_fusion.refs_0_), channel_id=1, source_target_pairs={{0,1},{1,0},{2,3},{3,2},{4,5},{5,4},{6,7},{7,6},{8,9},{9,8},{10,11... | collective-permute-start | bytes 1966088 | tf_op jit(solution)/shard_map/ppermute | solution.py:32
  177.9 69.3 %collective-permute-start.26 = (bf16[1024,512]{1,0:T(8,128)(2,1)S(1)}, bf16[1024,512]{1,0:T(8,128)(2,1)S(1)}, u32[]{:S(2)}, u32[]{:S(2)}) collective-permute-start(bf16[1024,512]{1,0:T(8,128)(2,1)S(1)} %copy-done.8), channel_id=1, source_target_pairs={{0,4},{4,0},{8,12},{12,8},{1,5},{5,1},{9,13},{13,9},{2,6},{6,2},{1... | collective-permute-start | bytes 3145736 | tf_op jit(solution)/shard_map/ppermute | solution.py:45
  213.0 47.9 %collective-permute-start.27 = (bf16[512,1024]{1,0:T(8,128)(2,1)S(1)}, bf16[512,1024]{1,0:T(8,128)(2,1)S(1)}, u32[]{:S(2)}, u32[]{:S(2)}) collective-permute-start(bf16[512,1024]{1,0:T(8,128)(2,1)S(1)} %collective-permute-done.25.refs_4_.refs_9_.df), channel_id=1, source_target_pairs={{0,4},{4,0},{8,12},{12,8},{1,5},{5,1},{9,13},{13,9},{2,6},{6,2},{1... | collective-permute-start | bytes 3145736 | tf_op jit(solution)/shard_map/ppermute | solution.py:45
  284.4 33.3 %collective-permute-start.30 = (bf16[160,2048]{1,0:T(8,128)(2,1)}, bf16[160,2048]{1,0:T(8,128)(2,1)S(1)}, u32[]{:S(2)}, u32[]{:S(2)}) collective-permute-start(bf16[160,2048]{1,0:T(8,128)(2,1)} %get-tuple-element.118), channel_id=1, source_target_pairs={{0,16},{16,0},{1,17},{17,1},{2,18},{18,2},{3,19},{19,3},{4,20},{20... | collective-permute-start | bytes 1966088 | tf_op jit(solution)/shard_map/ppermute | solution.py:28
  286.7 31.1 %collective-permute-start.29 = (bf16[160,2048]{1,0:T(8,128)(2,1)}, bf16[160,2048]{1,0:T(8,128)(2,1)S(1)}, u32[]{:S(2)}, u32[]{:S(2)}) collective-permute-start(bf16[160,2048]{1,0:T(8,128)(2,1)} %get-tuple-element.117), channel_id=1, source_target_pairs={{0,2},{2,0},{1,3},{3,1},{4,6},{6,4},{5,7},{7,5},{8,10},{10,8},{9,1... | collective-permute-start | bytes 1966088 | tf_op jit(solution)/shard_map/ppermute | solution.py:36
  323.4 465.5 %all-reduce.3.cloned.1.call-start = ((), (), s32[]{:S(2)}) async-start(), calls=%async_computation.2 | async-start | bytes 4194304 | tf_op jit(solution)/shard_map/psum | solution.py:976
  325.7 34.8 %collective-permute-start.34 = (bf16[160,2048]{1,0:T(8,128)(2,1)}, bf16[160,2048]{1,0:T(8,128)(2,1)S(1)}, u32[]{:S(2)}, u32[]{:S(2)}) collective-permute-start(bf16[160,2048]{1,0:T(8,128)(2,1)} %get-tuple-element.244), channel_id=1, source_target_pairs={{0,18},{1,19},{2,16},{3,17},{16,2},{17,3},{18,0},{19,1},{4,22},{5,... | collective-permute-start | bytes 1966088 | tf_op jit(solution)/shard_map/ppermute | solution.py:41
  327.2 33.4 %collective-permute-start.35 = (bf16[160,2048]{1,0:T(8,128)(2,1)S(1)}, bf16[160,2048]{1,0:T(8,128)(2,1)S(1)}, u32[]{:S(2)}, u32[]{:S(2)}) collective-permute-start(bf16[160,2048]{1,0:T(8,128)(2,1)S(1)} %fusion.22.refs_0_), channel_id=1, source_target_pairs={{0,1},{1,0},{2,3},{3,2},{4,5},{5,4},{6,7},{7,6},{8,9},{9,8},{10,11... | collective-permute-start | bytes 1966088 | tf_op jit(solution)/shard_map/ppermute | solution.py:32
  412.0 37.1 %collective-permute-start.42 = (bf16[160,2048]{1,0:T(8,128)(2,1)}, bf16[160,2048]{1,0:T(8,128)(2,1)}, u32[]{:S(2)}, u32[]{:S(2)}) collective-permute-start(bf16[160,2048]{1,0:T(8,128)(2,1)} %get-tuple-element.138), channel_id=1, source_target_pairs={{0,18},{1,19},{2,16},{3,17},{16,2},{17,3},{18,0},{19,1},{4,22},{5,... | collective-permute-start | bytes 1966088 | tf_op jit(solution)/shard_map/ppermute | solution.py:41
  413.4 59.4 %collective-permute-start.41 = (bf16[160,2048]{1,0:T(8,128)(2,1)}, bf16[160,2048]{1,0:T(8,128)(2,1)}, u32[]{:S(2)}, u32[]{:S(2)}) collective-permute-start(bf16[160,2048]{1,0:T(8,128)(2,1)} %get-tuple-element.137), channel_id=1, source_target_pairs={{0,16},{16,0},{1,17},{17,1},{2,18},{18,2},{3,19},{19,3},{4,20},{20... | collective-permute-start | bytes 1966088 | tf_op jit(solution)/shard_map/ppermute | solution.py:28
  415.0 57.7 %collective-permute-start.40 = (bf16[160,2048]{1,0:T(8,128)(2,1)}, bf16[160,2048]{1,0:T(8,128)(2,1)}, u32[]{:S(2)}, u32[]{:S(2)}) collective-permute-start(bf16[160,2048]{1,0:T(8,128)(2,1)} %get-tuple-element.136), channel_id=1, source_target_pairs={{0,2},{2,0},{1,3},{3,1},{4,6},{6,4},{5,7},{7,5},{8,10},{10,8},{9,1... | collective-permute-start | bytes 1966088 | tf_op jit(solution)/shard_map/ppermute | solution.py:36
  476.6 30.2 %collective-permute-start.44 = (bf16[160,2048]{1,0:T(8,128)(2,1)S(1)}, bf16[160,2048]{1,0:T(8,128)(2,1)S(1)}, u32[]{:S(2)}, u32[]{:S(2)}) collective-permute-start(bf16[160,2048]{1,0:T(8,128)(2,1)S(1)} %get-tuple-element.143), channel_id=1, source_target_pairs={{0,2},{2,0},{1,3},{3,1},{4,6},{6,4},{5,7},{7,5},{8,10},{10,8},{9,1... | collective-permute-start | bytes 1966088 | tf_op jit(solution)/shard_map/ppermute | solution.py:36
  539.4 61.7 %collective-permute-start.50 = (bf16[1024,512]{1,0:T(8,128)(2,1)}, bf16[1024,512]{1,0:T(8,128)(2,1)}, u32[]{:S(2)}, u32[]{:S(2)}) collective-permute-start(bf16[1024,512]{1,0:T(8,128)(2,1)} %convolution_convert_fusion.3), channel_id=1, source_target_pairs={{0,16},{16,0},{1,17},{17,1},{2,18},{18,2},{3,19},{19,3},{4,20},{20... | collective-permute-start | bytes 3145736 | tf_op jit(solution)/shard_map/ppermute | solution.py:28
  547.5 50.8 %collective-permute-start.49 = (bf16[640,512]{1,0:T(8,128)(2,1)S(1)}, bf16[640,512]{1,0:T(8,128)(2,1)S(1)}, u32[]{:S(2)}, u32[]{:S(2)}) collective-permute-start(bf16[640,512]{1,0:T(8,128)(2,1)S(1)} %get-tuple-element.205), channel_id=1, source_target_pairs={{0,4},{4,0},{8,12},{12,8},{1,5},{5,1},{9,13},{13,9},{2,6},{6,2},{1... | collective-permute-start | bytes 1966088 | tf_op jit(solution)/shard_map/ppermute | solution.py:45
  548.6 49.7 %collective-permute-start.48 = (bf16[640,512]{1,0:T(8,128)(2,1)S(1)}, bf16[640,512]{1,0:T(8,128)(2,1)S(1)}, u32[]{:S(2)}, u32[]{:S(2)}) collective-permute-start(bf16[640,512]{1,0:T(8,128)(2,1)S(1)} %get-tuple-element.206), channel_id=1, source_target_pairs={{0,8},{4,12},{8,0},{12,4},{1,9},{5,13},{9,1},{13,5},{2,10},{6,14},... | collective-permute-start | bytes 1966088 | tf_op jit(solution)/shard_map/ppermute | solution.py:45
  551.2 47.1 %collective-permute-start.47 = (bf16[640,512]{1,0:T(8,128)(2,1)S(1)}, bf16[640,512]{1,0:T(8,128)(2,1)S(1)}, u32[]{:S(2)}, u32[]{:S(2)}) collective-permute-start(bf16[640,512]{1,0:T(8,128)(2,1)S(1)} %get-tuple-element.204), channel_id=1, source_target_pairs={{0,12},{4,8},{8,4},{12,0},{1,13},{5,9},{9,5},{13,1},{2,14},{6,10},... | collective-permute-start | bytes 1966088 | tf_op jit(solution)/shard_map/ppermute | solution.py:45
  607.2 88.4 %collective-permute-start.64 = (bf16[1024,512]{1,0:T(8,128)(2,1)}, bf16[1024,512]{1,0:T(8,128)(2,1)}, u32[]{:S(2)}, u32[]{:S(2)}) collective-permute-start(bf16[1024,512]{1,0:T(8,128)(2,1)} %convolution_convert_fusion.1), channel_id=1, source_target_pairs={{0,16},{16,0},{1,17},{17,1},{2,18},{18,2},{3,19},{19,3},{4,20},{20... | collective-permute-start | bytes 3145736 | tf_op jit(solution)/shard_map/ppermute | solution.py:28
  612.8 97.7 %collective-permute-start.52 = (bf16[3072,512]{1,0:T(8,128)(2,1)}, bf16[3072,512]{1,0:T(8,128)(2,1)}, u32[]{:S(2)}, u32[]{:S(2)}) collective-permute-start(bf16[3072,512]{1,0:T(8,128)(2,1)} %get-tuple-element.158), channel_id=1, source_target_pairs={{0,16},{16,0},{1,17},{17,1},{2,18},{18,2},{3,19},{19,3},{4,20},{20... | collective-permute-start | bytes 9437192 | tf_op jit(solution)/shard_map/ppermute | solution.py:28
  628.8 48.3 %collective-permute-start.55 = (bf16[160,2048]{1,0:T(8,128)(2,1)S(1)}, bf16[160,2048]{1,0:T(8,128)(2,1)S(1)}, u32[]{:S(2)}, u32[]{:S(2)}) collective-permute-start(bf16[160,2048]{1,0:T(8,128)(2,1)S(1)} %slice.362), channel_id=1, source_target_pairs={{0,2},{2,0},{1,3},{3,1},{4,6},{6,4},{5,7},{7,5},{8,10},{10,8},{9,1... | collective-permute-start | bytes 1966088 | tf_op jit(solution)/shard_map/ppermute | solution.py:36
  700.5 58.9 %collective-permute-start.67 = (bf16[256,512]{1,0:T(8,128)(2,1)S(1)}, bf16[256,512]{1,0:T(8,128)(2,1)S(1)}, u32[]{:S(2)}, u32[]{:S(2)}) collective-permute-start(bf16[256,512]{1,0:T(8,128)(2,1)S(1)} %get-tuple-element.238), channel_id=1, source_target_pairs={{0,4},{4,0},{8,12},{12,8},{1,5},{5,1},{9,13},{13,9},{2,6},{6,2},{1... | collective-permute-start | bytes 786440 | tf_op jit(solution)/shard_map/ppermute | solution.py:45
  701.8 57.7 %collective-permute-start.66 = (bf16[256,512]{1,0:T(8,128)(2,1)S(1)}, bf16[256,512]{1,0:T(8,128)(2,1)S(1)}, u32[]{:S(2)}, u32[]{:S(2)}) collective-permute-start(bf16[256,512]{1,0:T(8,128)(2,1)S(1)} %get-tuple-element.239), channel_id=1, source_target_pairs={{0,8},{4,12},{8,0},{12,4},{1,9},{5,13},{9,1},{13,5},{2,10},{6,14},... | collective-permute-start | bytes 786440 | tf_op jit(solution)/shard_map/ppermute | solution.py:45
  703.3 56.2 %collective-permute-start.65 = (bf16[256,512]{1,0:T(8,128)(2,1)S(1)}, bf16[256,512]{1,0:T(8,128)(2,1)S(1)}, u32[]{:S(2)}, u32[]{:S(2)}) collective-permute-start(bf16[256,512]{1,0:T(8,128)(2,1)S(1)} %get-tuple-element.237), channel_id=1, source_target_pairs={{0,12},{4,8},{8,4},{12,0},{1,13},{5,9},{9,5},{13,1},{2,14},{6,10},... | collective-permute-start | bytes 786440 | tf_op jit(solution)/shard_map/ppermute | solution.py:45
  707.4 99.6 %collective-permute-start.60 = (bf16[3072,512]{1,0:T(8,128)(2,1)}, bf16[3072,512]{1,0:T(8,128)(2,1)S(1)}, u32[]{:S(2)}, u32[]{:S(2)}) collective-permute-start(bf16[3072,512]{1,0:T(8,128)(2,1)} %get-tuple-element.156), channel_id=1, source_target_pairs={{0,16},{16,0},{1,17},{17,1},{2,18},{18,2},{3,19},{19,3},{4,20},{20... | collective-permute-start | bytes 9437192 | tf_op jit(solution)/shard_map/ppermute | solution.py:28
  759.4 38.0 %collective-permute-start.53 = (bf16[160,2048]{1,0:T(8,128)(2,1)}, bf16[160,2048]{1,0:T(8,128)(2,1)}, u32[]{:S(2)}, u32[]{:S(2)}) collective-permute-start(bf16[160,2048]{1,0:T(8,128)(2,1)} %fusion.12), channel_id=1, source_target_pairs={{0,2},{2,0},{1,3},{3,1},{4,6},{6,4},{5,7},{7,5},{8,10},{10,8},{9,1... | collective-permute-start | bytes 1966088 | tf_op jit(solution)/shard_map/ppermute | solution.py:36
  759.4 49.2 %collective-permute-start.63 = (bf16[320,2048]{1,0:T(8,128)(2,1)}, bf16[320,2048]{1,0:T(8,128)(2,1)}, u32[]{:S(2)}, u32[]{:S(2)}) collective-permute-start(bf16[320,2048]{1,0:T(8,128)(2,1)} %pad_maximum_fusion.6), channel_id=1, source_target_pairs={{0,1},{1,0},{2,3},{3,2},{4,5},{5,4},{6,7},{7,6},{8,9},{9,8},{10,11... | collective-permute-start | bytes 3932168 | tf_op jit(solution)/shard_map/ppermute | solution.py:32
  (116 other events, 1415.6 us)
Sparse Core Ops, SparseCore 0:
  153.8 180.3 all-gather.2
  337.0 167.0 all-gather.4
  630.7 116.6 all-reduce.2
